TPU v7x, 32 devices: a whole 2x2x4 slice. The times are simulated.
32 devices in a mesh: seq: 4 (over y, x), tm: 8 (over z, core).
Axes of the slice: x: 2, y: 2, z: 4, core: 2. Of those that a mesh axis runs over, the one named last changes fastest.
Arguments:
- tokens: bfloat16 [4, 8, 2048, 512], P(None, 'seq', 'tm'), may hold values from -6 to 6
- lengths: int32 [4, 8], P(None, 'seq'), may hold values from 256 to 2048, as said below
- cotangent: bfloat16 [4, 8, 2048, 512], P(None, 'seq', 'tm'), may hold values from -6 to 6
- norm_gain: bfloat16 [512], P(('seq', 'tm')), may hold values from 0.099609375 to 1.8984375
- norm_shift: bfloat16 [512], P(('seq', 'tm')), may hold values from -3 to 3
- input_proj: bfloat16 [512, 512], P(('seq', 'tm')), may hold values from -0.25 to 0.25
- decay_log: bfloat16 [256], P(('seq', 'tm')), may hold values from -13 to 0
- phase_log: bfloat16 [256], P(('seq', 'tm')), may hold values from -5 to -0.5
- gamma_log: bfloat16 [256], P(('seq', 'tm')), may hold values from -7 to 1
- output_proj: bfloat16 [512, 512], P(('seq', 'tm')), may hold values from -0.25 to 0.25
- skip_gain: bfloat16 [512], P(('seq', 'tm')), may hold values from -3 to 3
- gate_weight: bfloat16 [512, 1024], P(('seq', 'tm')), may hold values from -0.75 to 0.75
- gate_bias: bfloat16 [1024], P(('seq', 'tm')), may hold values from -3 to 3
Outputs:
- block_out: bfloat16 [4, 8, 2048, 512], P(None, 'seq', 'tm')
- tokens_gradient: bfloat16 [4, 8, 2048, 512], P(None, 'seq', 'tm')
- norm_gain_gradient: float32 [512], P(('seq', 'tm'))
- norm_shift_gradient: float32 [512], P(('seq', 'tm'))
- input_proj_gradient: float32 [512, 512], P(('seq', 'tm'))
- decay_log_gradient: float32 [256], P(('seq', 'tm'))
- phase_log_gradient: float32 [256], P(('seq', 'tm'))
- gamma_log_gradient: float32 [256], P(('seq', 'tm'))
- output_proj_gradient: float32 [512, 512], P(('seq', 'tm'))
- skip_gain_gradient: float32 [512], P(('seq', 'tm'))
- gate_weight_gradient: float32 [512, 1024], P(('seq', 'tm'))
- gate_bias_gradient: float32 [1024], P(('seq', 'tm'))
Inputs may be any that keep to these rules, and one draw needn't show every extreme that they name: `lengths`: in every micro-batch, among the 2 sequences that share an index of seq, one uses all 2048 positions; positions from a sequence's length on are padding.
All inputs are finite; a program needn't handle non-finite values.
Results may differ from a plain program's by a relative error of at most 0.02.
Values may be sent and summed in bfloat16 or wider, within the bound.
No kernel may reach another device: no remote copies, remote signals or barrier semaphores. Data moves between devices by JAX's collectives and lax.ppermute only.
A program may use at most 128 MiB of HBM per device.

v0:
```python
import jax
import jax.numpy as jnp
from jax import lax
from jax.sharding import PartitionSpec as P


def prefix(part, axis, combine, identity, reverse):
    count = lax.axis_size(axis)
    place = lax.axis_index(axis)
    ahead = count - 1 - place if reverse else place
    gathered = jax.tree.map(lambda a: lax.all_gather(a, axis), part)
    state = jax.tree.map(lambda a, e: jnp.zeros_like(a) + jnp.asarray(e, a.dtype), part, identity)

    def one(step, state):
        source = count - 1 - step if reverse else step
        return combine(
            state, jax.tree.map(lambda a: lax.dynamic_index_in_dim(a, source, 0, False), gathered)
        )

    return lax.fori_loop(0, ahead, one, state)


def carry_combine(earlier, latter):
    early_re, early_im, early_pow_re, early_pow_im = earlier
    late_re, late_im, late_pow_re, late_pow_im = latter
    return (
        late_re + late_pow_re * early_re - late_pow_im * early_im,
        late_im + late_pow_re * early_im + late_pow_im * early_re,
        late_pow_re * early_pow_re - late_pow_im * early_pow_im,
        late_pow_re * early_pow_im + late_pow_im * early_pow_re,
    )


def stretch_scan(lam_re, lam_im, drive_re, drive_im, backward):
    if backward:
        drive_re = drive_re[:, ::-1]
        drive_im = drive_im[:, ::-1]
    seq_count, stretch_len, state_count = drive_re.shape
    block_len = 16
    block_count = stretch_len // block_len
    split_re = drive_re.reshape(seq_count, block_count, block_len, state_count)
    split_im = drive_im.reshape(seq_count, block_count, block_len, state_count)
    acc_re = jnp.zeros((seq_count, block_count, state_count), jnp.float32)
    acc_im = jnp.zeros((seq_count, block_count, state_count), jnp.float32)
    power_re = jnp.ones((state_count,), jnp.float32)
    power_im = jnp.zeros((state_count,), jnp.float32)
    inner_re = []
    inner_im = []
    powers_re = []
    powers_im = []
    for step in range(block_len):
        next_re = lam_re * acc_re - lam_im * acc_im + split_re[:, :, step]
        next_im = lam_re * acc_im + lam_im * acc_re + split_im[:, :, step]
        acc_re, acc_im = (next_re, next_im)
        inner_re.append(acc_re)
        inner_im.append(acc_im)
        new_pow_re = lam_re * power_re - lam_im * power_im
        new_pow_im = lam_re * power_im + lam_im * power_re
        power_re, power_im = (new_pow_re, new_pow_im)
        powers_re.append(power_re)
        powers_im.append(power_im)
    local_re = jnp.moveaxis(jnp.stack(inner_re, axis=2), 1, 0)
    local_im = jnp.moveaxis(jnp.stack(inner_im, axis=2), 1, 0)
    table_re = jnp.stack(powers_re, axis=0)
    table_im = jnp.stack(powers_im, axis=0)

    def across(carry, block_item):
        carry_re, carry_im = carry
        block_re, block_im = block_item
        full_re = block_re + table_re * carry_re[:, None] - table_im * carry_im[:, None]
        full_im = block_im + table_re * carry_im[:, None] + table_im * carry_re[:, None]
        return ((full_re[:, -1], full_im[:, -1]), (full_re, full_im))

    start = jnp.zeros((seq_count, state_count), jnp.float32)
    unused, (whole_re, whole_im) = lax.scan(across, (start, start), (local_re, local_im))
    out_re = jnp.moveaxis(whole_re, 0, 1).reshape(seq_count, stretch_len, state_count)
    out_im = jnp.moveaxis(whole_im, 0, 1).reshape(seq_count, stretch_len, state_count)
    if backward:
        out_re = out_re[:, ::-1]
        out_im = out_im[:, ::-1]
    return (out_re, out_im)


def micro_step(gathered, token_block, cot_block, span, position, steps_up):
    norm_gain = gathered[0].astype(jnp.float32)
    norm_shift = gathered[1].astype(jnp.float32)
    input_proj = gathered[2]
    decay_rate = jnp.exp(gathered[3].astype(jnp.float32))
    phase_step = jnp.exp(gathered[4].astype(jnp.float32))
    input_scale = jnp.exp(gathered[5].astype(jnp.float32))
    output_proj = gathered[6]
    skip_gain = gathered[7].astype(jnp.float32)
    gate_weight = gathered[8]
    gate_bias = gathered[9].astype(jnp.float32)
    state_count = decay_rate.shape[0]
    model_width = token_block.shape[-1]
    inputs = token_block.astype(jnp.float32)
    average = jnp.mean(inputs, axis=-1, keepdims=True)
    centred = inputs - average
    inverse = lax.rsqrt(jnp.mean(centred * centred, axis=-1, keepdims=True) + 1e-05)
    whitened = centred * inverse
    normed = (whitened * norm_gain + norm_shift).astype(jnp.bfloat16)
    normed_wide = normed.astype(jnp.float32)
    drive = jnp.einsum("sch,hk->sck", normed, input_proj, preferred_element_type=jnp.float32)
    drive_re = drive[..., :state_count]
    drive_im = drive[..., state_count:]
    modulus = jnp.exp(-decay_rate)
    lam_re = modulus * jnp.cos(phase_step)
    lam_im = modulus * jnp.sin(phase_step)
    power_mod = jnp.exp(-steps_up * decay_rate)
    power_re = power_mod * jnp.cos(steps_up * phase_step)
    power_im = power_mod * jnp.sin(steps_up * phase_step)
    local_re, local_im = stretch_scan(
        lam_re, lam_im, input_scale * drive_re, input_scale * drive_im, False
    )
    zero_state = jnp.zeros((local_re.shape[0], state_count), jnp.float32)
    ones_power = jnp.ones((state_count,), jnp.float32)
    zero_power = jnp.zeros((state_count,), jnp.float32)
    carried = prefix(
        (local_re[:, -1], local_im[:, -1], power_re[-1], power_im[-1]),
        "tm",
        carry_combine,
        (zero_state, zero_state, ones_power, zero_power),
        False,
    )
    carry_re = carried[0][:, None]
    carry_im = carried[1][:, None]
    state_re = local_re + power_re * carry_re - power_im * carry_im
    state_im = local_im + power_re * carry_im + power_im * carry_re
    state_low = jnp.concatenate([state_re, state_im], axis=-1).astype(jnp.bfloat16)
    mixed = jnp.einsum("sck,kh->sch", state_low, output_proj, preferred_element_type=jnp.float32)
    mixed = mixed + skip_gain * normed_wide
    activated_wide, gelu_pull = jax.vjp(jax.nn.gelu, mixed)
    activated = activated_wide.astype(jnp.bfloat16)
    gated = (
        jnp.einsum("sch,hk->sck", activated, gate_weight, preferred_element_type=jnp.float32)
        + gate_bias
    )
    value_part = gated[..., :model_width]
    gate_part = gated[..., model_width:]
    live_mask = (position[None, :] < span[:, None]).astype(jnp.float32)[..., None]
    opened = jax.nn.sigmoid(gate_part)
    block_out = (inputs + live_mask * value_part * opened).astype(jnp.bfloat16)
    incoming = cot_block.astype(jnp.float32)
    masked = incoming * live_mask
    d_value = masked * opened
    d_gate = masked * value_part * opened * (1.0 - opened)
    d_pre = jnp.concatenate([d_value, d_gate], axis=-1).astype(jnp.bfloat16)
    gate_weight_grad = jnp.einsum(
        "sch,sck->hk", activated, d_pre, preferred_element_type=jnp.float32
    )
    gate_bias_grad = jnp.sum(d_pre, axis=(0, 1), dtype=jnp.float32)
    d_act = jnp.einsum("sck,hk->sch", d_pre, gate_weight, preferred_element_type=jnp.float32)
    d_mixed = gelu_pull(d_act)[0].astype(jnp.bfloat16)
    d_mixed_wide = d_mixed.astype(jnp.float32)
    output_proj_grad = jnp.einsum(
        "sck,sch->kh", state_low, d_mixed, preferred_element_type=jnp.float32
    )
    skip_grad = jnp.sum(normed_wide * d_mixed_wide, axis=(0, 1))
    d_state = jnp.einsum("sch,kh->sck", d_mixed, output_proj, preferred_element_type=jnp.float32)
    adj_local_re, adj_local_im = stretch_scan(
        lam_re, -lam_im, d_state[..., :state_count], d_state[..., state_count:], True
    )
    returned = prefix(
        (adj_local_re[:, 0], adj_local_im[:, 0], power_re[-1], -power_im[-1]),
        "tm",
        carry_combine,
        (zero_state, zero_state, ones_power, zero_power),
        True,
    )
    back_re = returned[0][:, None]
    back_im = returned[1][:, None]
    reverse_re = power_re[::-1]
    reverse_im = -power_im[::-1]
    adjoint_re = adj_local_re + reverse_re * back_re - reverse_im * back_im
    adjoint_im = adj_local_im + reverse_re * back_im + reverse_im * back_re
    prior_re = jnp.concatenate([carry_re, state_re[:, :-1]], axis=1)
    prior_im = jnp.concatenate([carry_im, state_im[:, :-1]], axis=1)
    lam_sum_re = jnp.sum(adjoint_re * prior_re + adjoint_im * prior_im, axis=(0, 1))
    lam_sum_im = jnp.sum(adjoint_im * prior_re - adjoint_re * prior_im, axis=(0, 1))
    decay_grad = -decay_rate * (lam_sum_re * lam_re + lam_sum_im * lam_im)
    phase_grad = phase_step * (lam_sum_im * lam_re - lam_sum_re * lam_im)
    gamma_grad = input_scale * jnp.sum(adjoint_re * drive_re + adjoint_im * drive_im, axis=(0, 1))
    d_drive = jnp.concatenate([input_scale * adjoint_re, input_scale * adjoint_im], axis=-1).astype(
        jnp.bfloat16
    )
    input_proj_grad = jnp.einsum("sch,sck->hk", normed, d_drive, preferred_element_type=jnp.float32)
    d_normed = jnp.einsum("sck,hk->sch", d_drive, input_proj, preferred_element_type=jnp.float32)
    d_normed = d_normed + skip_gain * d_mixed_wide
    gain_grad = jnp.sum(d_normed * whitened, axis=(0, 1))
    shift_grad = jnp.sum(d_normed, axis=(0, 1))
    d_white = d_normed * norm_gain
    d_inputs = inverse * (
        d_white
        - jnp.mean(d_white, axis=-1, keepdims=True)
        - whitened * jnp.mean(d_white * whitened, axis=-1, keepdims=True)
    )
    tokens_grad = (incoming + d_inputs).astype(jnp.bfloat16)
    local_grads = (
        gain_grad,
        shift_grad,
        input_proj_grad,
        decay_grad,
        phase_grad,
        gamma_grad,
        output_proj_grad,
        skip_grad,
        gate_weight_grad,
        gate_bias_grad,
    )
    return (block_out, tokens_grad, local_grads)


def body(
    tokens,
    lengths,
    cotangent,
    norm_gain,
    norm_shift,
    input_proj,
    decay_log,
    phase_log,
    gamma_log,
    output_proj,
    skip_gain,
    gate_weight,
    gate_bias,
):
    micro_count = tokens.shape[0]
    stretch_len = tokens.shape[2]
    position = lax.axis_index("tm") * stretch_len + jnp.arange(stretch_len, dtype=jnp.int32)
    steps_up = jnp.arange(1, stretch_len + 1, dtype=jnp.int32).astype(jnp.float32)[:, None]
    block_outs = []
    tokens_grads = []
    owned_grads = None
    for micro in range(micro_count):
        gathered = (
            lax.all_gather(norm_gain, ("seq", "tm"), axis=0, tiled=True),
            lax.all_gather(norm_shift, ("seq", "tm"), axis=0, tiled=True),
            lax.all_gather(input_proj, ("seq", "tm"), axis=0, tiled=True),
            lax.all_gather(decay_log, ("seq", "tm"), axis=0, tiled=True),
            lax.all_gather(phase_log, ("seq", "tm"), axis=0, tiled=True),
            lax.all_gather(gamma_log, ("seq", "tm"), axis=0, tiled=True),
            lax.all_gather(output_proj, ("seq", "tm"), axis=0, tiled=True),
            lax.all_gather(skip_gain, ("seq", "tm"), axis=0, tiled=True),
            lax.all_gather(gate_weight, ("seq", "tm"), axis=0, tiled=True),
            lax.all_gather(gate_bias, ("seq", "tm"), axis=0, tiled=True),
        )
        block_out, tokens_grad, local_grads = micro_step(
            gathered, tokens[micro], cotangent[micro], lengths[micro], position, steps_up
        )
        block_outs.append(block_out)
        tokens_grads.append(tokens_grad)
        owned_part = (
            lax.psum_scatter(local_grads[0], ("seq", "tm"), scatter_dimension=0, tiled=True),
            lax.psum_scatter(local_grads[1], ("seq", "tm"), scatter_dimension=0, tiled=True),
            lax.psum_scatter(local_grads[2], ("seq", "tm"), scatter_dimension=0, tiled=True),
            lax.psum_scatter(local_grads[3], ("seq", "tm"), scatter_dimension=0, tiled=True),
            lax.psum_scatter(local_grads[4], ("seq", "tm"), scatter_dimension=0, tiled=True),
            lax.psum_scatter(local_grads[5], ("seq", "tm"), scatter_dimension=0, tiled=True),
            lax.psum_scatter(local_grads[6], ("seq", "tm"), scatter_dimension=0, tiled=True),
            lax.psum_scatter(local_grads[7], ("seq", "tm"), scatter_dimension=0, tiled=True),
            lax.psum_scatter(local_grads[8], ("seq", "tm"), scatter_dimension=0, tiled=True),
            lax.psum_scatter(local_grads[9], ("seq", "tm"), scatter_dimension=0, tiled=True),
        )
        owned_grads = (
            owned_part if owned_grads is None else jax.tree.map(jnp.add, owned_grads, owned_part)
        )
    return (
        jnp.stack(block_outs),
        jnp.stack(tokens_grads),
        owned_grads[0],
        owned_grads[1],
        owned_grads[2],
        owned_grads[3],
        owned_grads[4],
        owned_grads[5],
        owned_grads[6],
        owned_grads[7],
        owned_grads[8],
        owned_grads[9],
    )


def solution(mesh):
    return jax.shard_map(
        body,
        mesh=mesh,
        in_specs=(
            P(None, "seq", "tm", None),
            P(None, "seq"),
            P(None, "seq", "tm", None),
            P(("seq", "tm")),
            P(("seq", "tm")),
            P(("seq", "tm"), None),
            P(("seq", "tm")),
            P(("seq", "tm")),
            P(("seq", "tm")),
            P(("seq", "tm"), None),
            P(("seq", "tm")),
            P(("seq", "tm"), None),
            P(("seq", "tm")),
        ),
        out_specs=(
            P(None, "seq", "tm", None),
            P(None, "seq", "tm", None),
            P(("seq", "tm")),
            P(("seq", "tm")),
            P(("seq", "tm"), None),
            P(("seq", "tm")),
            P(("seq", "tm")),
            P(("seq", "tm")),
            P(("seq", "tm"), None),
            P(("seq", "tm")),
            P(("seq", "tm"), None),
            P(("seq", "tm")),
        ),
        check_vma=False,
    )
```

profile of v0, /device:TPU:0, one launch (start us, length us, event | category | flops | bytes accessed | tf_op | source)
XLA Modules:
  0.0 1334.1 jit_solution(5344209893929161593)
XLA Ops:
  14.0 42.1 %all-reduce.15 = (bf16[1024]{0:T(1024)(128)(2,1)S(1)}, bf16[512]{0:T(512)(128)(2,1)S(1)}, bf16[512]{0:T(512)(128)(2,1)S(1)}, bf16[512]{0:T(512)(128)(2,1)S(1)}, ...) all-reduce(bf16[1024]{0:T(1024)(128)(2,1)S(1)} %dynamic-update-slic, ...), channel_id=1, replica_groups=mesh['seq'=4,'tm'=8] {'seq','tm'}, use_global_device_ids=true, to_apply=%add.6 | all-reduce | flops 3328 | bytes 13312
  63.4 42.6 %all_gather.63 = bf16[512,512]{1,0:T(8,128)(2,1)S(1)} all-gather(bf16[16,512]{1,0:T(8,128)(2,1)} %param.50), channel_id=1, replica_groups=mesh['seq'=4,'tm'=8] {'seq','tm'}, dimensions={0}, use_global_device_ids=true | all-gather | bytes 540672 | tf_op jit(solution)/shard_map/all_gather | solution.py:240
  120.6 28.5 %while.260 = (s32[]{:T(128)}, f32[2,256]{1,0:T(2,128)S(1)}, f32[2,256]{1,0:T(2,128)S(1)}, f32[16,2,16,256]{3,2,1,0:T(8,128)S(1)}, f32[16,2,16,256]{3,2,1,0:T(8,1...) while((s32[]{:T(128)}, f32[2,256]{1,0:T(2,128)S(1)}, ...), condition=%wide.region_15.16_spmd, body=%wide.region_14.15_spmd.sunk | while | flops 69634 | bytes 391285 | solution.py:75
  151.0 12.7 all-gather.4
  163.8 8.7 all-gather.16
  172.5 10.1 all-gather.17
  184.4 12.7 all-gather.5
  203.2 28.7 %while.258 = (s32[]{:T(128)}, f32[2,256]{1,0:T(2,128)S(1)}, f32[2,256]{1,0:T(2,128)S(1)}, f32[16,2,16,256]{3,2,1,0:T(8,128)}, f32[16,2,16,256]{3,2,1,0:T(8,128)}...) while((s32[]{:T(128)}, f32[2,256]{1,0:T(2,128)S(1)}, ...), condition=%wide.region_9.10_spmd, body=%wide.region_8.9_spmd.sunk | while | flops 69634 | bytes 391285 | solution.py:75
  233.1 12.7 all-gather.2
  247.8 12.7 all-gather.3
  262.3 28.8 %while.256 = (s32[]{:T(128)}, f32[2,256]{1,0:T(2,128)S(1)}, f32[2,256]{1,0:T(2,128)S(1)}, f32[16,2,16,256]{3,2,1,0:T(8,128)}, f32[16,2,16,256]{3,2,1,0:T(8,128)}...) while((s32[]{:T(128)}, f32[2,256]{1,0:T(2,128)S(1)}, ...), condition=%wide.region_3.4_spmd, body=%wide.region_2.3_spmd.sunk | while | flops 69634 | bytes 391285 | solution.py:75
  292.3 14.2 %all-gather = f32[16,1,256]{2,1,0:T(1,128)S(1)} all-gather(f32[2,1,256]{2,1,0:T(1,128)S(1)} %slice.1424), channel_id=2, replica_groups=mesh['seq'=4,'tm'=8] {'tm'}, dimensions={0}, use_global_device_ids=true | all-gather | bytes 18432 | tf_op jit(solution)/shard_map/all_gather | solution.py:11
  308.5 12.7 all-gather.1
  322.5 12.6 all-gather.18
  343.9 39.0 %all_gather.68 = bf16[512,512]{1,0:T(8,128)(2,1)S(1)} all-gather(bf16[16,512]{1,0:T(8,128)(2,1)} %param.54), channel_id=1, replica_groups=mesh['seq'=4,'tm'=8] {'seq','tm'}, dimensions={0}, use_global_device_ids=true | all-gather | bytes 540672 | tf_op jit(solution)/shard_map/all_gather | solution.py:244
  401.5 4.8 rev.61
  406.2 4.1 fusion.288
  415.1 4.7 rev.67
  423.8 4.7 rev.60
  432.6 4.7 rev.66
  447.9 59.2 %while.264 = (s32[]{:T(128)}, f32[2,256]{1,0:T(2,128)S(1)}, f32[2,256]{1,0:T(2,128)}, f32[16,2,16,256]{3,2,1,0:T(8,128)}, f32[16,2,16,256]{3,2,1,0:T(8,128)}, /*...) while((s32[]{:T(128)}, f32[2,256]{1,0:T(2,128)S(1)}, ...), condition=%wide.region_25.26_spmd, body=%wide.region_24.25_spmd.sunk | while | flops 69634 | bytes 391285 | solution.py:75
  509.6 4.7 rev.62
  516.8 4.7 rev.65
  525.3 28.5 %while.266 = (s32[]{:T(128)}, f32[2,256]{1,0:T(2,128)S(1)}, f32[2,256]{1,0:T(2,128)S(1)}, f32[16,2,16,256]{3,2,1,0:T(8,128)}, f32[16,2,16,256]{3,2,1,0:T(8,128)}...) while((s32[]{:T(128)}, f32[2,256]{1,0:T(2,128)S(1)}, ...), condition=%wide.region_31.32_spmd, body=%wide.region_30.31_spmd.sunk | while | flops 69634 | bytes 391285 | solution.py:75
  556.4 4.7 rev.68
  563.5 4.8 rev.69
  568.3 13.1 all-gather.8
  581.4 12.9 all-gather.9
  595.0 5.2 while.265
  600.1 12.9 all-gather.10
  613.7 12.9 all-gather.11
  626.7 5.0 while.267
  646.0 28.8 %while.262 = (s32[]{:T(128)}, f32[2,256]{1,0:T(2,128)S(1)}, f32[2,256]{1,0:T(2,128)S(1)}, f32[16,2,16,256]{3,2,1,0:T(8,128)}, f32[16,2,16,256]{3,2,1,0:T(8,128)}...) while((s32[]{:T(128)}, f32[2,256]{1,0:T(2,128)S(1)}, ...), condition=%wide.region_21.22_spmd, body=%wide.region_20.21_spmd.sunk | while | flops 69634 | bytes 391285 | solution.py:75
  676.7 12.7 all-gather.6
  691.3 12.7 all-gather.7
  716.5 4.8 rev.71
  721.3 4.3 fusion.280
  726.3 4.7 rev.70
  764.9 28.3 %while.268 = (s32[]{:T(128)}, f32[2,256]{1,0:T(2,128)S(1)}, f32[2,256]{1,0:T(2,128)S(1)}, f32[16,2,16,256]{3,2,1,0:T(8,128)S(1)}, f32[16,2,16,256]{3,2,1,0:T(8,1...) while((s32[]{:T(128)}, f32[2,256]{1,0:T(2,128)S(1)}, ...), condition=%wide.region_37.38_spmd, body=%wide.region_36.37_spmd.sunk | while | flops 69634 | bytes 391285 | solution.py:75
  822.9 28.3 %while.270 = (s32[]{:T(128)}, f32[2,256]{1,0:T(2,128)S(1)}, f32[2,256]{1,0:T(2,128)S(1)}, f32[16,2,16,256]{3,2,1,0:T(8,128)S(1)}, f32[16,2,16,256]{3,2,1,0:T(8,1...) while((s32[]{:T(128)}, f32[2,256]{1,0:T(2,128)S(1)}, ...), condition=%wide.region_43.44_spmd, body=%wide.region_42.43_spmd.sunk | while | flops 69634 | bytes 391285 | solution.py:75
  862.2 14.2 %all-gather.12 = f32[16,1,256]{2,1,0:T(1,128)S(1)} all-gather(f32[2,1,256]{2,1,0:T(1,128)S(1)} %copy-done.249), channel_id=14, replica_groups=mesh['seq'=4,'tm'=8] {'tm'}, dimensions={0}, use_global_device_ids=true | all-gather | bytes 18432 | tf_op jit(solution)/shard_map/all_gather | solution.py:11
  876.4 12.7 all-gather.13
  889.7 12.7 all-gather.14
  902.5 12.9 all-gather.15
  944.1 38.3 %all-reduce.14 = (f32[512]{0:T(512)S(1)}, f32[512]{0:T(512)S(1)}, f32[256]{0:T(256)S(1)}, f32[256]{0:T(256)S(1)}, f32[256]{0:T(256)S(1)}, /*index=5*/f32[512]{0:T(512)S(1)}, f32[1024]{0:T(1024)S(1)}) all-reduce(f32[512]{0:T(512)S(1)} %add_add_fusion.3, ...), channel_id=48, replica_groups=mesh['seq'=4,'tm'=8] {'seq','tm'}, use_global_device_ids=true, to_apply=%region_49.50.clone | all-reduce | flops 3328 | bytes 26624
  993.9 62.7 %reduce-scatter.4.cloned.1.call-done = f32[16,512]{1,0:T(8,128)} async-done(((f32[512,512]{1,0:T(8,128)}), f32[16,512]{1,0:T(8,128)}) %reduce-scatter.4.cloned.1.call-update) | async-done | bytes 32784 | tf_op jit(solution)/shard_map/reduce_scatter | solution.py:257
  1056.6 134.2 %reduce-scatter.6.cloned.1.call-done = f32[16,512]{1,0:T(8,128)} async-done(((f32[512,512]{1,0:T(8,128)}), f32[16,512]{1,0:T(8,128)}) %reduce-scatter.6.cloned.1.call-update) | async-done | bytes 32784 | tf_op jit(solution)/shard_map/reduce_scatter | solution.py:261
  1190.7 136.4 %reduce-scatter.8.cloned.1.call-done = f32[16,1024]{1,0:T(8,128)} async-done(((f32[512,1024]{1,0:T(8,128)}), f32[16,1024]{1,0:T(8,128)}) %reduce-scatter.8.cloned.1.call-update) | async-done | bytes 65552 | tf_op jit(solution)/shard_map/reduce_scatter | solution.py:263
  (1928 shorter events, 522.1 us)
Async XLA Ops:
  7.2 98.8 %copy-start = (bf16[4,2,256,512]{3,2,1,0:T(8,128)(2,1)S(1)}, bf16[4,2,256,512]{3,2,1,0:T(8,128)(2,1)}, u32[]{:S(2)}) copy-start(bf16[4,2,256,512]{3,2,1,0:T(8,128)(2,1)} %param.45) | copy-start | bytes 6291460
  7.2 384.2 %all-gather.21.cloned.1.call-start = ((), (), s32[]{:S(2)}) async-start(), calls=%async_computation.3 | async-start | bytes 1081344 | tf_op jit(solution)/shard_map/all_gather | solution.py:246
  7.9 1048.6 %reduce-scatter.4.cloned.1.call-start = ((), (), s32[]{:S(2)}) async-start(), calls=%async_computation.4 | async-start | bytes 1081344 | tf_op jit(solution)/shard_map/reduce_scatter | solution.py:257
  56.1 50.8 %copy-start.243 = (bf16[256]{0:T(256)(128)(2,1)}, bf16[256]{0:T(256)(128)(2,1)S(1)}, u32[]{:S(2)}) copy-start(bf16[256]{0:T(256)(128)(2,1)S(1)} %get-tuple-element.1710) | copy-start | bytes 1540
  56.1 50.8 %copy-start.246 = (bf16[256]{0:T(256)(128)(2,1)}, bf16[256]{0:T(256)(128)(2,1)S(1)}, u32[]{:S(2)}) copy-start(bf16[256]{0:T(256)(128)(2,1)S(1)} %get-tuple-element.1711) | copy-start | bytes 1540
  56.1 51.7 %copy-start.282 = (bf16[256]{0:T(256)(128)(2,1)}, bf16[256]{0:T(256)(128)(2,1)S(1)}, u32[]{:S(2)}) copy-start(bf16[256]{0:T(256)(128)(2,1)S(1)} %get-tuple-element.1709) | copy-start | bytes 1540
  56.9 57.7 %copy-start.192 = (f32[256]{0:T(256)}, f32[256]{0:T(256)S(1)}, u32[]{:S(2)}) copy-start(f32[256]{0:T(256)S(1)} %get-tuple-element.2754) | copy-start | bytes 3076
  57.0 58.7 %copy-start.188 = (f32[256]{0:T(256)}, f32[256]{0:T(256)S(1)}, u32[]{:S(2)}) copy-start(f32[256]{0:T(256)S(1)} %get-tuple-element.2760) | copy-start | bytes 3076
  119.7 44.1 %copy-start.269 = (f32[1,1,256]{2,1,0:T(1,128)S(1)}, f32[1,1,256]{2,1,0:T(1,128)}, u32[]{:S(2)}) copy-start(f32[1,1,256]{2,1,0:T(1,128)} %slice_bitcast_fusion) | copy-start | bytes 3076
  119.7 52.8 %copy-start.264 = (f32[1,1,256]{2,1,0:T(1,128)S(1)}, f32[1,1,256]{2,1,0:T(1,128)}, u32[]{:S(2)}) copy-start(f32[1,1,256]{2,1,0:T(1,128)} %get-tuple-element.2541) | copy-start | bytes 3076
  120.6 76.9 %copy-start.101 = (f32[2,16,1,256]{3,2,1,0:T(1,128)S(1)}, f32[2,16,1,256]{3,2,1,0:T(1,128)}, u32[]{:S(2)}) copy-start(f32[2,16,1,256]{3,2,1,0:T(1,128)} %get-tuple-element.2511) | copy-start | bytes 98308
  149.1 48.4 %copy-start.127 = (f32[2,16,1,256]{3,1,2,0:T(8,128)S(1)}, f32[2,16,1,256]{3,1,2,0:T(8,128)}, u32[]{:S(2)}) copy-start(f32[2,16,1,256]{3,1,2,0:T(8,128)} %get-tuple-element.2074) | copy-start | bytes 98308
  149.1 49.1 %copy-start.100 = (f32[2,16,1,256]{3,2,1,0:T(1,128)S(1)}, f32[2,16,1,256]{3,2,1,0:T(1,128)}, u32[]{:S(2)}) copy-start(f32[2,16,1,256]{3,2,1,0:T(1,128)} %get-tuple-element.2510) | copy-start | bytes 98308
  149.1 51.8 %copy-start.165 = (f32[2,16,1,256]{3,2,1,0:T(1,128)S(1)}, f32[2,16,1,256]{3,2,1,0:T(1,128)}, u32[]{:S(2)}) copy-start(f32[2,16,1,256]{3,2,1,0:T(1,128)} %get-tuple-element.2508) | copy-start | bytes 98308
  150.9 52.3 %copy-start.27 = (f32[2,16,16,256]{3,2,1,0:T(8,128)}, f32[2,16,16,256]{3,2,1,0:T(8,128)S(1)}, u32[]{:S(2)}) copy-start(f32[2,16,16,256]{3,2,1,0:T(8,128)S(1)} %copy.1027) | copy-start | bytes 1572868
  197.5 140.4 %copy-start.164 = (f32[2,256]{1,0:T(2,128)}, f32[2,256]{1,0:T(2,128)S(1)}, u32[]{:S(2)}) copy-start(f32[2,256]{1,0:T(2,128)S(1)} %get-tuple-element.1211) | copy-start | bytes 6148
  233.0 29.3 %copy-start.29 = (f32[2,16,16,256]{3,2,1,0:T(8,128)}, f32[2,16,16,256]{3,2,1,0:T(8,128)S(1)}, u32[]{:S(2)}) copy-start(f32[2,16,16,256]{3,2,1,0:T(8,128)S(1)} %copy.991) | copy-start | bytes 1572868
  262.3 60.1 %copy-start.263 = (f32[1,1,256]{2,1,0:T(1,128)S(1)}, f32[1,1,256]{2,1,0:T(1,128)}, u32[]{:S(2)}) copy-start(f32[1,1,256]{2,1,0:T(1,128)} %get-tuple-element.2540) | copy-start | bytes 3076
  291.1 47.9 %copy-start.219 = (f32[256]{0:T(256)S(1)}, f32[256]{0:T(256)}, u32[]{:S(2)}) copy-start(f32[256]{0:T(256)} %get-tuple-element.2035) | copy-start | bytes 3076
  291.1 49.3 %copy-start.217 = (f32[256]{0:T(256)S(1)}, f32[256]{0:T(256)}, u32[]{:S(2)}) copy-start(f32[256]{0:T(256)} %get-tuple-element.2034) | copy-start | bytes 3076
  291.2 49.3 %copy-start.261 = (f32[256]{0:T(256)S(1)}, f32[256]{0:T(256)}, u32[]{:S(2)}) copy-start(f32[256]{0:T(256)} %get-tuple-element.2033) | copy-start | bytes 3076
  291.2 49.3 %copy-start.262 = (f32[256]{0:T(256)S(1)}, f32[256]{0:T(256)}, u32[]{:S(2)}) copy-start(f32[256]{0:T(256)} %get-tuple-element.2036) | copy-start | bytes 3076
  291.2 50.8 %copy-start.252 = (f32[2,256]{1,0:T(2,128)S(1)}, f32[2,256]{1,0:T(2,128)}, u32[]{:S(2)}) copy-start(f32[2,256]{1,0:T(2,128)} %get-tuple-element.1409) | copy-start | bytes 6148
  292.3 48.2 %copy-start.31 = (f32[2,16,16,256]{3,2,1,0:T(8,128)}, f32[2,16,16,256]{3,2,1,0:T(8,128)S(1)}, u32[]{:S(2)}) copy-start(f32[2,16,16,256]{3,2,1,0:T(8,128)S(1)} %copy.955) | copy-start | bytes 1572868
  321.3 17.7 %copy-start.83 = (f32[8,256]{1,0:T(8,128)}, f32[8,256]{1,0:T(8,128)S(1)}, u32[]{:S(2)}) copy-start(f32[8,256]{1,0:T(8,128)S(1)} %get-tuple-element.4354) | copy-start | bytes 24580
  423.8 17.7 %copy-start.190 = (f32[256]{0:T(256)S(1)}, f32[256]{0:T(256)}, u32[]{:S(2)}) copy-start(f32[256]{0:T(256)} %get-tuple-element.2757) | copy-start | bytes 3076
  553.8 14.5 %copy-start.251 = (f32[2,1,256]{2,1,0:T(1,128)S(1)}, f32[2,1,256]{2,1,0:T(1,128)}, u32[]{:S(2)}) copy-start(f32[2,1,256]{2,1,0:T(1,128)} %slice.1578) | copy-start | bytes 6148
  553.8 41.1 %copy-start.84 = (f32[8,256]{1,0:T(8,128)S(1)}, f32[8,256]{1,0:T(8,128)}, u32[]{:S(2)}) copy-start(f32[8,256]{1,0:T(8,128)} %copy-done.83) | copy-start | bytes 24580
  553.8 41.1 %copy-start.173 = (f32[8,1,256]{2,0,1:T(8,128)S(1)}, f32[8,1,256]{2,0,1:T(8,128)}, u32[]{:S(2)}) copy-start(f32[8,1,256]{2,0,1:T(8,128)} %copy.2247) | copy-start | bytes 24580
  556.4 75.3 %copy-start.229 = (f32[2,1,256]{2,1,0:T(1,128)S(1)}, f32[2,1,256]{2,1,0:T(1,128)}, u32[]{:S(2)}) copy-start(f32[2,1,256]{2,1,0:T(1,128)} %broadcast_in_dim.33) | copy-start | bytes 6148
  689.4 17.4 %copy-start.223 = (f32[512]{0:T(512)S(1)}, f32[512]{0:T(512)}, u32[]{:S(2)}) copy-start(f32[512]{0:T(512)} %copy-done.220) | copy-start | bytes 6148
  749.1 12.9 copy-start.129
  749.1 12.9 copy-start.133
  795.1 13.0 copy-start.106
  799.4 18.6 %copy-start.103 = (f32[2,16,1,256]{3,2,1,0:T(1,128)S(1)}, f32[2,16,1,256]{3,2,1,0:T(1,128)}, u32[]{:S(2)}) copy-start(f32[2,16,1,256]{3,2,1,0:T(1,128)} %get-tuple-element.2326) | copy-start | bytes 98308
  800.0 19.4 %copy-start.102 = (f32[2,16,1,256]{3,2,1,0:T(1,128)S(1)}, f32[2,16,1,256]{3,2,1,0:T(1,128)}, u32[]{:S(2)}) copy-start(f32[2,16,1,256]{3,2,1,0:T(1,128)} %get-tuple-element.2325) | copy-start | bytes 98308
  802.6 16.8 %copy-start.104 = (f32[2,16,1,256]{3,2,1,0:T(1,128)S(1)}, f32[2,16,1,256]{3,2,1,0:T(1,128)}, u32[]{:S(2)}) copy-start(f32[2,16,1,256]{3,2,1,0:T(1,128)} %get-tuple-element.2310) | copy-start | bytes 98308
  802.6 17.4 %copy-start.167 = (f32[2,16,1,256]{3,2,1,0:T(1,128)S(1)}, f32[2,16,1,256]{3,2,1,0:T(1,128)}, u32[]{:S(2)}) copy-start(f32[2,16,1,256]{3,2,1,0:T(1,128)} %get-tuple-element.2324) | copy-start | bytes 98308
  802.6 17.4 %copy-start.168 = (f32[2,16,1,256]{3,2,1,0:T(1,128)S(1)}, f32[2,16,1,256]{3,2,1,0:T(1,128)}, u32[]{:S(2)}) copy-start(f32[2,16,1,256]{3,2,1,0:T(1,128)} %get-tuple-element.2309) | copy-start | bytes 98308
  802.6 18.7 %copy-start.166 = (f32[2,16,1,256]{3,2,1,0:T(1,128)S(1)}, f32[2,16,1,256]{3,2,1,0:T(1,128)}, u32[]{:S(2)}) copy-start(f32[2,16,1,256]{3,2,1,0:T(1,128)} %get-tuple-element.2308) | copy-start | bytes 98308
  856.8 19.6 %copy-start.250 = (f32[2,1,256]{2,1,0:T(1,128)S(1)}, f32[2,1,256]{2,1,0:T(1,128)}, u32[]{:S(2)}) copy-start(f32[2,1,256]{2,1,0:T(1,128)} %slice.1651) | copy-start | bytes 6148
  859.5 56.4 %copy-start.39 = (f32[2,256,256]{2,1,0:T(8,128)S(1)}, f32[2,256,256]{2,1,0:T(8,128)}, u32[]{:S(2)}) copy-start(f32[2,256,256]{2,1,0:T(8,128)} %get-tuple-element.1807) | copy-start | bytes 1572868
  859.5 56.4 %copy-start.225 = (f32[2,1,256]{2,1,0:T(1,128)S(1)}, f32[2,1,256]{2,1,0:T(1,128)}, u32[]{:S(2)}) copy-start(f32[2,1,256]{2,1,0:T(1,128)} %broadcast_in_dim.37) | copy-start | bytes 6148
  859.5 56.4 %copy-start.226 = (f32[2,1,256]{2,1,0:T(1,128)S(1)}, f32[2,1,256]{2,1,0:T(1,128)}, u32[]{:S(2)}) copy-start(f32[2,1,256]{2,1,0:T(1,128)} %broadcast_in_dim.36) | copy-start | bytes 6148
  924.1 266.6 %reduce-scatter.6.cloned.1.call-start = ((), (), s32[]{:S(2)}) async-start(), calls=%async_computation.5 | async-start | bytes 1081344 | tf_op jit(solution)/shard_map/reduce_scatter | solution.py:261
  929.5 397.6 %reduce-scatter.8.cloned.1.call-start = ((), (), s32[]{:S(2)}) async-start(), calls=%async_computation.6 | async-start | bytes 2162688 | tf_op jit(solution)/shard_map/reduce_scatter | solution.py:263
  941.4 48.3 %copy-start.280 = (f32[2,256]{1,0:T(2,128)S(1)}, f32[2,256]{1,0:T(2,128)}, u32[]{:S(2)}) copy-start(f32[2,256]{1,0:T(2,128)} %get-tuple-element.1389) | copy-start | bytes 6148
  941.4 48.3 %copy-start.281 = (f32[2,256]{1,0:T(2,128)S(1)}, f32[2,256]{1,0:T(2,128)}, u32[]{:S(2)}) copy-start(f32[2,256]{1,0:T(2,128)} %get-tuple-element.1410) | copy-start | bytes 6148
  (246 other events, 766.8 us)
Sparse Core Ops, SparseCore 0:
  11.0 56.4 all-gather.20
  924.2 132.2 reduce-scatter.3
  1059.5 131.2 reduce-scatter.5
  1193.4 133.6 reduce-scatter.7
where the time goes:
time: 1350 us; the launch traced here: 1330 us
  blocking collectives  401 us (30%)
  waiting for transfers between devices  334 us (25%)
  local copies, waits for them, and re-layouts  333 us (25%)
  other arithmetic  196 us (15%)
  matrix products  47 us (3%)
  between operations  18.5 us (1%)
    all_gather x19, blocking collectives, prefix(): gathered = jax.tree.map(lambda a: lax.all_gather(a, axis), part)  239 us
    dynamic_slice x128, local copies, waits for them, and re-layouts, stretch_scan(): lax.scan(across, (start, start), (local_re, local_im))  138 us
    reduce_scatter x1, waiting for transfers between devices, body(): lax.psum_scatter(local_grads[8], ('seq', 'tm'), scatter_dimension=0, tile...  136 us
    reduce_scatter x1, waiting for transfers between devices, body(): lax.psum_scatter(local_grads[6], ('seq', 'tm'), scatter_dimension=0, tile...  134 us
    dynamic_update_slice x128, other arithmetic, stretch_scan(): lax.scan(across, (start, start), (local_re, local_im))  92.9 us
    unnamed x2, blocking collectives  80.4 us
    reduce_scatter x1, waiting for transfers between devices, body(): lax.psum_scatter(local_grads[2], ('seq', 'tm'), scatter_dimension=0, tile...  62.7 us
    all_gather x1, blocking collectives, body(): lax.all_gather(input_proj, ('seq', 'tm'), axis=0, tiled=True)  42.6 us
  transfers between devices with their start and end apart: 4, of which 3 were waited for; matrix products, arithmetic and copies ran while one was open for 13% of the time, Pallas kernels for 0%

commit v1 on v0

v1 whole, which is shorter than its diff:
```python
import math

import jax
import jax.numpy as jnp
from jax import lax
from jax.experimental import pallas as pl
from jax.experimental.pallas import tpu as pltpu
from jax.sharding import Mesh, PartitionSpec as P

F32 = jnp.float32
BF = jnp.bfloat16
AXES = ("seq", "tmc", "core")
CHIPS = ("seq", "tmc")
LIMIT = pltpu.CompilerParams(vmem_limit_bytes=56 << 20)
GELU_K = math.sqrt(2.0 / math.pi)
STEPS = 32


def dot(a, b):
    return lax.dot_general(a, b, (((1,), (0,)), ((), ())), preferred_element_type=F32)


def dot_rows(a, b):
    return lax.dot_general(a, b, (((0,), (0,)), ((), ())), preferred_element_type=F32)


def whole(shape):
    return pl.BlockSpec(shape, lambda *_: (0,) * len(shape))


def prepare_kernel(span, base, tok, cot, wh_out, wht_out, inv_out, cotl_out):
    count, length, width = tok.shape
    part = 16
    for i in range(0, length, part):
        x = tok[:, i : i + part, :].astype(F32)
        mean = jnp.mean(x, axis=-1, keepdims=True)
        c = x - mean
        inv = lax.rsqrt(jnp.mean(c * c, axis=-1, keepdims=True) + 1e-05)
        wh = jnp.swapaxes(c * inv, 0, 1).reshape(part * count, width)
        rows = slice(i * count, (i + part) * count)
        wh_out[rows, :] = wh.astype(BF)
        wide = jnp.broadcast_to(inv, (count, part, 128))
        inv_out[rows, :] = jnp.swapaxes(wide, 0, 1).reshape(part * count, 128)
        y = jnp.swapaxes(cot[:, i : i + part, :].astype(F32), 0, 1)
        seq_id = lax.broadcasted_iota(jnp.int32, (1, count, 128), 1)
        ends = jnp.zeros((1, count, 128), jnp.int32)
        for s in range(count):
            ends = jnp.where(seq_id == s, span[s], ends)
        place = base[0] + i + lax.broadcasted_iota(jnp.int32, (part, 1, 128), 0)
        live = jnp.where(place < ends, 1.0, 0.0)
        y = y * jnp.concatenate([live] * (width // 128), axis=-1)
        cotl_out[rows, :] = y.reshape(part * count, width).astype(BF)
    step = 256
    for i in range(0, length * count, step):
        wht_out[:, i : i + step] = wh_out[i : i + step, :].T


def prepare(span, base, tok, cot):
    count, length, width = tok.shape
    total = count * length
    smem = pl.BlockSpec(memory_space=pltpu.SMEM)
    return pl.pallas_call(
        prepare_kernel,
        out_shape=(
            jax.ShapeDtypeStruct((total, width), BF),
            jax.ShapeDtypeStruct((width, total), BF),
            jax.ShapeDtypeStruct((total, 128), F32),
            jax.ShapeDtypeStruct((total, width), BF),
        ),
        in_specs=[smem, smem, whole(tok.shape), whole(cot.shape)],
        compiler_params=LIMIT,
        name="prepare",
    )(span, base, tok, cot)


def assemble_one(place, dests, own, other):
    pieces = own.shape[0]
    for half, ref in enumerate((own, other)):
        for q in range(pieces):
            owner = jnp.bitwise_xor(place, 2 * q + half)
            row = pl.multiple_of(owner * 16, 16)
            for k, d in enumerate(dests):
                d[pl.ds(row, 16), :] = ref[q, 16 * k : 16 * (k + 1), :]


def vector_rows(acc):
    half = acc.shape[1] // 2
    gain, shift, skip = acc[0:1], acc[1:2], acc[2:3]
    rate = jnp.exp(acc[3:4, :half])
    phase = jnp.exp(acc[3:4, half:])
    scale = jnp.exp(acc[4:5])
    modulus = jnp.exp(-rate)
    lam = jnp.concatenate([modulus * jnp.cos(phase), modulus * jnp.sin(phase)], axis=1)
    rates = jnp.concatenate([rate, phase], axis=1)
    shifted = (acc[7:8] + acc[8:9]) * scale
    return (lam, rates, scale, shifted, skip * gain, skip * shift, acc[5:6], acc[6:7])


def assemble_first_kernel(place, own, other, b_out, bt_out, vec_out):
    pieces, _, width = own.shape
    acc = jnp.zeros((16, width), F32)
    for ref in (own, other):
        for q in range(pieces):
            acc = acc + ref[q, 16:32, :].astype(F32)
    rows = vector_rows(acc)
    for k, r in enumerate(rows):
        vec_out[k : k + 1, :] = r
    assemble_one(place[0], (b_out,), own, other)
    b_out[...] = (b_out[...].astype(F32) * rows[2]).astype(BF)
    bt_out[...] = b_out[...].T


def assemble_first(place, own, other):
    width = own.shape[-1]
    smem = pl.BlockSpec(memory_space=pltpu.SMEM)
    return pl.pallas_call(
        assemble_first_kernel,
        out_shape=(
            jax.ShapeDtypeStruct((width, width), BF),
            jax.ShapeDtypeStruct((width, width), BF),
            jax.ShapeDtypeStruct((8, width), F32),
        ),
        in_specs=[smem, whole(own.shape), whole(other.shape)],
        compiler_params=LIMIT,
        name="assemble_first",
    )(place, own, other)


def assemble_rest_kernel(place, own, other, c_out, ct_out, g_out, gt_out):
    width = c_out.shape[0]
    assemble_one(place[0], (c_out, g_out.at[:, :width], g_out.at[:, width:]), own, other)
    ct_out[...] = c_out[...].T
    gt_out[...] = g_out[...].T


def assemble_rest(place, own, other):
    width = own.shape[-1]
    smem = pl.BlockSpec(memory_space=pltpu.SMEM)
    return pl.pallas_call(
        assemble_rest_kernel,
        out_shape=(
            jax.ShapeDtypeStruct((width, width), BF),
            jax.ShapeDtypeStruct((width, width), BF),
            jax.ShapeDtypeStruct((width, 2 * width), BF),
            jax.ShapeDtypeStruct((2 * width, width), BF),
        ),
        in_specs=[smem, whole(own.shape), whole(other.shape)],
        compiler_params=LIMIT,
        name="assemble_rest",
    )(place, own, other)


def complex_step(lr, li, xr, xi, ur, ui):
    return lr * xr - li * xi + ur, lr * xi + li * xr + ui


def lam_rows(vec, count):
    half = vec.shape[1] // 2
    return (
        jnp.broadcast_to(vec[0:1, :half], (count, half)),
        jnp.broadcast_to(vec[0:1, half:], (count, half)),
    )


def drive_kernel(wh, b, vec, u_out, end_out):
    i = pl.program_id(0)
    count, width = end_out.shape
    half = width // 2

    @pl.when(i == 0)
    def _():
        end_out[...] = jnp.zeros_like(end_out)

    u_out[...] = dot(wh[...], b[...]) + vec[3:4, :]
    lr, li = lam_rows(vec, count)
    xr, xi = end_out[:, :half], end_out[:, half:]
    for t in range(u_out.shape[0] // count):
        rows = slice(t * count, (t + 1) * count)
        xr, xi = complex_step(lr, li, xr, xi, u_out[rows, :half], u_out[rows, half:])
    end_out[:, :half] = xr
    end_out[:, half:] = xi


def drive(wh, b, vec, count):
    total, width = wh.shape
    rows = STEPS * count
    return pl.pallas_call(
        drive_kernel,
        grid=(total // rows,),
        out_shape=(
            jax.ShapeDtypeStruct((total, width), F32),
            jax.ShapeDtypeStruct((count, width), F32),
        ),
        in_specs=[
            pl.BlockSpec((rows, width), lambda i: (i, 0)),
            whole(b.shape),
            whole(vec.shape),
        ],
        out_specs=(
            pl.BlockSpec((rows, width), lambda i: (i, 0)),
            whole((count, width)),
        ),
        compiler_params=LIMIT,
        name="drive",
    )(wh, b, vec)


def middle_kernel(
    span, base, u, wh, cotl, tok, carry, vec, c, ct, g, gt,
    block_out, st_out, act_out, dpre_out, dm_out, dst_out, end_out, sums_out, bias_out,
    state, sbuf, mix, pre, slope, dact, power,
):
    i = pl.program_id(0)
    count, width = end_out.shape
    half = width // 2
    rows = u.shape[0]
    steps = rows // count

    @pl.when(i == 0)
    def _():
        state[...] = carry[...]
        end_out[...] = jnp.zeros_like(end_out)
        sums_out[...] = jnp.zeros_like(sums_out)
        bias_out[...] = jnp.zeros_like(bias_out)
        power[:, :half] = jnp.ones((count, half), F32)
        power[:, half:] = jnp.zeros((count, half), F32)

    lr, li = lam_rows(vec, count)
    xr, xi = state[:, :half], state[:, half:]
    for t in range(steps):
        r = slice(t * count, (t + 1) * count)
        xr, xi = complex_step(lr, li, xr, xi, u[r, :half], u[r, half:])
        sbuf[r, :half] = xr
        sbuf[r, half:] = xi
    state[:, :half] = xr
    state[:, half:] = xi
    st_out[...] = sbuf[...].astype(BF)
    mix[...] = dot(st_out[...], c[...])
    part = 32
    for k in range(0, rows, part):
        r = slice(k, k + part)
        x = mix[r, :] + wh[r, :].astype(F32) * vec[4:5, :] + vec[5:6, :]
        sq = x * x
        th = jnp.tanh(x * (GELU_K + (GELU_K * 0.044715) * sq))
        q = 0.5 * th + 0.5
        a = x * q
        act_out[r, :] = a.astype(BF)
        slope[r, :] = q + a * (1.0 - q) * (2.0 * GELU_K + (6.0 * GELU_K * 0.044715) * sq)
    pre[...] = dot(act_out[...], g[...])
    seq_id = lax.broadcasted_iota(jnp.int32, (count, 128), 0)
    ends = jnp.zeros((count, 128), jnp.int32)
    for s in range(count):
        ends = jnp.where(seq_id == s, span[s], ends)
    first = base[0] + i * steps
    bias_v = jnp.zeros((count, width), F32)
    bias_g = jnp.zeros((count, width), F32)
    for k in range(0, rows, part):
        r = slice(k, k + part)
        v = pre[r, :width] + vec[6:7, :]
        gate = pre[r, width:] + vec[7:8, :]
        sig = 0.5 * jnp.tanh(0.5 * gate) + 0.5
        y = v * sig
        ct_live = cotl[r, :].astype(F32)
        dv = ct_live * sig
        dg = ct_live * y * (1.0 - sig)
        dpre_out[r, :width] = dv.astype(BF)
        dpre_out[r, width:] = dg.astype(BF)
        n = part // count
        bias_v = bias_v + jnp.sum(dv.reshape(n, count, width), axis=0)
        bias_g = bias_g + jnp.sum(dg.reshape(n, count, width), axis=0)
        t0 = k // count
        place = first + t0 + lax.broadcasted_iota(jnp.int32, (n, 1, 128), 0)
        live = jnp.where(place < ends[None], 1.0, 0.0)
        y = y.reshape(n, count, width) * jnp.concatenate([live] * (width // 128), axis=-1)
        mix[r, :] = y.reshape(part, width)
    bias_out[:, :width] += bias_v
    bias_out[:, width:] += bias_g
    for k in range(0, steps, 16):
        y = jnp.swapaxes(mix[k * count : (k + 16) * count, :].reshape(16, count, width), 0, 1)
        block_out[:, k : k + 16, :] = (tok[:, k : k + 16, :].astype(F32) + y).astype(BF)
    dact[...] = dot(dpre_out[...], gt[...])
    s1 = jnp.zeros((count, width), F32)
    s2 = jnp.zeros((count, width), F32)
    for k in range(0, rows, part):
        r = slice(k, k + part)
        d = dact[r, :] * slope[r, :]
        dm_out[r, :] = d.astype(BF)
        n = part // count
        s1 = s1 + jnp.sum((d * wh[r, :].astype(F32)).reshape(n, count, width), axis=0)
        s2 = s2 + jnp.sum(d.reshape(n, count, width), axis=0)
    sums_out[:, :width] += s1
    sums_out[:, width:] += s2
    dst_out[...] = dot(dm_out[...], ct[...])
    ar = jnp.zeros((count, half), F32)
    ai = jnp.zeros((count, half), F32)
    for t in range(steps - 1, -1, -1):
        r = slice(t * count, (t + 1) * count)
        ar, ai = complex_step(lr, -li, ar, ai, dst_out[r, :half], dst_out[r, half:])
    pr, pi = power[:, :half], power[:, half:]
    end_out[:, :half] += pr * ar - pi * ai
    end_out[:, half:] += pr * ai + pi * ar
    br, bi = lr, -li
    for _ in range(int(math.log2(steps))):
        br, bi = br * br - bi * bi, 2.0 * br * bi
    power[:, :half] = pr * br - pi * bi
    power[:, half:] = pr * bi + pi * br


def middle(span, base, u, wh, cotl, tok, carry, vec, c, ct, g, gt):
    total, width = u.shape
    count = carry.shape[0]
    length = total // count
    rows = STEPS * count
    smem = pl.BlockSpec(memory_space=pltpu.SMEM)

    def block(w):
        return pl.BlockSpec((rows, w), lambda i: (i, 0))

    side = pl.BlockSpec((count, STEPS, width), lambda i: (0, i, 0))
    return pl.pallas_call(
        middle_kernel,
        grid=(total // rows,),
        out_shape=(
            jax.ShapeDtypeStruct((count, length, width), BF),
            jax.ShapeDtypeStruct((total, width), BF),
            jax.ShapeDtypeStruct((total, width), BF),
            jax.ShapeDtypeStruct((total, 2 * width), BF),
            jax.ShapeDtypeStruct((total, width), BF),
            jax.ShapeDtypeStruct((total, width), F32),
            jax.ShapeDtypeStruct((count, width), F32),
            jax.ShapeDtypeStruct((count, 2 * width), F32),
            jax.ShapeDtypeStruct((count, 2 * width), F32),
        ),
        in_specs=[
            smem, smem, block(width), block(width), block(width), side, whole(carry.shape),
            whole(vec.shape), whole(c.shape), whole(ct.shape), whole(g.shape), whole(gt.shape),
        ],
        out_specs=(
            side, block(width), block(width), block(2 * width), block(width), block(width),
            whole((count, width)), whole((count, 2 * width)), whole((count, 2 * width)),
        ),
        scratch_shapes=[
            pltpu.VMEM((count, width), F32),
            pltpu.VMEM((rows, width), F32),
            pltpu.VMEM((rows, width), F32),
            pltpu.VMEM((rows, 2 * width), F32),
            pltpu.VMEM((rows, width), F32),
            pltpu.VMEM((rows, width), F32),
            pltpu.VMEM((count, width), F32),
        ],
        compiler_params=LIMIT,
        name="middle",
    )(span, base, u, wh, cotl, tok, carry, vec, c, ct, g, gt)


def weights_kernel(st, act, dpre, dm, gate_out, proj_out, acc_gate, acc_proj):
    i = pl.program_id(0)

    @pl.when(i == 0)
    def _():
        acc_gate[...] = jnp.zeros_like(acc_gate)
        acc_proj[...] = jnp.zeros_like(acc_proj)

    acc_gate[...] += dot_rows(act[...], dpre[...])
    acc_proj[...] += dot_rows(st[...], dm[...])

    @pl.when(i == pl.num_programs(0) - 1)
    def _():
        gate_out[...] = acc_gate[...].astype(BF)
        proj_out[...] = acc_proj[...].astype(BF)


def weights(st, act, dpre, dm):
    total, width = st.shape
    rows = 512

    def block(w):
        return pl.BlockSpec((rows, w), lambda i: (i, 0))

    return pl.pallas_call(
        weights_kernel,
        grid=(total // rows,),
        out_shape=(
            jax.ShapeDtypeStruct((width, 2 * width), BF),
            jax.ShapeDtypeStruct((width, width), BF),
        ),
        in_specs=[block(width), block(width), block(2 * width), block(width)],
        out_specs=(whole((width, 2 * width)), whole((width, width))),
        scratch_shapes=[pltpu.VMEM((width, 2 * width), F32), pltpu.VMEM((width, width), F32)],
        compiler_params=LIMIT,
        name="weights",
    )(st, act, dpre, dm)


def adjoint_kernel(dst, u, st, wht, back, carry, vec, adj_out, m_out, sums_out, now, acc):
    i = pl.program_id(0)
    count, width = back.shape
    half = width // 2
    rows = dst.shape[0]
    steps = rows // count

    @pl.when(i == 0)
    def _():
        now[...] = back[...]
        sums_out[...] = jnp.zeros_like(sums_out)
        acc[...] = jnp.zeros_like(acc)

    lr, li = lam_rows(vec, count)
    ar, ai = now[:, :half], now[:, half:]
    zero = jnp.zeros((count, half), F32)
    lsr, lsi, gam, csr, csi = zero, zero, zero, zero, zero
    for t in range(steps - 1, -1, -2):
        pair = slice((t - 1) * count, (t + 1) * count)
        both = st[pair, :].astype(F32)
        held = []
        for k in (1, 0):
            r = slice((t - 1 + k) * count, (t + k) * count)
            s = both[k * count : (k + 1) * count, :]
            sr, si = s[:, :half], s[:, half:]
            mr, mi = ar, ai
            if t == steps - 1 and k == 1:
                mr, mi = jnp.where(i == 0, 0.0, ar), jnp.where(i == 0, 0.0, ai)
            lsr = lsr + mr * sr + mi * si
            lsi = lsi + mi * sr - mr * si
            ar, ai = complex_step(lr, -li, ar, ai, dst[r, :half], dst[r, half:])
            gam = gam + ar * u[r, :half] + ai * u[r, half:]
            csr = csr + ar
            csi = csi + ai
            held.append(jnp.concatenate([ar, ai], axis=1))
        adj_out[pair, :] = jnp.concatenate([held[1], held[0]], axis=0).astype(BF)
    now[:, :half] = ar
    now[:, half:] = ai
    sums_out[0:count, :half] += lsr
    sums_out[0:count, half:] += lsi
    sums_out[count : 2 * count, :half] += csr
    sums_out[count : 2 * count, half:] += csi
    sums_out[2 * count :, :half] += gam
    acc[...] += dot(wht[...], adj_out[...])

    @pl.when(i == pl.num_programs(0) - 1)
    def _():
        cr, ci = carry[:, :half], carry[:, half:]
        sums_out[0:count, :half] += ar * cr + ai * ci
        sums_out[0:count, half:] += ai * cr - ar * ci
        m_out[...] = acc[...].astype(BF)


def adjoint(dst, u, st, wht, back, carry, vec):
    total, width = u.shape
    count = carry.shape[0]
    rows = STEPS * count
    blocks = total // rows

    def block(w):
        return pl.BlockSpec((rows, w), lambda i: (blocks - 1 - i, 0))

    return pl.pallas_call(
        adjoint_kernel,
        grid=(blocks,),
        out_shape=(
            jax.ShapeDtypeStruct((total, width), BF),
            jax.ShapeDtypeStruct((width, width), BF),
            jax.ShapeDtypeStruct((3 * count, width), F32),
        ),
        in_specs=[
            block(width), block(width), block(width),
            pl.BlockSpec((width, rows), lambda i: (0, blocks - 1 - i)),
            whole(back.shape), whole(carry.shape), whole(vec.shape),
        ],
        out_specs=(block(width), whole((width, width)), whole((3 * count, width))),
        scratch_shapes=[pltpu.VMEM((count, width), F32), pltpu.VMEM((width, width), F32)],
        compiler_params=LIMIT,
        name="adjoint",
    )(dst, u, st, wht, back, carry, vec)


def inputs_kernel(adj, dm, wh, inv, cot, bt, vec, grad_out, buf):
    count, steps, width = cot.shape
    buf[...] = dot(adj[...], bt[...])
    for k in range(0, steps, 16):
        r = slice(k * count, (k + 16) * count)
        w = wh[r, :].astype(F32)
        e = buf[r, :] + dm[r, :].astype(F32) * vec[4:5, :]
        mean = jnp.mean(e, axis=-1, keepdims=True)
        proj = jnp.mean(e * w, axis=-1, keepdims=True)
        wide = jnp.concatenate([inv[r, :]] * (width // 128), axis=-1)
        d = (e - mean - w * proj) * wide
        d = jnp.swapaxes(d.reshape(16, count, width), 0, 1)
        grad_out[:, k : k + 16, :] = (cot[:, k : k + 16, :].astype(F32) + d).astype(BF)


def inputs_gradient(adj, dm, wh, inv, cot, bt, vec):
    total, width = adj.shape
    count, length, _ = cot.shape
    rows = STEPS * count

    def block(w):
        return pl.BlockSpec((rows, w), lambda i: (i, 0))

    side = pl.BlockSpec((count, STEPS, width), lambda i: (0, i, 0))
    return pl.pallas_call(
        inputs_kernel,
        grid=(total // rows,),
        out_shape=jax.ShapeDtypeStruct(cot.shape, BF),
        in_specs=[
            block(width), block(width), block(width), block(128), side,
            whole(bt.shape), whole(vec.shape),
        ],
        out_specs=side,
        scratch_shapes=[pltpu.VMEM((rows, width), F32)],
        compiler_params=LIMIT,
        name="inputs_gradient",
    )(adj, dm, wh, inv, cot, bt, vec)


def swap(a, axis, size, bit):
    return lax.ppermute(a, axis, [(k, k ^ bit) for k in range(size)])


def spread(a, axis, size):
    parts = [a] + [swap(a, axis, size, k) for k in range(1, size)]
    return jnp.stack(parts)


def complex_mul(ar, ai, br, bi):
    return ar * br - ai * bi, ar * bi + ai * br


def carry_in(end, rates, length, place, axes_sizes, backward):
    half = end.shape[1] // 2
    rate, phase = rates[:half], rates[half:]
    sign = -1.0 if backward else 1.0

    def power(steps):
        steps = jnp.asarray(steps * length, F32)
        size = jnp.exp(-steps * rate)
        return size * jnp.cos(steps * phase), sign * size * jnp.sin(steps * phase)

    total_re, total_im = end[:, :half], end[:, half:]
    pre_re = jnp.zeros_like(total_re)
    pre_im = jnp.zeros_like(total_im)
    width = 1
    tm_size = axes_sizes["tmc"] * axes_sizes["core"]
    offset = place if not backward else tm_size - 1 - place
    while width < tm_size:
        both = jnp.concatenate([total_re, total_im], axis=1)
        if width == 1:
            got = swap(both, "core", 2, 1)
        else:
            got = swap(both, "tmc", axes_sizes["tmc"], width // 2)
        got_re, got_im = got[:, :half], got[:, half:]
        later = (offset // width) % 2 == 1
        ahead = offset % width
        mul_re, mul_im = power(ahead)
        add_re, add_im = complex_mul(mul_re, mul_im, got_re, got_im)
        pre_re = pre_re + jnp.where(later, add_re, 0.0)
        pre_im = pre_im + jnp.where(later, add_im, 0.0)
        wide_re, wide_im = power(width)
        first_re = jnp.where(later, got_re, total_re)
        first_im = jnp.where(later, got_im, total_im)
        last_re = jnp.where(later, total_re, got_re)
        last_im = jnp.where(later, total_im, got_im)
        move_re, move_im = complex_mul(wide_re, wide_im, first_re, first_im)
        total_re, total_im = last_re + move_re, last_im + move_im
        width *= 2
    return jnp.concatenate([pre_re, pre_im], axis=1)


def two_rows(row):
    high = row.astype(BF)
    return high, (row - high.astype(F32)).astype(BF)


def by_owner(row, owners):
    return row.reshape(owners, -1)


def reduce_to_owner(pack, core, chips):
    owners, rows, width = pack.shape
    halves = pack.reshape(chips, 2, rows, width)
    keep = lax.dynamic_index_in_dim(halves, core, 1, False)
    give = lax.dynamic_index_in_dim(halves, 1 - core, 1, False)
    got = swap(give, "core", 2, 1)
    both = (keep.astype(F32) + got.astype(F32)).astype(BF)
    parts = lax.all_to_all(both, CHIPS, 0, 0)
    return jnp.sum(parts.astype(F32), axis=0)


def make_body(sizes):
    chips = sizes["seq"] * sizes["tmc"]
    owners = chips * 2

    def body(
        tokens, lengths, cotangent, norm_gain, norm_shift, input_proj, decay_log, phase_log,
        gamma_log, output_proj, skip_gain, gate_weight, gate_bias,
    ):
        micro, per, length, width = tokens.shape
        count = micro * per
        half = width // 2
        core = lax.axis_index("core")
        chip_tm = lax.axis_index("tmc")
        tm_place = chip_tm * 2 + core
        place = lax.axis_index("seq") * (2 * sizes["tmc"]) + tm_place
        place_s = place.astype(jnp.int32).reshape(1)
        base = (tm_place * length).astype(jnp.int32).reshape(1)
        span = lengths.reshape(count)
        tok = tokens.reshape(count, length, width)
        cot = cotangent.reshape(count, length, width)

        gain = norm_gain.astype(F32)
        shift = norm_shift.astype(F32)
        skip = skip_gain.astype(F32)
        proj = input_proj.astype(F32)

        def placed(v):
            n = v.shape[0]
            wide = jnp.broadcast_to(v[None], (owners, n))
            mine = lax.broadcasted_iota(jnp.int32, (owners, n), 0) == place
            return jnp.where(mine, wide, jnp.zeros_like(wide)).reshape(owners * n)

        bias_row = placed(gate_bias)
        shifted = jnp.sum(shift[:, None] * proj, axis=0)
        shift_hi, shift_lo = two_rows(shifted)
        vec_rows = [
            placed(norm_gain), placed(norm_shift), placed(skip_gain),
            jnp.concatenate([placed(decay_log), placed(phase_log)]),
            jnp.concatenate([placed(gamma_log), placed(gamma_log)]),
            bias_row[:width], bias_row[width:], shift_hi, shift_lo,
        ]
        vec_rows = vec_rows + [jnp.zeros((width,), BF)] * (16 - len(vec_rows))
        scaled = (gain[:, None] * proj).astype(BF)
        first = jnp.concatenate([scaled, jnp.stack(vec_rows)], axis=0)
        rest = jnp.concatenate([output_proj, gate_weight[:, :width], gate_weight[:, width:]], axis=0)
        lead = first.shape[0]

        wh, wht, inv, cotl = prepare(span, base, tok, cot)

        n = width // owners
        if n % 16 == 0:
            along = spread(jnp.concatenate([first, rest], axis=0), "tmc", sizes["tmc"])
            own_first = spread(along[:, :lead], "seq", sizes["seq"]).reshape(chips, lead, width)
            other_first = swap(own_first, "core", 2, 1)
            b, bt, vec = assemble_first(place_s, own_first, other_first)
            own_rest = spread(along[:, lead:], "seq", sizes["seq"]).reshape(chips, -1, width)
            other_rest = swap(own_rest, "core", 2, 1)
        else:
            every = lax.all_gather(first, AXES)
            vec = jnp.concatenate(vector_rows(jnp.sum(every[:, n:].astype(F32), axis=0)), axis=0)
            b = (every[:, :n].reshape(width, width).astype(F32) * vec[2:3]).astype(BF)
            bt = b.T
            every = lax.all_gather(rest, AXES)
            c = every[:, :n].reshape(width, width)
            g = [every[:, k * n : (k + 1) * n].reshape(width, width) for k in (1, 2)]
            g = jnp.concatenate(g, axis=1)
            ct, gt = c.T, g.T

        u, end = drive(wh, b, vec, count)
        rates = vec[1]
        carry = carry_in(end, rates, length, tm_place, sizes, False)
        if n % 16 == 0:
            c, ct, g, gt = assemble_rest(place_s, own_rest, other_rest)
        block_out, st, act, dpre, dm, dst, back_end, sums, bias = middle(
            span, base, u, wh, cotl, tok, carry, vec, c, ct, g, gt
        )
        back = carry_in(back_end, rates, length, tm_place, sizes, True)
        gate_grad, proj_grad = weights(st, act, dpre, dm)
        sums = jnp.sum(sums, axis=0)
        bias = jnp.sum(bias, axis=0)
        small = [by_owner(r, owners) for v in (sums[:width], sums[width:], bias) for r in two_rows(v)]
        small = jnp.concatenate(small, axis=1)
        small = jnp.pad(small, ((0, 0), (0, width - small.shape[1])))[:, None, :]
        pack = jnp.concatenate(
            [
                proj_grad.reshape(owners, -1, width),
                gate_grad[:, :width].reshape(owners, -1, width),
                gate_grad[:, width:].reshape(owners, -1, width),
                jnp.pad(small, ((0, 0), (0, 7), (0, 0))),
            ],
            axis=1,
        )
        early = reduce_to_owner(pack, core, chips)

        adj, m, late = adjoint(dst, u, st, wht, back, carry, vec)
        late = jnp.sum(late.reshape(3, count, width), axis=1)
        col_hi, col_lo = two_rows(late[1])
        small = [
            by_owner(r, owners)
            for v in (late[0, :half], late[0, half:], late[2, :half])
            for r in two_rows(v)
        ]
        small = jnp.concatenate(small, axis=1)
        small = jnp.pad(small, ((0, 0), (0, width - small.shape[1])))[:, None, :]
        cols = jnp.broadcast_to(jnp.stack([col_hi, col_lo])[None], (owners, 2, width))
        pack = jnp.concatenate(
            [m.reshape(owners, -1, width), cols, small, jnp.zeros((owners, 5, width), BF)], axis=1
        )
        final = reduce_to_owner(pack, core, chips)
        tok_grad = inputs_gradient(adj, dm, wh, inv, cot, bt, vec)

        proj_sum = early[:n]
        gate_sum = jnp.concatenate([early[n : 2 * n], early[2 * n : 3 * n]], axis=1)
        row = early[3 * n]
        s1 = row[:n] + row[n : 2 * n]
        s2 = row[2 * n : 3 * n] + row[3 * n : 4 * n]
        bias_sum = row[4 * n : 6 * n] + row[6 * n : 8 * n]
        m_sum = final[:n]
        cols = final[n] + final[n + 1]
        row = final[n + 2]
        q = half // owners
        lam_re_sum = row[:q] + row[q : 2 * q]
        lam_im_sum = row[2 * q : 3 * q] + row[3 * q : 4 * q]
        gamma_grad = row[4 * q : 5 * q] + row[5 * q : 6 * q]
        scale = vec[2]
        in_grad = (gain[:, None] * m_sum + shift[:, None] * cols[None]) * scale[None]
        gain_grad = jnp.sum(m_sum * scale[None] * proj, axis=1) + skip * s1
        shift_grad = jnp.sum((cols * scale)[None] * proj, axis=1) + skip * s2
        skip_grad = gain * s1 + shift * s2
        rate = jnp.exp(decay_log.astype(F32))
        phase = jnp.exp(phase_log.astype(F32))
        modulus = jnp.exp(-rate)
        lam_re = modulus * jnp.cos(phase)
        lam_im = modulus * jnp.sin(phase)
        decay_grad = -rate * (lam_re_sum * lam_re + lam_im_sum * lam_im)
        phase_grad = phase * (lam_im_sum * lam_re - lam_re_sum * lam_im)
        return (
            block_out.reshape(tokens.shape), tok_grad.reshape(tokens.shape), gain_grad, shift_grad,
            in_grad, decay_grad, phase_grad, gamma_grad, proj_sum, skip_grad, gate_sum, bias_sum,
        )

    return body


def solution(mesh):
    seq, tm = mesh.shape["seq"], mesh.shape["tm"]
    fine = Mesh(mesh.devices.reshape(seq, tm // 2, 2), AXES)
    sizes = dict(zip(AXES, (seq, tm // 2, 2)))
    side = P(None, "seq", ("tmc", "core"), None)
    vec = P(AXES)
    mat = P(AXES, None)
    return jax.shard_map(
        make_body(sizes),
        mesh=fine,
        in_specs=(side, P(None, "seq"), side, vec, vec, mat, vec, vec, vec, mat, vec, mat, vec),
        out_specs=(side, side, vec, vec, mat, vec, vec, vec, mat, vec, mat, vec),
        check_vma=False,
    )
```

time: 1350 us -> 176 us (0.13); the launches traced: 1330 us -> 174 us
  blocking collectives: 401 us -> 0 us
  local copies, waits for them, and re-layouts: 333 us -> 10.1 us
  waiting for transfers between devices: 334 us -> 48 us
  other arithmetic: 196 us -> 22.6 us
  Pallas kernels: 0 us -> 67.9 us
  matrix products: 47 us -> 0 us
  starting transfers between devices: 0.16 us -> 24.2 us
  between operations: 18.5 us -> 1.26 us
    reduce_scatter x3 -> x0, waiting for transfers between devices: 333 us -> none  [the longest x1 136 us: body(): lax.psum_scatter(local_grads[8], ('seq', 'tm'), scatter_dimension=0, tile...]
    all_gather x21 -> x0, blocking collectives: 320 us -> none  [the longest x19 239 us: prefix(): gathered = jax.tree.map(lambda a: lax.all_gather(a, axis), part)]
    dynamic_slice x156 -> x0, local copies, waits for them, and re-layouts: 139 us -> none  [the longest x128 138 us: stretch_scan(): lax.scan(across, (start, start), (local_re, local_im))]
    dynamic_update_slice x128 -> x0, other arithmetic: 92.9 us -> none  [stretch_scan(): lax.scan(across, (start, start), (local_re, local_im))]
    unnamed x2 -> x0, blocking collectives: 80.4 us -> none
    pallas_call x0 -> x8, Pallas kernels: none -> 67.9 us  [the longest x1 20.1 us: middle(): pl.pallas_call(middle_kernel, grid=(total // rows,), out_shape=(jax.Shape...]
    rev x18 -> x0, local copies, waits for them, and re-layouts: 66.3 us -> none  [the longest x4 17.7 us: stretch_scan(): drive_im = drive_im[:, ::-1]]
    dot_general x36 -> x0, matrix products: 47 us -> none  [the longest x4 8.75 us: micro_step(): jnp.einsum('sck,hk->sch', d_pre, gate_weight, preferred_element_type=jnp....]
  transfers between devices with their start and end apart: 4 -> 21, of which waited for: 3 -> 11; matrix products, arithmetic and copies ran while one was open for 13% -> 10% of each run, Pallas kernels for 0% -> 20%
where the time goes in v1:
time: 176 us; the launch traced here: 174 us
  Pallas kernels  67.9 us (39%)
  waiting for transfers between devices  48 us (27%)
  starting transfers between devices  24.2 us (14%)
  other arithmetic  22.6 us (13%)
  local copies, waits for them, and re-layouts  10.1 us (6%)
    ppermute x19, waiting for transfers between devices, swap(): return lax.ppermute(a, axis, [(k, k ^ bit) for k in range(size)])  25.1 us
    all_to_all x2, waiting for transfers between devices, reduce_to_owner(): parts = lax.all_to_all(both, CHIPS, 0, 0)  22.9 us
    pallas_call x1, Pallas kernels, middle(): pl.pallas_call(middle_kernel, grid=(total // rows,), out_shape=(jax.Shape...  20.1 us
    ppermute x19, starting transfers between devices, swap(): return lax.ppermute(a, axis, [(k, k ^ bit) for k in range(size)])  16.2 us
    pallas_call x1, Pallas kernels, adjoint(): pl.pallas_call(adjoint_kernel, grid=(blocks,), out_shape=(jax.ShapeDtypeS...  9.87 us
    pallas_call x1, Pallas kernels, inputs_gradient(): pl.pallas_call(inputs_kernel, grid=(total // rows,), out_shape=jax.ShapeD...  9.23 us
    pallas_call x1, Pallas kernels, weights(): pl.pallas_call(weights_kernel, grid=(total // rows,), out_shape=(jax.Shap...  8.13 us
    all_to_all x2, starting transfers between devices, reduce_to_owner(): parts = lax.all_to_all(both, CHIPS, 0, 0)  7.97 us
  transfers between devices with their start and end apart: 21, of which 11 were waited for; matrix products, arithmetic and copies ran while one was open for 10% of the time, Pallas kernels for 20%

profile of v1, /device:TPU:0, one launch (start us, length us, event | category | flops | bytes accessed | tf_op | source)
XLA Modules:
  0.0 174.2 jit_solution(11588194184380454094)
XLA Ops:
  2.0 0.8 fusion.3
  3.7 0.8 broadcast_select_fusion.4
  4.8 0.8 broadcast_select_fusion.1
  5.9 0.7 fusion.17
  6.7 0.8 concatenate.68
  7.4 5.0 %collective-permute-start.2 = (bf16[80,512]{1,0:T(8,128)(2,1)S(1)}, bf16[80,512]{1,0:T(8,128)(2,1)S(1)}, u32[]{:S(2)}, u32[]{:S(2)}) collective-permute-start(bf16[80,512]{1,0:T(8,128)(2,1)S(1)} %concatenate.68), channel_id=1, source_target_pairs={{0,6},{2,4},{4,2},{6,0},{1,7},{3,5},{5,3},{7,1},{8,14},{10,12},{12... | collective-permute-start | bytes 245768 | tf_op jit(solution)/shard_map/ppermute | solution.py:517
  13.1 2.5 %collective-permute-done.2 = bf16[80,512]{1,0:T(8,128)(2,1)S(1)} collective-permute-done((bf16[80,512]{1,0:T(8,128)(2,1)S(1)}, bf16[80,512]{1,0:T(8,128)(2,1)S(1)}, u32[]{:S(2)}, u32[]{:S(2)}) %collective-permute-start.2) | collective-permute-done | bytes 81952 | tf_op jit(solution)/shard_map/ppermute | solution.py:517
  15.5 3.8 %collective-permute-done.1 = bf16[80,512]{1,0:T(8,128)(2,1)S(1)} collective-permute-done((bf16[80,512]{1,0:T(8,128)(2,1)S(1)}, bf16[80,512]{1,0:T(8,128)(2,1)S(1)}, u32[]{:S(2)}, u32[]{:S(2)}) %collective-permute-start.1) | collective-permute-done | bytes 81952 | tf_op jit(solution)/shard_map/ppermute | solution.py:517
  19.4 1.6 collective-permute-start.4
  21.0 1.5 collective-permute-start.3
  22.9 1.5 collective-permute-done.4
  24.4 2.5 %collective-permute-done.3 = bf16[4,32,512]{2,1,0:T(8,128)(2,1)S(1)} collective-permute-done((bf16[4,32,512]{2,1,0:T(8,128)(2,1)S(1)}, bf16[4,32,512]{2,1,0:T(8,128)(2,1)S(1)}, u32[]{:S(2)}, u32[]{:S(2)}) %collective-permute-start.3) | collective-permute-done | bytes 131104 | tf_op jit(solution)/shard_map/ppermute | solution.py:517
  26.9 1.7 collective-permute-done.5
  29.8 7.8 %prepare.1 = (bf16[2048,512]{1,0:T(8,128)(2,1)}, bf16[512,2048]{1,0:T(8,128)(2,1)}, f32[2048,128]{1,0:T(8,128)}, bf16[2048,512]{1,0:T(8,128)(2,1)}) custom-call(s32[8]{0:T(128)} %reshape.257.span, s32[1]{0:T(128)} %bitcast.base, bf16[8,256,512]{2,1,0:T(8,128)(2,1)} %bitcast.90, bf16[8,256,512]{2,1,0:T(8,128)(2,1)} %bitcast.92), custom_call_target="tpu_custom_call" | custom-call | tf_op jit(solution)/shard_map/prepare/pallas_call | solution.py:62
  37.6 1.2 collective-permute-start.10
  38.7 1.5 collective-permute-start.11
  40.2 0.9 collective-permute-start.12
  41.2 0.8 copy-done.3
  41.9 2.4 %assemble_first.1 = (bf16[512,512]{1,0:T(8,128)(2,1)}, bf16[512,512]{1,0:T(8,128)(2,1)}, f32[8,512]{1,0:T(8,128)}) custom-call(s32[1]{0:T(128)} %bitcast.3.place, bf16[16,32,512]{2,1,0:T(8,128)(2,1)} %bitcast.97, bf16[16,32,512]{2,1,0:T(8,128)(2,1)} %copy-done.3), custom_call_target="tpu_custom_call" | custom-call | tf_op jit(solution)/shard_map/assemble_first/pallas_call | solution.py:116
  44.3 7.2 %drive.1 = (f32[2048,512]{1,0:T(8,128)}, f32[8,512]{1,0:T(8,128)}) custom-call(bf16[2048,512]{1,0:T(8,128)(2,1)} %get-tuple-element.39.wh, bf16[512,512]{1,0:T(8,128)(2,1)} %get-tuple-element.40.b, f32[8,512]{1,0:T(8,128)} %get-tuple-element.41.vec), custom_call_target="tpu_custom_call" | custom-call | tf_op jit(solution)/shard_map/drive/pallas_call | solution.py:187
  51.5 0.9 multiply_multiply_fusion.2
  52.4 0.9 sine_multiply_fusion.1
  55.1 2.8 %collective-permute-done.8 = f32[8,512]{1,0:T(8,128)S(1)} collective-permute-done((f32[8,512]{1,0:T(8,128)S(1)}, f32[8,512]{1,0:T(8,128)S(1)}, u32[]{:S(2)}, u32[]{:S(2)}) %collective-permute-start.8) | collective-permute-done | bytes 16416 | tf_op jit(solution)/shard_map/ppermute | solution.py:517
  57.9 0.9 collective-permute-start.9
  58.8 0.8 multiply_multiply_fusion
  59.6 3.1 %collective-permute-done.9 = f32[8,512]{1,0:T(8,128)S(1)} collective-permute-done((f32[8,512]{1,0:T(8,128)S(1)}, f32[8,512]{1,0:T(8,128)S(1)}, u32[]{:S(2)}, u32[]{:S(2)}) %collective-permute-start.9) | collective-permute-done | bytes 16416 | tf_op jit(solution)/shard_map/ppermute | solution.py:517
  63.4 0.9 copy-done.2
  64.3 3.2 %assemble_rest.1 = (bf16[512,512]{1,0:T(8,128)(2,1)}, bf16[512,512]{1,0:T(8,128)(2,1)}, bf16[512,1024]{1,0:T(8,128)(2,1)}, bf16[1024,512]{1,0:T(8,128)(2,1)}) custom-call(s32[1]{0:T(128)} %bitcast.3.place, bf16[16,48,512]{2,1,0:T(8,128)(2,1)} %bitcast.95, bf16[16,48,512]{2,1,0:T(8,128)(2,1)} %copy-done.2), custom_call_target="tpu_custom_call" | custom-call | tf_op jit(solution)/shard_map/assemble_rest/pallas_call | solution.py:139
  67.5 20.1 %middle.1 = (bf16[8,256,512]{2,1,0:T(8,128)(2,1)}, bf16[2048,512]{1,0:T(8,128)(2,1)}, bf16[2048,512]{1,0:T(8,128)(2,1)}, bf16[2048,1024]{1,0:T(8,128)(2,1)}, bf1...) custom-call(s32[8]{0:T(128)} %reshape.257.span, ...), custom_call_target="tpu_custom_call" | custom-call | tf_op jit(solution)/shard_map/middle/pallas_call | solution.py:320
  87.6 0.8 reduce_sum.81
  88.6 8.1 %weights.1 = (bf16[512,1024]{1,0:T(8,128)(2,1)}, bf16[512,512]{1,0:T(8,128)(2,1)}) custom-call(bf16[2048,512]{1,0:T(8,128)(2,1)} %get-tuple-element.51.st, bf16[2048,512]{1,0:T(8,128)(2,1)} %get-tuple-element.60.act, bf16[2048,1024]{1,0:T(8,128)(2,1)} %get-tuple-element.61.dpre, bf16[2048,512]{1,0:T(8,128)(2,1)} %get-tuple-element.55.dm), custom_call_target="tpu_custom_call" | custom-call | tf_op jit(solution)/shard_map/weights/pallas_call | solution.py:380
  96.7 2.1 %fusion.15 = (bf16[512,512]{1,0:T(8,128)(2,1)S(1)}, bf16[512,512]{1,0:T(8,128)(2,1)}) fusion(bf16[512,1024]{1,0:T(8,128)(2,1)} %get-tuple-element.63), kind=kLoop, calls=%fused_computation.127 | loop fusion | bytes 2097152 | tf_op jit(solution)/shard_map/slice | solution.py:675
  99.5 3.2 %collective-permute-done.15 = f32[8,512]{1,0:T(8,128)S(1)} collective-permute-done((f32[8,512]{1,0:T(8,128)S(1)}, f32[8,512]{1,0:T(8,128)S(1)}, u32[]{:S(2)}, u32[]{:S(2)}) %collective-permute-start.15) | collective-permute-done | bytes 16416 | tf_op jit(solution)/shard_map/ppermute | solution.py:517
  103.6 3.9 %collective-permute-done.16 = f32[8,512]{1,0:T(8,128)S(1)} collective-permute-done((f32[8,512]{1,0:T(8,128)S(1)}, f32[8,512]{1,0:T(8,128)S(1)}, u32[]{:S(2)}, u32[]{:S(2)}) %collective-permute-start.16) | collective-permute-done | bytes 16416 | tf_op jit(solution)/shard_map/ppermute | solution.py:517
  108.1 9.9 %adjoint.1 = (bf16[2048,512]{1,0:T(8,128)(2,1)}, bf16[512,512]{1,0:T(8,128)(2,1)}, f32[24,512]{1,0:T(8,128)}) custom-call(f32[2048,512]{1,0:T(8,128)} %get-tuple-element.50.dst, f32[2048,512]{1,0:T(8,128)} %get-tuple-element.42.u, bf16[2048,512]{1,0:T(8,128)(2,1)} %get-tuple-element.51.st, bf16[512,2048]{1,0:T(8,128)(2,1)} %get-tuple-element.52.wht, ...), custom_call_target="tpu_custom_call" | custom-call | tf_op jit(solution)/shard_map/adjoint/pallas_call | solution.py:457
  118.0 0.8 bitcast_reduce_fusion
  119.3 1.4 maximum_maximum_fusion
  120.7 0.8 dynamic-slice_bitcast_fusion.1
  121.5 1.4 pad_maximum_fusion
  122.9 1.0 dynamic-slice_bitcast_fusion
  124.4 1.9 %fusion.1 = bf16[16,24,512]{2,1,0:T(8,128)(2,1)} fusion(bf16[16,24,512]{2,1,0:T(8,128)(2,1)} %collective-permute-done.17, bf16[16,2,24,512]{3,2,1,0:T(8,128)(2,1)S(1)} %maximum_maximum_fusion, s32[]{:T(128)S(6)} %select_n.322), kind=kLoop, calls=%fused_computation.8 | loop fusion | flops 786432 | bytes 1179652 | tf_op jit(solution)/shard_map/convert_element_type | solution.py:584
  126.2 4.3 %all-to-all-start = ((bf16[16,24,512]{2,1,0:T(8,128)(2,1)}), bf16[16,24,512]{2,1,0:T(8,128)(2,1)S(1)}, u32[]{:S(2)}, u32[]{:S(2)}) async-start(bf16[16,24,512]{2,1,0:T(8,128)(2,1)} %fusion.1), calls=%async_computation | async-start | bytes 786432 | tf_op jit(solution)/shard_map/all_to_all | solution.py:585
  130.6 2.4 %fusion = bf16[16,56,512]{2,1,0:T(8,128)(2,1)} fusion(bf16[16,56,512]{2,1,0:T(8,128)(2,1)} %collective-permute-done.18, bf16[16,2,56,512]{3,2,1,0:T(8,128)(2,1)S(1)} %pad_maximum_fusion, s32[]{:T(128)S(6)} %select_n.322), kind=kLoop, calls=%fused_computation.2 | loop fusion | flops 1835008 | bytes 2752516 | tf_op jit(solution)/shard_map/convert_element_type | solution.py:584
  133.0 11.2 %all-to-all-done = bf16[16,24,512]{2,1,0:T(8,128)(2,1)S(1)} async-done(((bf16[16,24,512]{2,1,0:T(8,128)(2,1)}), bf16[16,24,512]{2,1,0:T(8,128)(2,1)S(1)}, u32[]{:S(2)}, u32[]{:S(2)}) %all-to-all-start) | async-done | bytes 393248 | tf_op jit(solution)/shard_map/all_to_all | solution.py:585
  144.1 3.6 %all-to-all-start.1 = ((bf16[16,56,512]{2,1,0:T(8,128)(2,1)}), bf16[16,56,512]{2,1,0:T(8,128)(2,1)S(1)}, u32[]{:S(2)}, u32[]{:S(2)}) async-start(bf16[16,56,512]{2,1,0:T(8,128)(2,1)} %fusion), calls=%async_computation.1 | async-start | bytes 1835008 | tf_op jit(solution)/shard_map/all_to_all | solution.py:585
  147.8 9.2 %inputs_gradient.1 = bf16[8,256,512]{2,1,0:T(8,128)(2,1)} custom-call(bf16[2048,512]{1,0:T(8,128)(2,1)} %get-tuple-element.54.adj, bf16[2048,512]{1,0:T(8,128)(2,1)} %get-tuple-element.55.dm, bf16[2048,512]{1,0:T(8,128)(2,1)} %get-tuple-element.39.wh, f32[2048,128]{1,0:T(8,128)} %get-tuple-element.56.inv, bf16[8,256,512]{2,1,0:T(8,128)(2,1)} %bitcast.93, ...), custom_call_target="tpu_custom_call" | custom-call | tf_op jit(solution)/shard_map/inputs_gradient/pallas_call | solution.py:501
  159.0 0.8 fusion.5
  159.8 11.7 %all-to-all-done.1 = bf16[16,56,512]{2,1,0:T(8,128)(2,1)S(1)} async-done(((bf16[16,56,512]{2,1,0:T(8,128)(2,1)}), bf16[16,56,512]{2,1,0:T(8,128)(2,1)S(1)}, u32[]{:S(2)}, u32[]{:S(2)}) %all-to-all-start.1) | async-done | bytes 917536 | tf_op jit(solution)/shard_map/all_to_all | solution.py:585
  (125 shorter events, 15.1 us)
Async XLA Ops:
  0.6 28.3 %copy-start.12 = (s32[4,2]{0,1:T(2,128)S(1)}, s32[4,2]{0,1:T(2,128)}, u32[]{:S(2)}) copy-start(s32[4,2]{0,1:T(2,128)} %param.14) | copy-start | bytes 100
  7.4 8.1 %collective-permute-start.2 = (bf16[80,512]{1,0:T(8,128)(2,1)S(1)}, bf16[80,512]{1,0:T(8,128)(2,1)S(1)}, u32[]{:S(2)}, u32[]{:S(2)}) collective-permute-start(bf16[80,512]{1,0:T(8,128)(2,1)S(1)} %concatenate.68), channel_id=1, source_target_pairs={{0,6},{2,4},{4,2},{6,0},{1,7},{3,5},{5,3},{7,1},{8,14},{10,12},{12... | collective-permute-start | bytes 245768 | tf_op jit(solution)/shard_map/ppermute | solution.py:517
  12.5 6.9 %collective-permute-start.1 = (bf16[80,512]{1,0:T(8,128)(2,1)S(1)}, bf16[80,512]{1,0:T(8,128)(2,1)S(1)}, u32[]{:S(2)}, u32[]{:S(2)}) collective-permute-start(bf16[80,512]{1,0:T(8,128)(2,1)S(1)} %concatenate.68), channel_id=1, source_target_pairs={{0,4},{2,6},{4,0},{6,2},{1,5},{3,7},{5,1},{7,3},{8,12},{10,14},{12... | collective-permute-start | bytes 245768 | tf_op jit(solution)/shard_map/ppermute | solution.py:517
  12.5 6.9 %collective-permute-start = (bf16[80,512]{1,0:T(8,128)(2,1)S(1)}, bf16[80,512]{1,0:T(8,128)(2,1)S(1)}, u32[]{:S(2)}, u32[]{:S(2)}) collective-permute-start(bf16[80,512]{1,0:T(8,128)(2,1)S(1)} %concatenate.68), channel_id=1, source_target_pairs={{0,2},{2,0},{4,6},{6,4},{1,3},{3,1},{5,7},{7,5},{8,10},{10,8},{12,... | collective-permute-start | bytes 245768 | tf_op jit(solution)/shard_map/ppermute | solution.py:517
  19.4 5.0 %collective-permute-start.4 = (bf16[4,32,512]{2,1,0:T(8,128)(2,1)S(1)}, bf16[4,32,512]{2,1,0:T(8,128)(2,1)S(1)}, u32[]{:S(2)}, u32[]{:S(2)}) collective-permute-start(bf16[4,32,512]{2,1,0:T(8,128)(2,1)S(1)} %pad_maximum_fusion.6), channel_id=1, source_target_pairs={{0,16},{8,24},{16,0},{24,8},{1,17},{9,25},{17,1},{25,9},{2,18},{10... | collective-permute-start | bytes 393224 | tf_op jit(solution)/shard_map/ppermute | solution.py:517
  21.0 6.0 %collective-permute-start.3 = (bf16[4,32,512]{2,1,0:T(8,128)(2,1)S(1)}, bf16[4,32,512]{2,1,0:T(8,128)(2,1)S(1)}, u32[]{:S(2)}, u32[]{:S(2)}) collective-permute-start(bf16[4,32,512]{2,1,0:T(8,128)(2,1)S(1)} %pad_maximum_fusion.6), channel_id=1, source_target_pairs={{0,8},{8,0},{16,24},{24,16},{1,9},{9,1},{17,25},{25,17},{2,10},{10... | collective-permute-start | bytes 393224 | tf_op jit(solution)/shard_map/ppermute | solution.py:517
  22.4 6.2 %collective-permute-start.5 = (bf16[4,32,512]{2,1,0:T(8,128)(2,1)S(1)}, bf16[4,32,512]{2,1,0:T(8,128)(2,1)S(1)}, u32[]{:S(2)}, u32[]{:S(2)}) collective-permute-start(bf16[4,32,512]{2,1,0:T(8,128)(2,1)S(1)} %pad_maximum_fusion.6), channel_id=1, source_target_pairs={{0,24},{8,16},{16,8},{24,0},{1,25},{9,17},{17,9},{25,1},{2,26},{10... | collective-permute-start | bytes 393224 | tf_op jit(solution)/shard_map/ppermute | solution.py:517
  28.7 8.8 %copy-start.1 = (bf16[4,4,32,512]{3,2,1,0:T(8,128)(2,1)}, bf16[4,4,32,512]{3,2,1,0:T(8,128)(2,1)S(1)}, u32[]{:S(2)}) copy-start(bf16[4,4,32,512]{3,2,1,0:T(8,128)(2,1)S(1)} %pad_maximum_fusion.2) | copy-start | bytes 1572868
  28.8 12.4 %collective-permute-start.6 = (bf16[16,32,512]{2,1,0:T(8,128)(2,1)S(1)}, bf16[16,32,512]{2,1,0:T(8,128)(2,1)S(1)}, u32[]{:S(2)}, u32[]{:S(2)}) collective-permute-start(bf16[16,32,512]{2,1,0:T(8,128)(2,1)S(1)} %bitcast.96), channel_id=1, source_target_pairs={{0,1},{1,0},{2,3},{3,2},{4,5},{5,4},{6,7},{7,6},{8,9},{9,8},{10,11... | collective-permute-start | bytes 1572872 | tf_op jit(solution)/shard_map/ppermute | solution.py:517
  37.6 17.1 %collective-permute-start.10 = (bf16[4,48,512]{2,1,0:T(8,128)(2,1)S(1)}, bf16[4,48,512]{2,1,0:T(8,128)(2,1)S(1)}, u32[]{:S(2)}, u32[]{:S(2)}) collective-permute-start(bf16[4,48,512]{2,1,0:T(8,128)(2,1)S(1)} %pad_maximum_fusion.3), channel_id=1, source_target_pairs={{0,8},{8,0},{16,24},{24,16},{1,9},{9,1},{17,25},{25,17},{2,10},{10... | collective-permute-start | bytes 589832 | tf_op jit(solution)/shard_map/ppermute | solution.py:517
  38.7 15.9 %collective-permute-start.11 = (bf16[4,48,512]{2,1,0:T(8,128)(2,1)S(1)}, bf16[4,48,512]{2,1,0:T(8,128)(2,1)S(1)}, u32[]{:S(2)}, u32[]{:S(2)}) collective-permute-start(bf16[4,48,512]{2,1,0:T(8,128)(2,1)S(1)} %pad_maximum_fusion.3), channel_id=1, source_target_pairs={{0,16},{8,24},{16,0},{24,8},{1,17},{9,25},{17,1},{25,9},{2,18},{10... | collective-permute-start | bytes 589832 | tf_op jit(solution)/shard_map/ppermute | solution.py:517
  40.2 14.4 %collective-permute-start.12 = (bf16[4,48,512]{2,1,0:T(8,128)(2,1)S(1)}, bf16[4,48,512]{2,1,0:T(8,128)(2,1)S(1)}, u32[]{:S(2)}, u32[]{:S(2)}) collective-permute-start(bf16[4,48,512]{2,1,0:T(8,128)(2,1)S(1)} %pad_maximum_fusion.3), channel_id=1, source_target_pairs={{0,24},{8,16},{16,8},{24,0},{1,25},{9,17},{17,9},{25,1},{2,26},{10... | collective-permute-start | bytes 589832 | tf_op jit(solution)/shard_map/ppermute | solution.py:517
  41.1 0.8 copy-start.3
  51.5 1.8 %collective-permute-start.7 = (f32[8,512]{1,0:T(8,128)}, f32[8,512]{1,0:T(8,128)S(1)}, u32[]{:S(2)}, u32[]{:S(2)}) collective-permute-start(f32[8,512]{1,0:T(8,128)} %get-tuple-element.44), channel_id=1, source_target_pairs={{0,1},{1,0},{2,3},{3,2},{4,5},{5,4},{6,7},{7,6},{8,9},{9,8},{10,11... | collective-permute-start | bytes 49160 | tf_op jit(solution)/shard_map/ppermute | solution.py:517
  54.1 3.8 %collective-permute-start.8 = (f32[8,512]{1,0:T(8,128)S(1)}, f32[8,512]{1,0:T(8,128)S(1)}, u32[]{:S(2)}, u32[]{:S(2)}) collective-permute-start(f32[8,512]{1,0:T(8,128)S(1)} %pad_maximum_fusion.8), channel_id=1, source_target_pairs={{0,2},{2,0},{4,6},{6,4},{1,3},{3,1},{5,7},{7,5},{8,10},{10,8},{12,... | collective-permute-start | bytes 49160 | tf_op jit(solution)/shard_map/ppermute | solution.py:517
  54.8 8.6 %copy-start = (bf16[4,4,48,512]{3,2,1,0:T(8,128)(2,1)}, bf16[4,4,48,512]{3,2,1,0:T(8,128)(2,1)S(1)}, u32[]{:S(2)}) copy-start(bf16[4,4,48,512]{3,2,1,0:T(8,128)(2,1)S(1)} %pad_maximum_fusion.1) | copy-start | bytes 2359300
  54.8 8.6 %collective-permute-start.13 = (bf16[16,48,512]{2,1,0:T(8,128)(2,1)S(1)}, bf16[16,48,512]{2,1,0:T(8,128)(2,1)S(1)}, u32[]{:S(2)}, u32[]{:S(2)}) collective-permute-start(bf16[16,48,512]{2,1,0:T(8,128)(2,1)S(1)} %bitcast.94), channel_id=1, source_target_pairs={{0,1},{1,0},{2,3},{3,2},{4,5},{5,4},{6,7},{7,6},{8,9},{9,8},{10,11... | collective-permute-start | bytes 2359304 | tf_op jit(solution)/shard_map/ppermute | solution.py:517
  57.9 4.8 %collective-permute-start.9 = (f32[8,512]{1,0:T(8,128)S(1)}, f32[8,512]{1,0:T(8,128)S(1)}, u32[]{:S(2)}, u32[]{:S(2)}) collective-permute-start(f32[8,512]{1,0:T(8,128)S(1)} %pad_maximum_fusion.9), channel_id=1, source_target_pairs={{0,4},{2,6},{4,0},{6,2},{1,5},{3,7},{5,1},{7,3},{8,12},{10,14},{12... | collective-permute-start | bytes 49160 | tf_op jit(solution)/shard_map/ppermute | solution.py:517
  63.4 0.9 copy-start.2
  88.5 10.3 %collective-permute-start.14 = (f32[8,512]{1,0:T(8,128)}, f32[8,512]{1,0:T(8,128)S(1)}, u32[]{:S(2)}, u32[]{:S(2)}) collective-permute-start(f32[8,512]{1,0:T(8,128)} %get-tuple-element.53), channel_id=1, source_target_pairs={{0,1},{1,0},{2,3},{3,2},{4,5},{5,4},{6,7},{7,6},{8,9},{9,8},{10,11... | collective-permute-start | bytes 49160 | tf_op jit(solution)/shard_map/ppermute | solution.py:517
  96.7 2.1 %copy-start.5 = (f32[8,1024]{1,0:T(8,128)S(1)}, f32[8,1024]{1,0:T(8,128)}, u32[]{:S(2)}) copy-start(f32[8,1024]{1,0:T(8,128)} %get-tuple-element.65) | copy-start | bytes 98308
  96.7 2.2 %copy-start.6 = (f32[8,512]{1,0:T(8,128)S(1)}, f32[8,512]{1,0:T(8,128)}, u32[]{:S(2)}) copy-start(f32[8,512]{1,0:T(8,128)} %get-tuple-element.53) | copy-start | bytes 49156
  98.9 3.8 %collective-permute-start.15 = (f32[8,512]{1,0:T(8,128)S(1)}, f32[8,512]{1,0:T(8,128)S(1)}, u32[]{:S(2)}, u32[]{:S(2)}) collective-permute-start(f32[8,512]{1,0:T(8,128)S(1)} %pad_maximum_fusion.11), channel_id=1, source_target_pairs={{0,2},{2,0},{4,6},{6,4},{1,3},{3,1},{5,7},{7,5},{8,10},{10,8},{12,... | collective-permute-start | bytes 49160 | tf_op jit(solution)/shard_map/ppermute | solution.py:517
  102.7 4.7 %collective-permute-start.16 = (f32[8,512]{1,0:T(8,128)S(1)}, f32[8,512]{1,0:T(8,128)S(1)}, u32[]{:S(2)}, u32[]{:S(2)}) collective-permute-start(f32[8,512]{1,0:T(8,128)S(1)} %pad_maximum_fusion.12), channel_id=1, source_target_pairs={{0,4},{2,6},{4,0},{6,2},{1,5},{3,7},{5,1},{7,3},{8,12},{10,14},{12... | collective-permute-start | bytes 49160 | tf_op jit(solution)/shard_map/ppermute | solution.py:517
  121.5 2.9 %collective-permute-start.17 = (bf16[16,24,512]{2,1,0:T(8,128)(2,1)}, bf16[16,24,512]{2,1,0:T(8,128)(2,1)}, u32[]{:S(2)}, u32[]{:S(2)}) collective-permute-start(bf16[16,24,512]{2,1,0:T(8,128)(2,1)} %dynamic-slice_bitcast_fusion.1), channel_id=1, source_target_pairs={{0,1},{1,0},{2,3},{3,2},{4,5},{5,4},{6,7},{7,6},{8,9},{9,8},{10,11... | collective-permute-start | bytes 1179656 | tf_op jit(solution)/shard_map/ppermute | solution.py:517
  123.9 6.7 %collective-permute-start.18 = (bf16[16,56,512]{2,1,0:T(8,128)(2,1)}, bf16[16,56,512]{2,1,0:T(8,128)(2,1)}, u32[]{:S(2)}, u32[]{:S(2)}) collective-permute-start(bf16[16,56,512]{2,1,0:T(8,128)(2,1)} %dynamic-slice_bitcast_fusion), channel_id=1, source_target_pairs={{0,1},{1,0},{2,3},{3,2},{4,5},{5,4},{6,7},{7,6},{8,9},{9,8},{10,11... | collective-permute-start | bytes 2752520 | tf_op jit(solution)/shard_map/ppermute | solution.py:517
  126.2 17.9 %all-to-all-start = ((bf16[16,24,512]{2,1,0:T(8,128)(2,1)}), bf16[16,24,512]{2,1,0:T(8,128)(2,1)S(1)}, u32[]{:S(2)}, u32[]{:S(2)}) async-start(bf16[16,24,512]{2,1,0:T(8,128)(2,1)} %fusion.1), calls=%async_computation | async-start | bytes 786432 | tf_op jit(solution)/shard_map/all_to_all | solution.py:585
  144.1 27.5 %all-to-all-start.1 = ((bf16[16,56,512]{2,1,0:T(8,128)(2,1)}), bf16[16,56,512]{2,1,0:T(8,128)(2,1)S(1)}, u32[]{:S(2)}, u32[]{:S(2)}) async-start(bf16[16,56,512]{2,1,0:T(8,128)(2,1)} %fusion), calls=%async_computation.1 | async-start | bytes 1835008 | tf_op jit(solution)/shard_map/all_to_all | solution.py:585
  147.8 9.9 %copy-start.10 = (bf16[8]{0:T(256)(128)(2,1)S(1)}, bf16[8]{0:T(256)(128)(2,1)}, u32[]{:S(2)}) copy-start(bf16[8]{0:T(256)(128)(2,1)} %param.20) | copy-start | bytes 52
  147.8 9.9 %copy-start.11 = (bf16[8]{0:T(256)(128)(2,1)S(1)}, bf16[8]{0:T(256)(128)(2,1)}, u32[]{:S(2)}) copy-start(bf16[8]{0:T(256)(128)(2,1)} %param.19) | copy-start | bytes 52
  147.8 11.2 %copy-start.4 = (bf16[16,512]{1,0:T(8,128)(2,1)S(1)}, bf16[16,512]{1,0:T(8,128)(2,1)}, u32[]{:S(2)}) copy-start(bf16[16,512]{1,0:T(8,128)(2,1)} %param.18) | copy-start | bytes 49156
  147.8 25.1 %copy-start.7 = (bf16[16]{0:T(256)(128)(2,1)S(1)}, bf16[16]{0:T(256)(128)(2,1)}, u32[]{:S(2)}) copy-start(bf16[16]{0:T(256)(128)(2,1)} %param.17) | copy-start | bytes 100
  147.8 25.1 %copy-start.8 = (bf16[16]{0:T(256)(128)(2,1)S(1)}, bf16[16]{0:T(256)(128)(2,1)}, u32[]{:S(2)}) copy-start(bf16[16]{0:T(256)(128)(2,1)} %param.16) | copy-start | bytes 100
  147.8 25.1 %copy-start.9 = (bf16[16]{0:T(256)(128)(2,1)S(1)}, bf16[16]{0:T(256)(128)(2,1)}, u32[]{:S(2)}) copy-start(bf16[16]{0:T(256)(128)(2,1)} %param.23) | copy-start | bytes 100

commit v2 on v0

v2 whole, which is shorter than its diff:
```python
import math

import jax
import jax.numpy as jnp
from jax import lax
from jax.experimental import pallas as pl
from jax.experimental.pallas import tpu as pltpu
from jax.sharding import Mesh, PartitionSpec as P

F32 = jnp.float32
BF = jnp.bfloat16
AXES = ("seq", "tmc", "core")
GELU_K = math.sqrt(2.0 / math.pi)
VMEM = pl.BlockSpec(memory_space=pltpu.VMEM)
SIDE = 128
AHEAD = 4


def dot(a, b, ca=1, cb=0):
    return lax.dot_general(a, b, (((ca,), (cb,)), ((), ())), preferred_element_type=F32)


def call(body, name, outs, ins, scratch=(), limit=8, far_in=(), far_out=(), copies=0):
    far = pl.BlockSpec(memory_space=pltpu.HBM)
    ins = [
        pltpu.with_memory_space_constraint(a, pltpu.HBM) if k in far_in else a
        for k, a in enumerate(ins)
    ]
    scratch = [pltpu.VMEM(s, t) for s, t in scratch]
    return pl.pallas_call(
        body,
        out_shape=[
            pltpu.HBM(s, t) if k in far_out else jax.ShapeDtypeStruct(s, t)
            for k, (s, t) in enumerate(outs)
        ],
        in_specs=[far if k in far_in else VMEM for k in range(len(ins))],
        out_specs=[far if k in far_out else VMEM for k in range(len(outs))],
        scratch_shapes=scratch + ([pltpu.SemaphoreType.DMA((copies,))] if copies else []),
        compiler_params=pltpu.CompilerParams(vmem_limit_bytes=limit << 20),
        cost_estimate=pl.CostEstimate(flops=0, bytes_accessed=0, transcendentals=0),
        name=name,
    )(*ins)


class Copies:
    def __init__(self, sems):
        self.sems, self.count, self.out = sems, 0, []

    def start(self, src, dest, index):
        copy = pltpu.make_async_copy(src.at[index], dest.at[index], self.sems.at[self.count])
        copy.start()
        self.count += 1
        return copy

    def send(self, src, dest, index):
        self.out.append(self.start(src, dest, index))

    def finish(self):
        for copy in self.out:
            copy.wait()


def time_place():
    return (lax.axis_index("tmc") * 2 + lax.axis_index("core")).astype(jnp.int32)


def device_place():
    seq = lax.axis_index("seq").astype(jnp.int32)
    return seq * (2 * lax.axis_size("tmc")) + time_place()


def split(v):
    high = v.astype(BF)
    return high, (v - high.astype(F32)).astype(BF)


def complex_mul(ar, ai, br, bi):
    return ar * br - ai * bi, ar * bi + ai * br


def complex_step(lr, li, xr, xi, ur, ui):
    return lr * xr - li * xi + ur, lr * xi + li * xr + ui


def lam_rows(vec, count):
    half = vec.shape[1] // 2
    return (
        jnp.broadcast_to(vec[0:1, :half], (count, half)),
        jnp.broadcast_to(vec[0:1, half:], (count, half)),
    )


def swap_order(a, count):
    rows, width = a.shape
    return jnp.swapaxes(a.reshape(rows // count, count, width), 0, 1)


def pack_kernel(*refs):
    far, pack, flag, near, sems = refs[:10], refs[10], refs[11], refs[12:22], refs[22]
    flag[...] = jnp.broadcast_to(lax.axis_index("core").astype(F32), flag.shape)
    copies = [pltpu.make_async_copy(a, b, sems.at[k]) for k, (a, b) in enumerate(zip(far, near))]
    for copy in copies:
        copy.start()
    for copy in copies:
        copy.wait()
    gain, shift, skip, decay, phase, gamma, bias, proj, out_proj, gate = near
    n, width = proj.shape
    half = width // 2
    place = device_place()

    def at(v, size, start):
        length = v.shape[1]
        lane = lax.broadcasted_iota(jnp.int32, (length, size), 1)
        row = lax.broadcasted_iota(jnp.int32, (length, size), 0)
        pick = jnp.where(lane == row + length * place + start, 1.0, 0.0).astype(BF)
        return dot(v[...], pick)

    diag = lax.broadcasted_iota(jnp.int32, (n, n), 0) == lax.broadcasted_iota(jnp.int32, (n, n), 1)
    spread_gain = jnp.where(diag, jnp.broadcast_to(gain[...].astype(F32), (n, n)), 0.0).astype(BF)
    pack[0:n, :] = dot(spread_gain, proj[...]).astype(BF)
    moved = dot(shift[...], proj[...])
    bias_row = at(bias, 2 * width, 0)
    rows = [
        at(gain, width, 0), at(shift, width, 0), at(skip, width, 0),
        at(decay, width, 0) + at(phase, width, half),
        at(gamma, width, 0) + at(gamma, width, half),
        bias_row[:, :width], bias_row[:, width:], moved,
    ]
    pack[n : n + 8, :] = jnp.concatenate(rows, axis=0).astype(BF)
    for k, rest in enumerate((out_proj[...], gate[:, :width], gate[:, width:])):
        pack[(k + 1) * n + 8 : (k + 2) * n + 8, :] = rest


def whiten_kernel(tok, wh_out, inv_far, inv_out, sems):
    copies = Copies(sems)
    count, length, width = tok.shape
    part = 16
    for i in range(0, length, part):
        x = tok[:, i : i + part, :].astype(F32)
        mean = jnp.mean(x, axis=-1, keepdims=True)
        c = x - mean
        inv = lax.rsqrt(jnp.mean(c * c, axis=-1, keepdims=True) + 1e-05)
        rows = slice(i * count, (i + part) * count)
        wh_out[rows, :] = jnp.swapaxes(c * inv, 0, 1).reshape(part * count, width).astype(BF)
        wide = jnp.broadcast_to(inv, (count, part, SIDE))
        inv_out[rows, :] = jnp.swapaxes(wide, 0, 1).reshape(part * count, SIDE)
        if (i + part) % 64 == 0:
            copies.send(inv_out, inv_far, pl.ds((i + part - 64) * count, 64 * count))
    copies.finish()


def live_rows(lengths, start, steps, length, width):
    per, micro = lengths.shape
    used = lengths[...]
    ends = [
        jnp.broadcast_to(used[k : k + 1, m : m + 1], (1, SIDE)) for m in range(micro) for k in range(per)
    ]
    count = len(ends)
    ends = jnp.concatenate(ends, axis=0).reshape(count, 1, SIDE)
    first = time_place() * length + start
    place = first + lax.broadcasted_iota(jnp.int32, (count, steps, SIDE), 1)
    live = jnp.where(place < ends, 1.0, 0.0)
    return jnp.concatenate([live] * (width // SIDE), axis=-1)


def mask_kernel(ends, cot, out):
    count, length, width = cot.shape
    part = 16
    for i in range(0, length, part):
        live = live_rows(ends, i, part, length, width)
        y = jnp.swapaxes(cot[:, i : i + part, :].astype(F32) * live, 0, 1)
        out[i * count : (i + part) * count, :] = y.reshape(part * count, width)


def assemble(dests, own, other, start):
    place = device_place()
    for half, ref in enumerate((own, other)):
        for q in range(own.shape[0]):
            owner = jnp.bitwise_xor(place, 2 * q + half)
            row = pl.multiple_of(owner * 16, 16)
            for k, d in enumerate(dests):
                d[pl.ds(row, 16), :] = ref[q, start + 16 * k : start + 16 * (k + 1), :]


def vector_rows(acc):
    half = acc.shape[1] // 2
    gain, shift, skip = acc[0:1], acc[1:2], acc[2:3]
    rate = jnp.exp(acc[3:4, :half])
    phase = jnp.exp(acc[3:4, half:])
    scale = jnp.exp(acc[4:5])
    modulus = jnp.exp(-rate)
    lam = jnp.concatenate([modulus * jnp.cos(phase), modulus * jnp.sin(phase)], axis=1)
    shifted = acc[7:8] * scale
    bias = 0.5 * acc[5:7]
    return (lam, scale, shifted, skip * gain, skip * shift, bias[0:1], bias[1:2], gain)


def power_rows(lam, length, bits, place):
    half = lam.shape[1] // 2
    re, im = lam[:, :half], lam[:, half:]
    for _ in range(length.bit_length() - 1):
        re, im = complex_mul(re, im, re, im)
    one, zero = jnp.ones_like(re), jnp.zeros_like(re)
    now = {False: (one, zero), True: (one, zero)}
    rows, masks = [], []
    for bit in range(bits):
        taken = lax.rem(lax.shift_right_logical(place, bit), 2) == 1
        rows.append(jnp.concatenate([re, im], axis=1))
        for backward in (False, True):
            later = jnp.logical_not(taken) if backward else taken
            pr, pi = now[backward]
            sign = -1.0 if backward else 1.0
            row = jnp.concatenate([pr, sign * pi], axis=1)
            rows.append(jnp.where(later, row, 0.0))
            nr, ni = complex_mul(pr, pi, re, im)
            now[backward] = (jnp.where(later, nr, pr), jnp.where(later, ni, pi))
        rows.append(jnp.concatenate([re, -im], axis=1))
        masks.append(jnp.where(taken, 1.0, jnp.zeros((1, 2 * half), F32)))
        re, im = complex_mul(re, im, re, im)
    return rows + masks


def drive_body(wh, b, vec, pows, u_out, end_out, bits):
    count, width = end_out.shape
    half = width // 2
    total = wh.shape[0]
    length = total // count
    rows = power_rows(vec[0:1, :], length, bits, time_place())
    for k, r in enumerate(rows):
        pows[k : k + 1, :] = r
    lr, li = lam_rows(vec, count)
    xr = jnp.zeros((count, half), F32)
    xi = xr
    step = 256
    shifted = vec[2:3, :]
    for i in range(0, total, step):
        u_out[i : i + step, :] = dot(wh[i : i + step, :], b[...]) + shifted
        for t in range(i, i + step, count):
            r = slice(t, t + count)
            xr, xi = complex_step(lr, li, xr, xi, u_out[r, :half], u_out[r, half:])
    end_out[:, :half] = xr
    end_out[:, half:] = xi


def drive_gathered_kernel(bits, own, other, wh, b, vec, pows, u_out, end_out):
    acc = jnp.zeros((8, vec.shape[1]), F32)
    for ref in (own, other):
        for q in range(own.shape[0]):
            acc = acc + ref[q, 16:24, :].astype(F32)
    rows = vector_rows(acc)
    for k, r in enumerate(rows):
        vec[k : k + 1, :] = r
    assemble((b,), own, other, 0)
    b[...] = (b[...].astype(F32) * rows[1]).astype(BF)
    drive_body(wh, b, vec, pows, u_out, end_out, bits)


def drive_plain_kernel(bits, b, vec, wh, pows, u_out, end_out):
    drive_body(wh, b, vec, pows, u_out, end_out, bits)


def fold_rows(a, count):
    return jnp.sum(a.reshape(a.shape[0] // count, count, a.shape[1]), axis=0)


def middle_body(
    u, cotl, carry, vec, c, g, wh,
    st, dst, dm_out, y_out, end, sums,
    dm, y, act, dpre, mix, pre, slope, dact, total_grads, sems, put,
):
    count, width = carry.shape
    half = width // 2
    total = u.shape[0]
    rows = 256
    part = 32
    steps = rows // count
    blocks = total // rows
    copies = Copies(sems)
    lr, li = lam_rows(vec, count)
    state = [carry[:, :half], carry[:, half:]]
    zero = jnp.zeros((count, half), F32)
    wide_zero = jnp.zeros((count, width), F32)
    ends_sum = [zero, zero]
    power = [jnp.ones((count, half), F32), zero]
    totals = [wide_zero] * 4
    jump = (lr, -li)
    for _ in range(steps.bit_length() - 1):
        jump = complex_mul(*jump, *jump)

    def block(i):
        return slice(i * rows, (i + 1) * rows)

    def scan(i):
        now = tuple(state)
        for t in range(0, steps, 2):
            r = i * rows + t * count
            mid = r + count
            one = complex_step(lr, li, *now, u[r:mid, :half], u[r:mid, half:])
            last = mid + count
            now = complex_step(lr, li, *one, u[mid:last, :half], u[mid:last, half:])
            st[r:last, :half] = jnp.concatenate([one[0], now[0]], axis=0).astype(BF)
            st[r:last, half:] = jnp.concatenate([one[1], now[1]], axis=0).astype(BF)
        state[:] = now

    def activate(i):
        mix[i % 2] = dot(st[block(i), :], c[...])
        for k in range(0, rows, part):
            r = slice(i * rows + k, i * rows + k + part)
            x = mix[i % 2, k : k + part, :] + (wh[r, :].astype(F32) * vec[3:4, :] + vec[4:5, :])
            sq = x * x
            th = jnp.tanh(x * (GELU_K + (GELU_K * 0.044715) * sq))
            q = 0.5 * th + 0.5
            a = x * q
            act[r, :] = a.astype(BF)
            slope[i % 4, k : k + part, :] = q + a * (1.0 - q) * (
                2.0 * GELU_K + (6.0 * GELU_K * 0.044715) * sq
            )

    def gating(i):
        pre[i % 2] = dot(act[block(i), :], g[...])
        for k in range(0, rows, part):
            r = slice(i * rows + k, i * rows + k + part)
            v = pre[i % 2, k : k + part, :width] + vec[5:6, :]
            h = pre[i % 2, k : k + part, width:] + vec[6:7, :]
            th = jnp.tanh(h)
            vt = v * th
            ct = cotl[r, :]
            dv = ct + ct * th
            dg = dv * (v - vt)
            dpre[r, :width] = dv.astype(BF)
            dpre[r, width:] = dg.astype(BF)
            y[r, :] = (v + vt).astype(BF)
            totals[2] = totals[2] + fold_rows(dv, count)
            totals[3] = totals[3] + fold_rows(dg, count)
        copies.send(y, y_out, pl.ds(i * rows, rows))

    def back(i):
        dact[i % 2] = dot(dpre[block(i), :], g[...], 1, 1)
        for k in range(0, rows, part):
            r = slice(i * rows + k, i * rows + k + part)
            d = dact[i % 2, k : k + part, :] * slope[i % 4, k : k + part, :]
            dm[r, :] = d.astype(BF)
            totals[0] = totals[0] + fold_rows(d * wh[r, :].astype(F32), count)
            totals[1] = totals[1] + fold_rows(d, count)
        copies.send(dm, dm_out, pl.ds(i * rows, rows))

    def ends(i):
        dst[block(i), :] = dot(dm[block(i), :], c[...], 1, 1)
        now = (zero, zero)
        for t in range(steps - 1, -1, -1):
            r = slice(i * rows + t * count, i * rows + (t + 1) * count)
            now = complex_step(lr, -li, *now, dst[r, :half], dst[r, half:])
        ends_sum[:] = complex_step(*power, *now, *ends_sum)
        power[:] = complex_mul(*power, *jump)

    spans = ((0, 2), (2, 4), (4, 6), (6, blocks))
    tiles = [(act, dpre, 0), (act, dpre, width), (st, dm, 0)]
    tasks = []

    def product(first, last, k):
        a, b, start = tiles[k]
        r = slice(first * rows, last * rows)
        value = dot(a[r, :], b[r, start : start + width], 0, 0)
        if first:
            value = value + total_grads[k]
        if last == blocks:
            put(k, value)
        else:
            total_grads[k] = value

    stages = (scan, activate, gating, back, ends)
    for turn in range(blocks + len(stages) - 1):
        for depth in range(len(stages) - 1, -1, -1):
            if 0 <= turn - depth < blocks:
                stages[depth](turn - depth)
            if tasks and depth in (4, 2, 0):
                product(*tasks.pop(0))
        for first, last in spans:
            if turn - 3 == last - 1:
                tasks += [(first, last, k) for k in range(3)]
    for task in tasks:
        product(*task)
    end[:, :half] = ends_sum[0]
    end[:, half:] = ends_sum[1]
    for k, a in enumerate(totals):
        sums[k : k + 1, :] = jnp.sum(a, axis=0, keepdims=True)
    copies.finish()


def owner_of(q, core, crossed=False):
    tmc = lax.axis_size("tmc")
    seq = lax.axis_index("seq").astype(jnp.int32)
    differs = (0, 2 - core, 1 + core, 3)[q // tmc] if crossed else q // tmc
    return (jnp.bitwise_xor(seq, differs) * tmc + q % tmc) * 2 + core


def split_rows(grads, keep, give, index, crossed=False):
    core = lax.axis_index("core").astype(jnp.int32)
    for q in range(keep.shape[0]):
        for ref, side in ((keep, core), (give, 1 - core)):
            row = pl.multiple_of(owner_of(q, side, crossed) * 16, 16)
            ref[q, index : index + 16, :] = grads[pl.ds(row, 16), :]


def middle_gathered_kernel(u, cotl, carry, vec, own, other, wh, *refs):
    outs, scratch = refs[:8], refs[8:]
    *scratch, c, g, grads, sems = scratch
    width = c.shape[0]
    assemble((c, g.at[:, :width], g.at[:, width:]), own, other, 0)
    g[...] = (g[...].astype(F32) * 0.5).astype(BF)

    def put(k, value):
        grads[k] = value.astype(BF)
        split_rows(grads.at[k], outs[6], outs[7], 16 * k, True)

    middle_body(u, cotl, carry, vec, c, g, wh, *outs[:6], *scratch, sems, put)


def middle_plain_kernel(*refs):
    ins, outs, scratch = refs[:7], refs[7:14], refs[14:]
    width = outs[6].shape[0]

    def put(k, value):
        outs[6][:, k * width : (k + 1) * width] = value.astype(BF)

    middle_body(*ins, *outs[:6], *scratch, put)


def output_kernel(ends, y, tok, out, y_in, tok_in, sems):
    count, length, width = tok.shape
    part = 16
    pieces = 4
    step = length // pieces
    copies = Copies(sems)
    waits = [
        (
            copies.start(y, y_in, pl.ds(k * step * count, step * count)),
            copies.start(tok, tok_in, (slice(None), pl.ds(k * step, step))),
        )
        for k in range(pieces)
    ]
    for k in range(pieces):
        for copy in waits[k]:
            copy.wait()
        for i in range(k * step, (k + 1) * step, part):
            live = live_rows(ends, i, part, length, width)
            add = swap_order(y_in[i * count : (i + part) * count, :].astype(F32), count)
            x = tok_in[:, i : i + part, :].astype(F32) + live * add
            tok_in[:, i : i + part, :] = x.astype(BF)
        copies.send(tok_in, out, (slice(None), pl.ds(k * step, step)))
    copies.finish()


def adjoint_body(dst_in, u_in, st_in, wh, back, carry, vec, adj_out, adj, sems):
    count, width = back.shape
    half = width // 2
    total = u_in.shape[0]
    step = 256
    blocks = total // step
    copies = Copies(sems)
    lr, li = lam_rows(vec, count)
    ar, ai = back[:, :half], back[:, half:]
    zero = jnp.zeros((count, half), F32)
    lsr, lsi, gam, csr, csi = zero, zero, zero, zero, zero
    mr, mi = zero, zero
    m = jnp.zeros((width, width), F32)
    for block in range(blocks - 1, -1, -1):
        for t in range(block * step + step - 2 * count, block * step - 1, -2 * count):
            pair = slice(t, t + 2 * count)
            states = st_in[pair, :].astype(F32)
            held = []
            for k in (1, 0):
                r = slice(k * count, (k + 1) * count)
                sr, si = states[r, :half], states[r, half:]
                lsr = lsr + (mr * sr + mi * si)
                lsi = lsi + (mi * sr - mr * si)
                at = slice(t + k * count, t + (k + 1) * count)
                ar, ai = complex_step(lr, -li, ar, ai, dst_in[at, :half], dst_in[at, half:])
                mr, mi = ar, ai
                gam = gam + (ar * u_in[at, :half] + ai * u_in[at, half:])
                csr = csr + ar
                csi = csi + ai
                held.append((ar, ai))
            adj[pair, :half] = jnp.concatenate([held[1][0], held[0][0]], axis=0).astype(BF)
            adj[pair, half:] = jnp.concatenate([held[1][1], held[0][1]], axis=0).astype(BF)
        at = slice(block * step, (block + 1) * step)
        m = m + dot(wh[at, :], adj[at, :], 0, 0)
        copies.send(adj, adj_out, pl.ds(block * step, step))
    cr, ci = carry[:, :half], carry[:, half:]
    lsr = lsr + (ar * cr + ai * ci)
    lsi = lsi + (ai * cr - ar * ci)

    def row(a):
        return jnp.sum(a, axis=0, keepdims=True)

    cols = jnp.concatenate([row(csr), row(csi)], axis=1)
    return copies, m, cols, row(lsr), row(lsi), row(gam)


def by_owner(vectors, owners):
    out = jnp.zeros((owners, SIDE), F32)
    start = 0
    for v in vectors:
        size = v.shape[1]
        n = size // owners
        lane = lax.broadcasted_iota(jnp.int32, (owners, size), 1)
        row = lax.broadcasted_iota(jnp.int32, (owners, size), 0)
        mine = (lane >= row * n) & (lane < row * n + n)
        src = lax.broadcasted_iota(jnp.int32, (size, SIDE), 0)
        dest = lax.broadcasted_iota(jnp.int32, (size, SIDE), 1)
        for part in split(v):
            wide = jnp.where(mine, jnp.broadcast_to(part.astype(F32), (owners, size)), 0.0)
            fold = jnp.where(lax.rem(src, n) + start == dest, 1.0, 0.0)
            out = out + dot(wide.astype(BF), fold.astype(BF))
            start += n
    return out


def adjoint_gathered_kernel(
    dst, u, st, wh, back, carry, vec, sums, adj_out, keep, give,
    adj, grads, small, sems,
):
    width = vec.shape[1]
    owners = 2 * keep.shape[0]
    copies, m, cols, lsr, lsi, gam = adjoint_body(
        dst, u, st, wh, back, carry, vec, adj_out, adj, sems
    )
    bias = jnp.concatenate([sums[2:3, :], sums[3:4, :]], axis=1)
    small[:, :SIDE] = by_owner((lsr, lsi, gam), owners)
    small[:, SIDE:] = by_owner((sums[0:1, :], sums[1:2, :], bias), owners)
    grads[...] = m.astype(BF)
    split_rows(grads, keep, give, 0)
    row_id = lax.broadcasted_iota(jnp.int32, (8, width), 0)
    common = jnp.zeros((8, width), F32)
    for k, piece in enumerate(split(cols)):
        common = jnp.where(row_id == k, piece.astype(F32), common)
    core = lax.axis_index("core").astype(jnp.int32)
    rest = jnp.zeros((1, width - 2 * SIDE), F32)
    for q in range(keep.shape[0]):
        for ref, side in ((keep, core), (give, 1 - core)):
            row = jnp.concatenate([small[pl.ds(owner_of(q, side), 1), :], rest], axis=1)
            ref[q, 16:24, :] = jnp.where(row_id == 2, row, common).astype(BF)
    copies.finish()


def adjoint_plain_kernel(
    dst, u, st, wh, back, carry, vec, adj_out, m_out, rows_out, adj, sems
):
    half = vec.shape[1] // 2
    copies, m, cols, lsr, lsi, gam = adjoint_body(
        dst, u, st, wh, back, carry, vec, adj_out, adj, sems
    )
    m_out[...] = m.astype(BF)
    rows_out[0:1, :] = cols
    rows_out[1:2, :half] = lsr
    rows_out[1:2, half:] = lsi
    rows_out[2:3, :half] = gam
    copies.finish()


def inputs_kernel(adj, dm, cot, inv, wh, b, vec, out, adj_in, dm_in, cot_in, inv_in, buf, sems):
    count, length, width = cot.shape
    rows = 256
    part = 16
    steps = rows // count
    blocks = length * count // rows
    copies = Copies(sems)
    waits = []

    def fetch(i):
        if i < blocks:
            at = pl.ds(i * rows, rows)
            pairs = ((adj, adj_in), (dm, dm_in), (inv, inv_in))
            waits.append([copies.start(src, dest, at) for src, dest in pairs])
            waits[i].append(copies.start(cot, cot_in, (slice(None), pl.ds(i * steps, steps))))

    for i in range(AHEAD):
        fetch(i)
    for i in range(blocks):
        for copy in waits[i]:
            copy.wait()
        fetch(i + AHEAD)
        buf[i % 2] = dot(adj_in[i * rows : (i + 1) * rows, :], b[...], 1, 1)
        for k in range(0, rows, part * count):
            r = slice(i * rows + k, i * rows + k + part * count)
            w = wh[r, :].astype(F32)
            e = buf[i % 2, k : k + part * count, :] + dm_in[r, :].astype(F32) * vec[3:4, :]
            mean = jnp.mean(e, axis=-1, keepdims=True)
            proj = jnp.mean(e * w, axis=-1, keepdims=True)
            wide = jnp.concatenate([inv_in[r, :]] * (width // SIDE), axis=-1)
            d = swap_order((e - mean - w * proj) * wide, count)
            t = slice((i * rows + k) // count, (i * rows + k) // count + part)
            cot_in[:, t, :] = (cot_in[:, t, :].astype(F32) + d).astype(BF)
        copies.send(cot_in, out, (slice(None), pl.ds(i * steps, steps)))
    copies.finish()


def finish_kernel(parts, vec, proj, gain, shift, skip, decay, phase, *refs):
    far, near, sems = refs[:10], refs[10:20], refs[20]
    (
        gate_out, proj_out, in_out, gain_out, shift_out, skip_out, decay_out, phase_out, gamma_out, bias_out,
    ) = near
    n, width = proj.shape
    q = decay.shape[1]
    copies = []

    def ready(*ks):
        for k in ks:
            copies.append(pltpu.make_async_copy(near[k], far[k], sems.at[k]))
            copies[-1].start()

    late = jnp.sum(parts[:, 3 * n :, :].astype(F32), axis=0)
    scale = vec[1:2, :]
    diag = lax.broadcasted_iota(jnp.int32, (n, n), 0) == lax.broadcasted_iota(jnp.int32, (n, n), 1)

    def column(row):
        return jnp.sum(jnp.where(diag, jnp.broadcast_to(row, (n, n)), 0.0), axis=1, keepdims=True)

    def row(col):
        return jnp.sum(jnp.where(diag, jnp.broadcast_to(col, (n, n)), 0.0), axis=0, keepdims=True)

    def take(start, size):
        return small[:, start : start + size] + small[:, start + size : start + 2 * size]

    m = late[:n]
    cols = (late[n : n + 1] + late[n + 1 : n + 2]) * scale
    small = late[n + 2 : n + 3]
    m_scaled = m * scale
    weight = proj[...].astype(F32)
    gains, shifts, skips = (a[...].astype(F32) for a in (gain, shift, skip))
    in_out[...] = column(gains) * m_scaled + column(shifts) * cols
    ready(2)
    s1, s2 = take(SIDE, n), take(SIDE + 2 * n, n)
    gain_out[...] = row(jnp.sum(m_scaled * weight, axis=1, keepdims=True)) + skips * s1
    shift_out[...] = row(jnp.sum(cols * weight, axis=1, keepdims=True)) + skips * s2
    skip_out[...] = gains * s1 + shifts * s2
    bias_out[...] = 0.5 * take(SIDE + 4 * n, 2 * n)
    re, im = take(0, q), take(2 * q, q)
    gamma_out[...] = take(4 * q, q)
    rate = jnp.exp(decay[...].astype(F32))
    turn = jnp.exp(phase[...].astype(F32))
    modulus = jnp.exp(-rate)
    lam_re, lam_im = modulus * jnp.cos(turn), modulus * jnp.sin(turn)
    decay_out[...] = -rate * (re * lam_re + im * lam_im)
    phase_out[...] = turn * (im * lam_re - re * lam_im)
    ready(3, 4, 5, 6, 7, 8, 9)
    early = jnp.sum(parts[:, : 3 * n, :].astype(F32), axis=0)
    gate_out[:, :width] = 0.5 * early[:n]
    gate_out[:, width:] = 0.5 * early[n : 2 * n]
    proj_out[...] = early[2 * n :]
    ready(0, 1)
    for copy in copies:
        copy.wait()


def swap(a, axis, size, bit):
    return lax.ppermute(a, axis, [(k, k ^ bit) for k in range(size)])


def spread(a, axis, size):
    return jnp.stack([a] + [swap(a, axis, size, k) for k in range(1, size)])


def cross_pairs(owners, tmc, turn):
    return [(k, k ^ (2 * tmc << (k % 2 ^ turn))) for k in range(owners)]


def tie(first, *rest):
    return lax.optimization_barrier((first, *rest))


def cmul_rows(row, a):
    half = a.shape[1] // 2
    re, im = complex_mul(row[:half], row[half:], a[:, :half], a[:, half:])
    return jnp.concatenate([re, im], axis=1)


def carry_in(end, pows, bits, sizes, backward, during):
    total, pre = end, jnp.zeros_like(end)
    for bit in range(bits):
        total = during(bit, total)
        if bit == 0:
            got = swap(total, "core", 2, 1)
        else:
            got = swap(total, "tmc", sizes["tmc"], 1 << (bit - 1))
        taken = pows[4 * bits + bit][None]
        later = taken < 0.5 if backward else taken > 0.5
        wide = pows[4 * bit + (3 if backward else 0)]
        pre = pre + cmul_rows(pows[4 * bit + (2 if backward else 1)], got)
        total = jnp.where(later, total, got) + cmul_rows(wide, jnp.where(later, got, total))
    return pre


def add_low(*parts):
    return sum(a.astype(F32) for a in parts).astype(BF)


def make_body(sizes):
    chips = sizes["seq"] * sizes["tmc"]
    owners = chips * 2
    bits = (2 * sizes["tmc"]).bit_length() - 1

    def body(
        tokens, lengths, cotangent, norm_gain, norm_shift, input_proj, decay_log, phase_log,
        gamma_log, output_proj, skip_gain, gate_weight, gate_bias,
    ):
        micro, per, length, width = tokens.shape
        count = micro * per
        total = count * length
        half = width // 2
        n = width // owners
        fast = n % 16 == 0 and sizes["seq"] == 4
        tok = tokens.reshape(count, length, width)
        cot = cotangent.reshape(count, length, width)
        wide_bf, wide_f = ((total, width), BF), ((total, width), F32)

        vectors = (norm_gain, norm_shift, skip_gain, decay_log, phase_log, gamma_log, gate_bias)
        lead = n + 8
        ins = [v.reshape(1, -1) for v in vectors] + [input_proj, output_proj, gate_weight]
        pack, flag = call(
            pack_kernel, "pack", [((4 * n + 8, width), BF), ((1, width), F32)], ins, [(a.shape, BF) for a in ins],
            far_in=range(10) if fast else (), copies=10,
        )

        def whiten(t):
            thin = ((total, SIDE), F32)
            return call(
                whiten_kernel, "whiten", [wide_bf, thin], (t,), [thin], far_out=(1,), copies=length // 64
            )

        def mask(ct):
            return call(mask_kernel, "mask", [wide_f], (lengths.T, ct))[0]

        powers = ((-(-5 * bits // 8) * 8, width), F32)
        if fast:
            along = spread(pack, "tmc", sizes["tmc"])
            wh, inv = whiten(tok)
            along, wh = tie(along, wh)
            own_first = spread(along[:, :lead], "seq", sizes["seq"]).reshape(chips, lead, width)
            rest = along[:, lead:]
            rest = [rest] + [swap(rest, "seq", sizes["seq"], k) for k in (1, 2)]
            own_first, *rest = tie(own_first, *rest)
            other_first = swap(own_first, "core", 2, 1)
            forward = jnp.where(flag > 0.5, rest[2], rest[1])
            rest.append(lax.ppermute(forward, AXES, cross_pairs(owners, sizes["tmc"], 1)))
            b, vec, pows, u, end = call(
                lambda *r: drive_gathered_kernel(bits, *r), "drive",
                [((width, width), BF), ((8, width), F32), powers, wide_f, ((count, width), F32)],
                (own_first, other_first, wh),
            )
        else:
            wh, inv = whiten(tok)
            cotl = mask(cot)
            every = lax.all_gather(pack, AXES)
            vec = jnp.sum(every[:, n:lead].astype(F32), axis=0)
            vec = jnp.concatenate(vector_rows(vec), axis=0)
            mats = [every[:, :n]] + [every[:, lead + k * n : lead + (k + 1) * n] for k in range(3)]
            mats = [a.reshape(width, width) for a in mats]
            b = (mats[0].astype(F32) * vec[1:2]).astype(BF)
            c = mats[1]
            g = (jnp.concatenate(mats[2:], axis=1).astype(F32) * 0.5).astype(BF)
            pows, u, end = call(
                lambda *r: drive_plain_kernel(bits, *r), "drive",
                [powers, wide_f, ((count, width), F32)], (b, vec, wh),
            )

        held = {}

        def early_rest(bit, a):
            if fast and bit == 1:
                a, rest[3], late_cot = tie(a, rest[3], cot)
                held["cotl"] = mask(late_cot)
            if fast and bit == 2:
                a, held["cotl"] = tie(a, held["cotl"])
                parts = tie(a, *rest)[1:]
                held["own"] = jnp.stack(parts).reshape(chips, -1, width)
                held["other"] = swap(held["own"], "core", 2, 1)
            return a

        carry = carry_in(end, pows, bits, sizes, False, early_rest)
        if fast:
            cotl = held["cotl"]
        rows = 256
        blocks = total // rows
        side = ((count, length, width), BF)
        outs = [wide_bf, wide_f, wide_bf, wide_bf, ((count, width), F32), ((4, width), F32)]
        scratch = [wide_bf] * 3 + [
            ((total, 2 * width), BF), ((2, rows, width), F32), ((2, rows, 2 * width), F32),
            ((4, rows, width), F32), ((2, rows, width), F32), ((3, width, width), F32),
        ]
        if fast:
            ins = (u, cotl, carry, vec, held["own"], held["other"], wh)
            st, dst, dm, y, back_end, sums, keep, give = call(
                middle_gathered_kernel, "middle", outs + [((chips, 48, width), BF)] * 2, ins,
                scratch + [((width, width), BF), ((width, 2 * width), BF), ((3, width, width), BF)], limit=32, far_out=(2, 3), copies=2 * blocks,
            )
        else:
            st, dst, dm, y, back_end, sums, out_grads = call(
                middle_plain_kernel, "middle", outs + [((width, 3 * width), BF)],
                (u, cotl, carry, vec, c, g, wh), scratch,
                limit=32, far_out=(2, 3), copies=2 * blocks,
            )


        def seq_parts(both):
            both = both.reshape(sizes["seq"], sizes["tmc"], -1, width)
            return [both[0]] + [swap(both[k], "seq", sizes["seq"], k) for k in range(1, sizes["seq"])]

        def early_sums(bit, a):
            if fast and bit == 2:
                got = swap(give, "core", 2, 1)
                low, high = slice(0, chips // 2), slice(chips // 2, chips)
                high = add_low(keep[high], got[high])
                low = add_low(keep[low], got[low])
                a, high, low = tie(a, high, low)
                got = lax.ppermute(high, AXES, cross_pairs(owners, sizes["tmc"], 0))
                held["early"] = (low, got)
            return a

        back = carry_in(back_end, pows, bits, sizes, True, early_sums)

        ins = (dst, u, st, wh, back, carry, vec)
        if fast:
            adj, late_keep, late_give = call(
                adjoint_gathered_kernel, "adjoint",
                [wide_bf] + [((chips, 24, width), BF)] * 2, (*ins, sums),
                [wide_bf] + [((width, width), BF), ((owners, 2 * SIDE), F32)],
                limit=10, far_out=(0,), copies=blocks,
            )
            quarter = chips // 4
            low, high = (
                add_low(*(a[k : k + quarter] for a in held["early"])) for k in (0, quarter)
            )
            low, high, late_keep, late_give = tie(low, high, late_keep, late_give)
            early = add_low(low, lax.ppermute(high, AXES, cross_pairs(owners, sizes["tmc"], 1)))
            late = add_low(late_keep, swap(late_give, "core", 2, 1))
            late, y = tie(late, y)
            both = jnp.concatenate([early, add_low(*seq_parts(late))], axis=1)
            block_out = call(
                output_kernel, "output", [side], (lengths.T, y, tok), [wide_bf, side],
                limit=8, far_in=(1, 2), far_out=(0,), copies=12,
            )[0]
            both, adj, block_out = tie(both, adj, block_out)
            both = lax.all_to_all(both, "tmc", 0, 0)
        else:
            adj, m, late_rows = call(
                adjoint_plain_kernel, "adjoint",
                [wide_bf, ((width, width), BF), ((8, width), F32)], ins, [wide_bf],
                limit=10, far_out=(0,), copies=blocks,
            )
            block_out = call(
                output_kernel, "output", [side], (lengths.T, y, tok), [wide_bf, side],
                limit=8, far_in=(1, 2), far_out=(0,), copies=12,
            )[0]
        (tok_grad,) = call(
            inputs_kernel, "inputs", [side], (adj, dm, cot, inv, wh, b, vec),
            [wide_bf, wide_bf, side, ((total, SIDE), F32), ((2, rows, width), F32)],
            limit=14, far_in=range(4), far_out=(0,), copies=5 * blocks,
        )

        q = half // owners
        if fast:
            shapes = [(n, 2 * width), (n, width), (n, width)] + [(1, n)] * 3 + [(1, q)] * 3 + [(1, 2 * n)]
            shapes = [(a, F32) for a in shapes]
            rows = [v.reshape(1, -1) for v in (norm_gain, norm_shift, skip_gain, decay_log, phase_log)]
            grads = call(
                finish_kernel, "finish", shapes, (both, vec, input_proj, *rows), shapes,
                far_out=range(10), copies=10,
            )
            gate_sum, proj_sum, in_grad = grads[:3]
            gain_grad, shift_grad, skip_grad, decay_grad, phase_grad, gamma_grad, bias_sum = (
                a.reshape(-1) for a in grads[3:]
            )
        else:
            def scatter(a):
                return lax.psum_scatter(a.astype(F32), AXES, scatter_dimension=0, tiled=True)

            gate_sum = scatter(out_grads[:, : 2 * width]) * 0.5
            proj_sum = scatter(out_grads[:, 2 * width :])
            m_sum = scatter(m)
            cols = lax.psum(late_rows[0], AXES)
            lam_re_sum = scatter(late_rows[1, :half])
            lam_im_sum = scatter(late_rows[1, half:])
            gamma_grad = scatter(late_rows[2, :half])
            s1, s2 = scatter(sums[0]), scatter(sums[1])
            bias_sum = scatter(sums[2:].reshape(2 * width)) * 0.5
            gain = norm_gain.astype(F32)
            shift = norm_shift.astype(F32)
            skip = skip_gain.astype(F32)
            proj = input_proj.astype(F32)
            scale = vec[1]
            in_grad = (gain[:, None] * m_sum + shift[:, None] * cols[None]) * scale[None]
            gain_grad = jnp.sum(m_sum * scale[None] * proj, axis=1) + skip * s1
            shift_grad = jnp.sum((cols * scale)[None] * proj, axis=1) + skip * s2
            skip_grad = gain * s1 + shift * s2
            rate = jnp.exp(decay_log.astype(F32))
            phase = jnp.exp(phase_log.astype(F32))
            modulus = jnp.exp(-rate)
            lam_re = modulus * jnp.cos(phase)
            lam_im = modulus * jnp.sin(phase)
            decay_grad = -rate * (lam_re_sum * lam_re + lam_im_sum * lam_im)
            phase_grad = phase * (lam_im_sum * lam_re - lam_re_sum * lam_im)
        return (
            block_out.reshape(tokens.shape), tok_grad.reshape(tokens.shape), gain_grad, shift_grad,
            in_grad, decay_grad, phase_grad, gamma_grad, proj_sum, skip_grad, gate_sum, bias_sum,
        )

    return body


def solution(mesh):
    seq, tm = mesh.shape["seq"], mesh.shape["tm"]
    fine = Mesh(mesh.devices.reshape(seq, tm // 2, 2), AXES)
    sizes = dict(zip(AXES, (seq, tm // 2, 2)))
    side = P(None, "seq", ("tmc", "core"), None)
    vec = P(AXES)
    mat = P(AXES, None)
    return jax.shard_map(
        make_body(sizes),
        mesh=fine,
        in_specs=(side, P(None, "seq"), side, vec, vec, mat, vec, vec, vec, mat, vec, mat, vec),
        out_specs=(side, side, vec, vec, mat, vec, vec, vec, mat, vec, mat, vec),
        check_vma=False,
    )
```

time: 1350 us -> 93.6 us (0.07); the launches traced: 1330 us -> 93.3 us
  blocking collectives: 401 us -> 0 us
  local copies, waits for them, and re-layouts: 333 us -> 1.71 us
  waiting for transfers between devices: 334 us -> 25 us
  other arithmetic: 196 us -> 1.7 us
  matrix products: 47 us -> 0 us
  Pallas kernels: 0 us -> 36 us
  starting transfers between devices: 0.16 us -> 27.8 us
  between operations: 18.5 us -> 1.17 us
    reduce_scatter x3 -> x0, waiting for transfers between devices: 333 us -> none  [the longest x1 136 us: body(): lax.psum_scatter(local_grads[8], ('seq', 'tm'), scatter_dimension=0, tile...]
    all_gather x21 -> x0, blocking collectives: 320 us -> none  [the longest x19 239 us: prefix(): gathered = jax.tree.map(lambda a: lax.all_gather(a, axis), part)]
    dynamic_slice x156 -> x0, local copies, waits for them, and re-layouts: 139 us -> none  [the longest x128 138 us: stretch_scan(): lax.scan(across, (start, start), (local_re, local_im))]
    dynamic_update_slice x128 -> x0, other arithmetic: 92.9 us -> none  [stretch_scan(): lax.scan(across, (start, start), (local_re, local_im))]
    unnamed x2 -> x0, blocking collectives: 80.4 us -> none
    rev x18 -> x0, local copies, waits for them, and re-layouts: 66.3 us -> none  [the longest x4 17.7 us: stretch_scan(): drive_im = drive_im[:, ::-1]]
    dot_general x36 -> x0, matrix products: 47 us -> none  [the longest x4 8.75 us: micro_step(): jnp.einsum('sck,hk->sch', d_pre, gate_weight, preferred_element_type=jnp....]
    slice x293 -> x4, local copies, waits for them, and re-layouts: 42.3 us -> 0.06 us  [the longest x2 0.02 us: cmul_rows(): re, im = complex_mul(row[:half], row[half:], a[:, :half], a[:, half:])]
  transfers between devices with their start and end apart: 4 -> 25, of which waited for: 3 -> 19; matrix products, arithmetic and copies ran while one was open for 13% -> 0% of each run, Pallas kernels for 0% -> 22%
where the time goes in v2:
time: 93.6 us; the launch traced here: 93.3 us
  Pallas kernels  36 us (38%)
  starting transfers between devices  27.8 us (30%)
  waiting for transfers between devices  25 us (27%)
  local copies, waits for them, and re-layouts  1.71 us (2%)
  other arithmetic  1.7 us (2%)
  between operations  1.17 us (1%)
    pallas_call x9, Pallas kernels, call(): pl.pallas_call(body, out_shape=[pltpu.HBM(s, t) if k in far_out else jax....  36 us
    ppermute x21, waiting for transfers between devices, swap(): return lax.ppermute(a, axis, [(k, k ^ bit) for k in range(size)])  20.6 us
    ppermute x21, starting transfers between devices, swap(): return lax.ppermute(a, axis, [(k, k ^ bit) for k in range(size)])  20.3 us
    all_to_all x1, starting transfers between devices, body(): both = lax.all_to_all(both, 'tmc', 0, 0)  3.45 us
  transfers between devices with their start and end apart: 25, of which 19 were waited for; matrix products, arithmetic and copies ran while one was open for 0% of the time, Pallas kernels for 22%

profile of v2, /device:TPU:0, one launch (start us, length us, event | category | flops | bytes accessed | tf_op | source)
XLA Modules:
  0.0 93.3 jit_solution(8520504349652398628)
XLA Ops:
  0.6 1.2 %pack.1 = (bf16[72,512]{1,0:T(8,128)(2,1)S(1)}, f32[1,512]{1,0:T(1,128)S(1)}) custom-call(bf16[1,16]{1,0:T(2,128)(2,1)} %bitcast.65, bf16[1,16]{1,0:T(2,128)(2,1)} %bitcast.67, bf16[1,16]{1,0:T(2,128)(2,1)} %bitcast.69, bf16[1,8]{1,0:T(2,128)(2,1)} %bitcast.71, bf16[1,8]{1,0:T(2,128)(2,1)} %bitcast.73, bf16[1,8]{1,0:T(2,128)(2,1)} %bitcast.107, ...), custom_call_target="tpu_custom_call" | custom-call | tf_op jit(solution)/shard_map/pack/pallas_call | solution.py:30
  1.8 5.1 %collective-permute-start.2 = (bf16[72,512]{1,0:T(8,128)(2,1)S(1)}, bf16[72,512]{1,0:T(8,128)(2,1)S(1)}, u32[]{:S(2)}, u32[]{:S(2)}) collective-permute-start(bf16[72,512]{1,0:T(8,128)(2,1)S(1)} %get-tuple-element.69), channel_id=1, source_target_pairs={{0,6},{2,4},{4,2},{6,0},{1,7},{3,5},{5,3},{7,1},{8,14},{10,12},{12... | collective-permute-start | bytes 221192 | tf_op jit(solution)/shard_map/ppermute | solution.py:657
  6.9 0.6 collective-permute-start
  7.6 1.6 %copy-done = bf16[4,2,256,512]{3,2,1,0:T(8,128)(2,1)S(1)} copy-done((bf16[4,2,256,512]{3,2,1,0:T(8,128)(2,1)S(1)}, bf16[4,2,256,512]{3,2,1,0:T(8,128)(2,1)}, u32[]{:S(2)}) %copy-start) | copy-done | bytes 2097176
  9.2 3.3 %whiten.1 = (bf16[2048,512]{1,0:T(8,128)(2,1)S(1)}, f32[2048,128]{1,0:T(8,128)}) custom-call(bf16[8,256,512]{2,1,0:T(8,128)(2,1)S(1)} %bitcast.55), custom_call_target="tpu_custom_call" | custom-call | tf_op jit(solution)/shard_map/whiten/pallas_call | solution.py:30
  12.5 0.7 collective-permute-done.1
  13.2 1.6 %collective-permute-start.4 = (bf16[4,24,512]{2,1,0:T(8,128)(2,1)S(1)}, bf16[4,24,512]{2,1,0:T(8,128)(2,1)S(1)}, u32[]{:S(2)}, u32[]{:S(2)}) collective-permute-start(bf16[4,24,512]{2,1,0:T(8,128)(2,1)S(1)} %get-tuple-element.138), channel_id=1, source_target_pairs={{0,16},{8,24},{16,0},{24,8},{1,17},{9,25},{17,1},{25,9},{2,18},{10... | collective-permute-start | bytes 294920 | tf_op jit(solution)/shard_map/ppermute | solution.py:657
  14.8 1.5 %collective-permute-start.3 = (bf16[4,24,512]{2,1,0:T(8,128)(2,1)S(1)}, bf16[4,24,512]{2,1,0:T(8,128)(2,1)S(1)}, u32[]{:S(2)}, u32[]{:S(2)}) collective-permute-start(bf16[4,24,512]{2,1,0:T(8,128)(2,1)S(1)} %get-tuple-element.138), channel_id=1, source_target_pairs={{0,8},{8,0},{16,24},{24,16},{1,9},{9,1},{17,25},{25,17},{2,10},{10... | collective-permute-start | bytes 294920 | tf_op jit(solution)/shard_map/ppermute | solution.py:657
  16.3 0.5 collective-permute-start.5
  16.8 1.6 %collective-permute-start.7 = (bf16[4,48,512]{2,1,0:T(8,128)(2,1)S(1)}, bf16[4,48,512]{2,1,0:T(8,128)(2,1)S(1)}, u32[]{:S(2)}, u32[]{:S(2)}) collective-permute-start(bf16[4,48,512]{2,1,0:T(8,128)(2,1)S(1)} %slice.225), channel_id=1, source_target_pairs={{0,16},{8,24},{16,0},{24,8},{1,17},{9,25},{17,1},{25,9},{2,18},{10... | collective-permute-start | bytes 589832 | tf_op jit(solution)/shard_map/ppermute | solution.py:657
  18.4 1.5 %collective-permute-start.6 = (bf16[4,48,512]{2,1,0:T(8,128)(2,1)S(1)}, bf16[4,48,512]{2,1,0:T(8,128)(2,1)S(1)}, u32[]{:S(2)}, u32[]{:S(2)}) collective-permute-start(bf16[4,48,512]{2,1,0:T(8,128)(2,1)S(1)} %slice.225), channel_id=1, source_target_pairs={{0,8},{8,0},{16,24},{24,16},{1,9},{9,1},{17,25},{25,17},{2,10},{10... | collective-permute-start | bytes 589832 | tf_op jit(solution)/shard_map/ppermute | solution.py:657
  19.9 0.5 collective-permute-done.3
  20.4 2.5 %collective-permute-done.5 = bf16[4,24,512]{2,1,0:T(8,128)(2,1)S(1)} collective-permute-done((bf16[4,24,512]{2,1,0:T(8,128)(2,1)S(1)}, bf16[4,24,512]{2,1,0:T(8,128)(2,1)S(1)}, u32[]{:S(2)}, u32[]{:S(2)}) %collective-permute-start.5) | collective-permute-done | bytes 98336 | tf_op jit(solution)/shard_map/ppermute | solution.py:657
  23.0 1.4 %collective-permute-done.7 = bf16[4,48,512]{2,1,0:T(8,128)(2,1)S(1)} collective-permute-done((bf16[4,48,512]{2,1,0:T(8,128)(2,1)S(1)}, bf16[4,48,512]{2,1,0:T(8,128)(2,1)S(1)}, u32[]{:S(2)}, u32[]{:S(2)}) %collective-permute-start.7) | collective-permute-done | bytes 196640 | tf_op jit(solution)/shard_map/ppermute | solution.py:657
  24.4 0.9 collective-permute-done.6
  25.4 1.0 %collective-permute-start.10 = (bf16[4,48,512]{2,1,0:T(8,128)(2,1)S(1)}, bf16[4,48,512]{2,1,0:T(8,128)(2,1)S(1)}, u32[]{:S(2)}, u32[]{:S(2)}) collective-permute-start(bf16[4,48,512]{2,1,0:T(8,128)(2,1)S(1)} %broadcast_select_fusion), channel_id=1, source_target_pairs={{0,16},{1,9},{2,18},{3,11},{4,20},{5,13},{6,22},{7,15},{8,24},{9,1... | collective-permute-start | bytes 589832 | tf_op jit(solution)/shard_map/ppermute | solution.py:745
  26.4 0.7 collective-permute-done.8.r_1_
  27.0 1.5 %drive.1 = (bf16[512,512]{1,0:T(8,128)(2,1)S(1)}, f32[8,512]{1,0:T(8,128)S(1)}, f32[16,512]{1,0:T(8,128)S(1)}, f32[2048,512]{1,0:T(8,128)S(1)}, f32[8,512]{1,0:T(8,128)S(1)}) custom-call(bf16[16,24,512]{2,1,0:T(8,128)(2,1)S(1)} %bitcast.61, bf16[16,24,512]{2,1,0:T(8,128)(2,1)S(1)} %collective-permute-done.8.r_1_, bf16[2048,512]{1,0:T(8,128)(2,1)S(1)} %get-tuple-element.73.r_2_.wh), custom_call_target="tpu_custom_call" | custom-call | tf_op jit(solution)/shard_map/drive/pallas_call | solution.py:30
  28.8 1.0 %collective-permute-done.9 = f32[8,512]{1,0:T(8,128)S(1)} collective-permute-done((f32[8,512]{1,0:T(8,128)S(1)}, f32[8,512]{1,0:T(8,128)S(1)}, u32[]{:S(2)}, u32[]{:S(2)}) %collective-permute-start.9) | collective-permute-done | bytes 16416 | tf_op jit(solution)/shard_map/ppermute | solution.py:657
  29.8 1.3 %collective-permute-done.10 = bf16[4,48,512]{2,1,0:T(8,128)(2,1)S(1)} collective-permute-done((bf16[4,48,512]{2,1,0:T(8,128)(2,1)S(1)}, bf16[4,48,512]{2,1,0:T(8,128)(2,1)S(1)}, u32[]{:S(2)}, u32[]{:S(2)}) %collective-permute-start.10) | collective-permute-done | bytes 196640 | tf_op jit(solution)/shard_map/ppermute | solution.py:745
  31.1 0.4 collective-permute-start.11
  31.5 1.3 %mask.1.cotl = f32[2048,512]{1,0:T(8,128)S(1)} custom-call(s32[2,4]{1,0:T(2,128)S(1)} %bitcast.63, bf16[8,256,512]{2,1,0:T(8,128)(2,1)S(1)} %bitcast.57), custom_call_target="tpu_custom_call" | custom-call | tf_op jit(solution)/shard_map/mask/pallas_call | solution.py:30
  32.9 2.0 %collective-permute-done.11 = f32[8,512]{1,0:T(8,128)S(1)} collective-permute-done((f32[8,512]{1,0:T(8,128)S(1)}, f32[8,512]{1,0:T(8,128)S(1)}, u32[]{:S(2)}, u32[]{:S(2)}) %collective-permute-start.11) | collective-permute-done | bytes 16416 | tf_op jit(solution)/shard_map/ppermute | solution.py:657
  35.1 1.3 %collective-permute-start.12 = (f32[8,512]{1,0:T(8,128)S(1)}, f32[8,512]{1,0:T(8,128)S(1)}, u32[]{:S(2)}, u32[]{:S(2)}) collective-permute-start(f32[8,512]{1,0:T(8,128)S(1)} %maximum_add_fusion.1), channel_id=1, source_target_pairs={{0,4},{2,6},{4,0},{6,2},{1,5},{3,7},{5,1},{7,3},{8,12},{10,14},{12... | collective-permute-start | bytes 49160 | tf_op jit(solution)/shard_map/ppermute | solution.py:657
  36.4 3.4 %collective-permute-done.12 = f32[8,512]{1,0:T(8,128)S(1)} collective-permute-done((f32[8,512]{1,0:T(8,128)S(1)}, f32[8,512]{1,0:T(8,128)S(1)}, u32[]{:S(2)}, u32[]{:S(2)}) %collective-permute-start.12) | collective-permute-done | bytes 16416 | tf_op jit(solution)/shard_map/ppermute | solution.py:657
  39.8 13.3 %middle.1 = (bf16[2048,512]{1,0:T(8,128)(2,1)S(1)}, f32[2048,512]{1,0:T(8,128)S(1)}, bf16[2048,512]{1,0:T(8,128)(2,1)}, bf16[2048,512]{1,0:T(8,128)(2,1)}, f32[8...) custom-call(f32[2048,512]{1,0:T(8,128)S(1)} %get-tuple-element.75.u,, ...), custom_call_target="tpu_custom_call" | custom-call | tf_op jit(solution)/shard_map/middle/pallas_call | solution.py:30
  53.2 0.5 collective-permute-start.16
  53.7 0.7 collective-permute-done.14
  54.4 0.5 collective-permute-start.15
  54.9 3.3 %collective-permute-done.15 = f32[8,512]{1,0:T(8,128)S(1)} collective-permute-done((f32[8,512]{1,0:T(8,128)S(1)}, f32[8,512]{1,0:T(8,128)S(1)}, u32[]{:S(2)}, u32[]{:S(2)}) %collective-permute-start.15) | collective-permute-done | bytes 16416 | tf_op jit(solution)/shard_map/ppermute | solution.py:657
  58.5 1.3 %collective-permute-start.18 = (f32[8,512]{1,0:T(8,128)S(1)}, f32[8,512]{1,0:T(8,128)S(1)}, u32[]{:S(2)}, u32[]{:S(2)}) collective-permute-start(f32[8,512]{1,0:T(8,128)S(1)} %maximum_add_fusion.4), channel_id=1, source_target_pairs={{0,4},{2,6},{4,0},{6,2},{1,5},{3,7},{5,1},{7,3},{8,12},{10,14},{12... | collective-permute-start | bytes 49160 | tf_op jit(solution)/shard_map/ppermute | solution.py:657
  59.8 1.5 %collective-permute-start.17 = (bf16[8,48,512]{2,1,0:T(8,128)(2,1)S(1)}, bf16[8,48,512]{2,1,0:T(8,128)(2,1)S(1)}, u32[]{:S(2)}, u32[]{:S(2)}) collective-permute-start(bf16[8,48,512]{2,1,0:T(8,128)(2,1)S(1)} %get-tuple-element.95), channel_id=1, source_target_pairs={{0,8},{1,17},{2,10},{3,19},{4,12},{5,21},{6,14},{7,23},{8,0},{9,25... | collective-permute-start | bytes 1179656 | tf_op jit(solution)/shard_map/ppermute | solution.py:816
  61.3 1.9 %collective-permute-done.18 = f32[8,512]{1,0:T(8,128)S(1)} collective-permute-done((f32[8,512]{1,0:T(8,128)S(1)}, f32[8,512]{1,0:T(8,128)S(1)}, u32[]{:S(2)}, u32[]{:S(2)}) %collective-permute-start.18) | collective-permute-done | bytes 16416 | tf_op jit(solution)/shard_map/ppermute | solution.py:657
  63.2 3.4 %adjoint.1 = (bf16[2048,512]{1,0:T(8,128)(2,1)}, bf16[16,24,512]{2,1,0:T(8,128)(2,1)S(1)}, bf16[16,24,512]{2,1,0:T(8,128)(2,1)S(1)}) custom-call(f32[2048,512]{1,0:T(8,128)S(1)} %get-tuple-element.96.dst, f32[2048,512]{1,0:T(8,128)S(1)} %get-tuple-element.75.u, bf16[2048,512]{1,0:T(8,128)(2,1)S(1)} %get-tuple-element.97.st, ...), custom_call_target="tpu_custom_call" | custom-call | tf_op jit(solution)/shard_map/adjoint/pallas_call | solution.py:30
  66.6 0.9 %collective-permute-done.17 = bf16[8,48,512]{2,1,0:T(8,128)(2,1)S(1)} collective-permute-done((bf16[8,48,512]{2,1,0:T(8,128)(2,1)S(1)}, bf16[8,48,512]{2,1,0:T(8,128)(2,1)S(1)}, u32[]{:S(2)}, u32[]{:S(2)}) %collective-permute-start.17) | collective-permute-done | bytes 393248 | tf_op jit(solution)/shard_map/ppermute | solution.py:816
  67.8 1.5 %collective-permute-start.19 = (bf16[4,48,512]{2,1,0:T(8,128)(2,1)S(1)}, bf16[4,48,512]{2,1,0:T(8,128)(2,1)S(1)}, u32[]{:S(2)}, u32[]{:S(2)}) collective-permute-start(bf16[4,48,512]{2,1,0:T(8,128)(2,1)S(1)} %get-tuple-element.103), channel_id=1, source_target_pairs={{0,16},{1,9},{2,18},{3,11},{4,20},{5,13},{6,22},{7,15},{8,24},{9,1... | collective-permute-start | bytes 589832 | tf_op jit(solution)/shard_map/ppermute | solution.py:835
  69.6 1.5 %collective-permute-start.21 = (bf16[4,24,512]{2,1,0:T(8,128)(2,1)S(1)}, bf16[4,24,512]{2,1,0:T(8,128)(2,1)S(1)}, u32[]{:S(2)}, u32[]{:S(2)}) collective-permute-start(bf16[4,24,512]{2,1,0:T(8,128)(2,1)S(1)} %get-tuple-element.134), channel_id=1, source_target_pairs={{0,8},{8,0},{16,24},{24,16},{1,9},{9,1},{17,25},{25,17},{2,10},{10... | collective-permute-start | bytes 294920 | tf_op jit(solution)/shard_map/ppermute | solution.py:657
  71.1 1.4 %collective-permute-start.23 = (bf16[4,24,512]{2,1,0:T(8,128)(2,1)S(1)}, bf16[4,24,512]{2,1,0:T(8,128)(2,1)S(1)}, u32[]{:S(2)}, u32[]{:S(2)}) collective-permute-start(bf16[4,24,512]{2,1,0:T(8,128)(2,1)S(1)} %get-tuple-element.135), channel_id=1, source_target_pairs={{0,24},{8,16},{16,8},{24,0},{1,25},{9,17},{17,9},{25,1},{2,26},{10... | collective-permute-start | bytes 294920 | tf_op jit(solution)/shard_map/ppermute | solution.py:657
  72.5 0.6 collective-permute-start.22
  73.1 0.3 collective-permute-done.19
  73.5 4.1 %output.1 = bf16[8,256,512]{2,1,0:T(8,128)(2,1)} custom-call(s32[2,4]{1,0:T(2,128)S(1)} %bitcast.64, bf16[2048,512]{1,0:T(8,128)(2,1)} %get-tuple-element.109.y, bf16[8,256,512]{2,1,0:T(8,128)(2,1)} %bitcast.54), custom_call_target="tpu_custom_call" | custom-call | tf_op jit(solution)/shard_map/output/pallas_call | solution.py:30
  77.7 0.4 collective-permute-done.23
  78.1 0.9 collective-permute-done.22
  79.1 0.7 pad_maximum_fusion.3
  79.8 3.5 %all-to-all-start = ((bf16[4,72,512]{2,1,0:T(8,128)(2,1)}), bf16[4,72,512]{2,1,0:T(8,128)(2,1)S(1)}, u32[]{:S(2)}, u32[]{:S(2)}) async-start(bf16[4,72,512]{2,1,0:T(8,128)(2,1)} %pad_maximum_fusion.3), calls=%async_computation | async-start | bytes 589824 | tf_op jit(solution)/shard_map/all_to_all | solution.py:844
  83.3 6.9 %inputs.1 = bf16[8,256,512]{2,1,0:T(8,128)(2,1)} custom-call(bf16[2048,512]{1,0:T(8,128)(2,1)} %get-tuple-element.111.adj, bf16[2048,512]{1,0:T(8,128)(2,1)} %get-tuple-element.112.dm, bf16[8,256,512]{2,1,0:T(8,128)(2,1)} %bitcast.56, f32[2048,128]{1,0:T(8,128)} %get-tuple-element.113.inv, bf16[2048,512]{1,0:T(8,128)(2,1)S(1)} %get-tuple-element.73.r_2_.wh, ...), custom_call_target="tpu_custom_call" | custom-call | tf_op jit(solution)/shard_map/inputs/pallas_call | solution.py:30
  90.3 1.8 %all-to-all-done.parts = bf16[4,72,512]{2,1,0:T(8,128)(2,1)S(1)} async-done(((bf16[4,72,512]{2,1,0:T(8,128)(2,1)}), bf16[4,72,512]{2,1,0:T(8,128)(2,1)S(1)}, u32[]{:S(2)}, u32[]{:S(2)}) %all-to-all-start) | async-done | bytes 294944 | tf_op jit(solution)/shard_map/all_to_all | solution.py:844
  92.1 1.0 %finish.1 = (f32[16,1024]{1,0:T(8,128)}, f32[16,512]{1,0:T(8,128)}, f32[16,512]{1,0:T(8,128)}, f32[1,16]{1,0:T(1,128)}, f32[1,16]{1,0:T(1,128)}, /*index=5*/f32[...) custom-call(bf16[4,72,512]{2,1,0:T(8,128)(2,1)S(1)} %all-to-all-done.parts, ...), custom_call_target="tpu_custom_call" | custom-call | tf_op jit(solution)/shard_map/finish/pallas_call | solution.py:30
  (66 shorter events, 1.7 us)
Async XLA Ops:
  1.8 10.7 %collective-permute-start.2 = (bf16[72,512]{1,0:T(8,128)(2,1)S(1)}, bf16[72,512]{1,0:T(8,128)(2,1)S(1)}, u32[]{:S(2)}, u32[]{:S(2)}) collective-permute-start(bf16[72,512]{1,0:T(8,128)(2,1)S(1)} %get-tuple-element.69), channel_id=1, source_target_pairs={{0,6},{2,4},{4,2},{6,0},{1,7},{3,5},{5,3},{7,1},{8,14},{10,12},{12... | collective-permute-start | bytes 221192 | tf_op jit(solution)/shard_map/ppermute | solution.py:657
  6.9 6.2 %collective-permute-start.1 = (bf16[72,512]{1,0:T(8,128)(2,1)S(1)}, bf16[72,512]{1,0:T(8,128)(2,1)S(1)}, u32[]{:S(2)}, u32[]{:S(2)}) collective-permute-start(bf16[72,512]{1,0:T(8,128)(2,1)S(1)} %get-tuple-element.69), channel_id=1, source_target_pairs={{0,4},{2,6},{4,0},{6,2},{1,5},{3,7},{5,1},{7,3},{8,12},{10,14},{12... | collective-permute-start | bytes 221192 | tf_op jit(solution)/shard_map/ppermute | solution.py:657
  6.9 6.2 %collective-permute-start = (bf16[72,512]{1,0:T(8,128)(2,1)S(1)}, bf16[72,512]{1,0:T(8,128)(2,1)S(1)}, u32[]{:S(2)}, u32[]{:S(2)}) collective-permute-start(bf16[72,512]{1,0:T(8,128)(2,1)S(1)} %get-tuple-element.69), channel_id=1, source_target_pairs={{0,2},{2,0},{4,6},{6,4},{1,3},{3,1},{5,7},{7,5},{8,10},{10,8},{12,... | collective-permute-start | bytes 221192 | tf_op jit(solution)/shard_map/ppermute | solution.py:657
  7.6 1.6 %copy-start = (bf16[4,2,256,512]{3,2,1,0:T(8,128)(2,1)S(1)}, bf16[4,2,256,512]{3,2,1,0:T(8,128)(2,1)}, u32[]{:S(2)}) copy-start(bf16[4,2,256,512]{3,2,1,0:T(8,128)(2,1)} %param.13) | copy-start | bytes 6291460
  13.2 6.7 %collective-permute-start.4 = (bf16[4,24,512]{2,1,0:T(8,128)(2,1)S(1)}, bf16[4,24,512]{2,1,0:T(8,128)(2,1)S(1)}, u32[]{:S(2)}, u32[]{:S(2)}) collective-permute-start(bf16[4,24,512]{2,1,0:T(8,128)(2,1)S(1)} %get-tuple-element.138), channel_id=1, source_target_pairs={{0,16},{8,24},{16,0},{24,8},{1,17},{9,25},{17,1},{25,9},{2,18},{10... | collective-permute-start | bytes 294920 | tf_op jit(solution)/shard_map/ppermute | solution.py:657
  14.8 5.6 %collective-permute-start.3 = (bf16[4,24,512]{2,1,0:T(8,128)(2,1)S(1)}, bf16[4,24,512]{2,1,0:T(8,128)(2,1)S(1)}, u32[]{:S(2)}, u32[]{:S(2)}) collective-permute-start(bf16[4,24,512]{2,1,0:T(8,128)(2,1)S(1)} %get-tuple-element.138), channel_id=1, source_target_pairs={{0,8},{8,0},{16,24},{24,16},{1,9},{9,1},{17,25},{25,17},{2,10},{10... | collective-permute-start | bytes 294920 | tf_op jit(solution)/shard_map/ppermute | solution.py:657
  16.3 6.6 %collective-permute-start.5 = (bf16[4,24,512]{2,1,0:T(8,128)(2,1)S(1)}, bf16[4,24,512]{2,1,0:T(8,128)(2,1)S(1)}, u32[]{:S(2)}, u32[]{:S(2)}) collective-permute-start(bf16[4,24,512]{2,1,0:T(8,128)(2,1)S(1)} %get-tuple-element.138), channel_id=1, source_target_pairs={{0,24},{8,16},{16,8},{24,0},{1,25},{9,17},{17,9},{25,1},{2,26},{10... | collective-permute-start | bytes 294920 | tf_op jit(solution)/shard_map/ppermute | solution.py:657
  16.8 7.6 %collective-permute-start.7 = (bf16[4,48,512]{2,1,0:T(8,128)(2,1)S(1)}, bf16[4,48,512]{2,1,0:T(8,128)(2,1)S(1)}, u32[]{:S(2)}, u32[]{:S(2)}) collective-permute-start(bf16[4,48,512]{2,1,0:T(8,128)(2,1)S(1)} %slice.225), channel_id=1, source_target_pairs={{0,16},{8,24},{16,0},{24,8},{1,17},{9,25},{17,1},{25,9},{2,18},{10... | collective-permute-start | bytes 589832 | tf_op jit(solution)/shard_map/ppermute | solution.py:657
  18.4 6.9 %collective-permute-start.6 = (bf16[4,48,512]{2,1,0:T(8,128)(2,1)S(1)}, bf16[4,48,512]{2,1,0:T(8,128)(2,1)S(1)}, u32[]{:S(2)}, u32[]{:S(2)}) collective-permute-start(bf16[4,48,512]{2,1,0:T(8,128)(2,1)S(1)} %slice.225), channel_id=1, source_target_pairs={{0,8},{8,0},{16,24},{24,16},{1,9},{9,1},{17,25},{25,17},{2,10},{10... | collective-permute-start | bytes 589832 | tf_op jit(solution)/shard_map/ppermute | solution.py:657
  22.9 8.6 %copy-start.1 = (bf16[4,2,256,512]{3,2,1,0:T(8,128)(2,1)S(1)}, bf16[4,2,256,512]{3,2,1,0:T(8,128)(2,1)}, u32[]{:S(2)}) copy-start(bf16[4,2,256,512]{3,2,1,0:T(8,128)(2,1)} %param.15) | copy-start | bytes 6291460
  22.9 8.6 %copy-start.3 = (s32[4,2]{0,1:T(2,128)S(1)}, s32[4,2]{0,1:T(2,128)}, u32[]{:S(2)}) copy-start(s32[4,2]{0,1:T(2,128)} %param.14) | copy-start | bytes 100
  25.3 1.7 %collective-permute-start.8 = (bf16[16,24,512]{2,1,0:T(8,128)(2,1)S(1)}, bf16[16,24,512]{2,1,0:T(8,128)(2,1)S(1)}, u32[]{:S(2)}, u32[]{:S(2)}) collective-permute-start(bf16[16,24,512]{2,1,0:T(8,128)(2,1)S(1)} %bitcast.60), channel_id=1, source_target_pairs={{0,1},{1,0},{2,3},{3,2},{4,5},{5,4},{6,7},{7,6},{8,9},{9,8},{10,11... | collective-permute-start | bytes 1179656 | tf_op jit(solution)/shard_map/ppermute | solution.py:657
  25.4 5.7 %collective-permute-start.10 = (bf16[4,48,512]{2,1,0:T(8,128)(2,1)S(1)}, bf16[4,48,512]{2,1,0:T(8,128)(2,1)S(1)}, u32[]{:S(2)}, u32[]{:S(2)}) collective-permute-start(bf16[4,48,512]{2,1,0:T(8,128)(2,1)S(1)} %broadcast_select_fusion), channel_id=1, source_target_pairs={{0,16},{1,9},{2,18},{3,11},{4,20},{5,13},{6,22},{7,15},{8,24},{9,1... | collective-permute-start | bytes 589832 | tf_op jit(solution)/shard_map/ppermute | solution.py:745
  28.5 1.2 %collective-permute-start.9 = (f32[8,512]{1,0:T(8,128)S(1)}, f32[8,512]{1,0:T(8,128)S(1)}, u32[]{:S(2)}, u32[]{:S(2)}) collective-permute-start(f32[8,512]{1,0:T(8,128)S(1)} %get-tuple-element.76), channel_id=1, source_target_pairs={{0,1},{1,0},{2,3},{3,2},{4,5},{5,4},{6,7},{7,6},{8,9},{9,8},{10,11... | collective-permute-start | bytes 49160 | tf_op jit(solution)/shard_map/ppermute | solution.py:657
  31.1 3.7 %collective-permute-start.11 = (f32[8,512]{1,0:T(8,128)S(1)}, f32[8,512]{1,0:T(8,128)S(1)}, u32[]{:S(2)}, u32[]{:S(2)}) collective-permute-start(f32[8,512]{1,0:T(8,128)S(1)} %maximum_add_fusion), channel_id=1, source_target_pairs={{0,2},{2,0},{4,6},{6,4},{1,3},{3,1},{5,7},{7,5},{8,10},{10,8},{12,... | collective-permute-start | bytes 49160 | tf_op jit(solution)/shard_map/ppermute | solution.py:657
  35.0 4.8 %collective-permute-start.13 = (bf16[16,48,512]{2,1,0:T(8,128)(2,1)S(1)}, bf16[16,48,512]{2,1,0:T(8,128)(2,1)S(1)}, u32[]{:S(2)}, u32[]{:S(2)}) collective-permute-start(bf16[16,48,512]{2,1,0:T(8,128)(2,1)S(1)} %bitcast.58), channel_id=1, source_target_pairs={{0,1},{1,0},{2,3},{3,2},{4,5},{5,4},{6,7},{7,6},{8,9},{9,8},{10,11... | collective-permute-start | bytes 2359304 | tf_op jit(solution)/shard_map/ppermute | solution.py:657
  35.1 4.7 %collective-permute-start.12 = (f32[8,512]{1,0:T(8,128)S(1)}, f32[8,512]{1,0:T(8,128)S(1)}, u32[]{:S(2)}, u32[]{:S(2)}) collective-permute-start(f32[8,512]{1,0:T(8,128)S(1)} %maximum_add_fusion.1), channel_id=1, source_target_pairs={{0,4},{2,6},{4,0},{6,2},{1,5},{3,7},{5,1},{7,3},{8,12},{10,14},{12... | collective-permute-start | bytes 49160 | tf_op jit(solution)/shard_map/ppermute | solution.py:657
  53.1 1.2 %collective-permute-start.14 = (f32[8,512]{1,0:T(8,128)S(1)}, f32[8,512]{1,0:T(8,128)S(1)}, u32[]{:S(2)}, u32[]{:S(2)}) collective-permute-start(f32[8,512]{1,0:T(8,128)S(1)} %get-tuple-element.91), channel_id=1, source_target_pairs={{0,1},{1,0},{2,3},{3,2},{4,5},{5,4},{6,7},{7,6},{8,9},{9,8},{10,11... | collective-permute-start | bytes 49160 | tf_op jit(solution)/shard_map/ppermute | solution.py:657
  53.2 5.0 %collective-permute-start.16 = (bf16[16,48,512]{2,1,0:T(8,128)(2,1)S(1)}, bf16[16,48,512]{2,1,0:T(8,128)(2,1)S(1)}, u32[]{:S(2)}, u32[]{:S(2)}) collective-permute-start(bf16[16,48,512]{2,1,0:T(8,128)(2,1)S(1)} %get-tuple-element.93), channel_id=1, source_target_pairs={{0,1},{1,0},{2,3},{3,2},{4,5},{5,4},{6,7},{7,6},{8,9},{9,8},{10,11... | collective-permute-start | bytes 2359304 | tf_op jit(solution)/shard_map/ppermute | solution.py:657
  54.4 3.8 %collective-permute-start.15 = (f32[8,512]{1,0:T(8,128)S(1)}, f32[8,512]{1,0:T(8,128)S(1)}, u32[]{:S(2)}, u32[]{:S(2)}) collective-permute-start(f32[8,512]{1,0:T(8,128)S(1)} %maximum_add_fusion.3), channel_id=1, source_target_pairs={{0,2},{2,0},{4,6},{6,4},{1,3},{3,1},{5,7},{7,5},{8,10},{10,8},{12,... | collective-permute-start | bytes 49160 | tf_op jit(solution)/shard_map/ppermute | solution.py:657
  58.5 4.7 %collective-permute-start.18 = (f32[8,512]{1,0:T(8,128)S(1)}, f32[8,512]{1,0:T(8,128)S(1)}, u32[]{:S(2)}, u32[]{:S(2)}) collective-permute-start(f32[8,512]{1,0:T(8,128)S(1)} %maximum_add_fusion.4), channel_id=1, source_target_pairs={{0,4},{2,6},{4,0},{6,2},{1,5},{3,7},{5,1},{7,3},{8,12},{10,14},{12... | collective-permute-start | bytes 49160 | tf_op jit(solution)/shard_map/ppermute | solution.py:657
  59.8 7.8 %collective-permute-start.17 = (bf16[8,48,512]{2,1,0:T(8,128)(2,1)S(1)}, bf16[8,48,512]{2,1,0:T(8,128)(2,1)S(1)}, u32[]{:S(2)}, u32[]{:S(2)}) collective-permute-start(bf16[8,48,512]{2,1,0:T(8,128)(2,1)S(1)} %get-tuple-element.95), channel_id=1, source_target_pairs={{0,8},{1,17},{2,10},{3,19},{4,12},{5,21},{6,14},{7,23},{8,0},{9,25... | collective-permute-start | bytes 1179656 | tf_op jit(solution)/shard_map/ppermute | solution.py:816
  67.7 1.8 %collective-permute-start.20 = (bf16[16,24,512]{2,1,0:T(8,128)(2,1)S(1)}, bf16[16,24,512]{2,1,0:T(8,128)(2,1)S(1)}, u32[]{:S(2)}, u32[]{:S(2)}) collective-permute-start(bf16[16,24,512]{2,1,0:T(8,128)(2,1)S(1)} %get-tuple-element.105), channel_id=1, source_target_pairs={{0,1},{1,0},{2,3},{3,2},{4,5},{5,4},{6,7},{7,6},{8,9},{9,8},{10,11... | collective-permute-start | bytes 1179656 | tf_op jit(solution)/shard_map/ppermute | solution.py:657
  67.8 5.7 %collective-permute-start.19 = (bf16[4,48,512]{2,1,0:T(8,128)(2,1)S(1)}, bf16[4,48,512]{2,1,0:T(8,128)(2,1)S(1)}, u32[]{:S(2)}, u32[]{:S(2)}) collective-permute-start(bf16[4,48,512]{2,1,0:T(8,128)(2,1)S(1)} %get-tuple-element.103), channel_id=1, source_target_pairs={{0,16},{1,9},{2,18},{3,11},{4,20},{5,13},{6,22},{7,15},{8,24},{9,1... | collective-permute-start | bytes 589832 | tf_op jit(solution)/shard_map/ppermute | solution.py:835
  69.6 8.1 %collective-permute-start.21 = (bf16[4,24,512]{2,1,0:T(8,128)(2,1)S(1)}, bf16[4,24,512]{2,1,0:T(8,128)(2,1)S(1)}, u32[]{:S(2)}, u32[]{:S(2)}) collective-permute-start(bf16[4,24,512]{2,1,0:T(8,128)(2,1)S(1)} %get-tuple-element.134), channel_id=1, source_target_pairs={{0,8},{8,0},{16,24},{24,16},{1,9},{9,1},{17,25},{25,17},{2,10},{10... | collective-permute-start | bytes 294920 | tf_op jit(solution)/shard_map/ppermute | solution.py:657
  71.1 7.0 %collective-permute-start.23 = (bf16[4,24,512]{2,1,0:T(8,128)(2,1)S(1)}, bf16[4,24,512]{2,1,0:T(8,128)(2,1)S(1)}, u32[]{:S(2)}, u32[]{:S(2)}) collective-permute-start(bf16[4,24,512]{2,1,0:T(8,128)(2,1)S(1)} %get-tuple-element.135), channel_id=1, source_target_pairs={{0,24},{8,16},{16,8},{24,0},{1,25},{9,17},{17,9},{25,1},{2,26},{10... | collective-permute-start | bytes 294920 | tf_op jit(solution)/shard_map/ppermute | solution.py:657
  72.5 6.5 %collective-permute-start.22 = (bf16[4,24,512]{2,1,0:T(8,128)(2,1)S(1)}, bf16[4,24,512]{2,1,0:T(8,128)(2,1)S(1)}, u32[]{:S(2)}, u32[]{:S(2)}) collective-permute-start(bf16[4,24,512]{2,1,0:T(8,128)(2,1)S(1)} %get-tuple-element.136), channel_id=1, source_target_pairs={{0,16},{8,24},{16,0},{24,8},{1,17},{9,25},{17,1},{25,9},{2,18},{10... | collective-permute-start | bytes 294920 | tf_op jit(solution)/shard_map/ppermute | solution.py:657
  79.8 12.3 %all-to-all-start = ((bf16[4,72,512]{2,1,0:T(8,128)(2,1)}), bf16[4,72,512]{2,1,0:T(8,128)(2,1)S(1)}, u32[]{:S(2)}, u32[]{:S(2)}) async-start(bf16[4,72,512]{2,1,0:T(8,128)(2,1)} %pad_maximum_fusion.3), calls=%async_computation | async-start | bytes 589824 | tf_op jit(solution)/shard_map/all_to_all | solution.py:844
  83.3 8.8 %copy-start.2 = (bf16[16,512]{1,0:T(8,128)(2,1)S(1)}, bf16[16,512]{1,0:T(8,128)(2,1)}, u32[]{:S(2)}) copy-start(bf16[16,512]{1,0:T(8,128)(2,1)} %proj.1) | copy-start | bytes 49156
  83.3 8.8 %copy-start.4 = (bf16[16]{0:T(256)(128)(2,1)S(1)}, bf16[16]{0:T(256)(128)(2,1)}, u32[]{:S(2)}) copy-start(bf16[16]{0:T(256)(128)(2,1)} %param.16) | copy-start | bytes 100
  83.3 8.8 %copy-start.5 = (bf16[16]{0:T(256)(128)(2,1)S(1)}, bf16[16]{0:T(256)(128)(2,1)}, u32[]{:S(2)}) copy-start(bf16[16]{0:T(256)(128)(2,1)} %param.17) | copy-start | bytes 100
  83.3 8.8 %copy-start.6 = (bf16[16]{0:T(256)(128)(2,1)S(1)}, bf16[16]{0:T(256)(128)(2,1)}, u32[]{:S(2)}) copy-start(bf16[16]{0:T(256)(128)(2,1)} %param.23) | copy-start | bytes 100
  83.3 8.8 %copy-start.7 = (bf16[8]{0:T(256)(128)(2,1)S(1)}, bf16[8]{0:T(256)(128)(2,1)}, u32[]{:S(2)}) copy-start(bf16[8]{0:T(256)(128)(2,1)} %param.19) | copy-start | bytes 52
  83.3 8.8 %copy-start.8 = (bf16[8]{0:T(256)(128)(2,1)S(1)}, bf16[8]{0:T(256)(128)(2,1)}, u32[]{:S(2)}) copy-start(bf16[8]{0:T(256)(128)(2,1)} %param.20) | copy-start | bytes 52

commit v3 on v2

--- a/solution.py
+++ b/solution.py
@@ -265,8 +265,8 @@
 
 def middle_body(
     u, cotl, carry, vec, c, g, wh,
-    st, dst, dm_out, y_out, end, sums,
-    dm, y, act, dpre, mix, pre, slope, dact, total_grads, sems, put,
+    st, dst, act, dpre, dm, y, end, sums,
+    mix, pre, slope, dact,
 ):
     count, width = carry.shape
     half = width // 2
@@ -275,7 +275,6 @@
     part = 32
     steps = rows // count
     blocks = total // rows
-    copies = Copies(sems)
     lr, li = lam_rows(vec, count)
     state = [carry[:, :half], carry[:, half:]]
     zero = jnp.zeros((count, half), F32)
@@ -332,7 +331,6 @@
             y[r, :] = (v + vt).astype(BF)
             totals[2] = totals[2] + fold_rows(dv, count)
             totals[3] = totals[3] + fold_rows(dg, count)
-        copies.send(y, y_out, pl.ds(i * rows, rows))
 
     def back(i):
         dact[i % 2] = dot(dpre[block(i), :], g[...], 1, 1)
@@ -342,7 +340,6 @@
             dm[r, :] = d.astype(BF)
             totals[0] = totals[0] + fold_rows(d * wh[r, :].astype(F32), count)
             totals[1] = totals[1] + fold_rows(d, count)
-        copies.send(dm, dm_out, pl.ds(i * rows, rows))
 
     def ends(i):
         dst[block(i), :] = dot(dm[block(i), :], c[...], 1, 1)
@@ -353,45 +350,23 @@
         ends_sum[:] = complex_step(*power, *now, *ends_sum)
         power[:] = complex_mul(*power, *jump)
 
-    spans = ((0, 2), (2, 4), (4, 6), (6, blocks))
-    tiles = [(act, dpre, 0), (act, dpre, width), (st, dm, 0)]
-    tasks = []
-
-    def product(first, last, k):
-        a, b, start = tiles[k]
-        r = slice(first * rows, last * rows)
-        value = dot(a[r, :], b[r, start : start + width], 0, 0)
-        if first:
-            value = value + total_grads[k]
-        if last == blocks:
-            put(k, value)
-        else:
-            total_grads[k] = value
-
     stages = (scan, activate, gating, back, ends)
     for turn in range(blocks + len(stages) - 1):
         for depth in range(len(stages) - 1, -1, -1):
             if 0 <= turn - depth < blocks:
                 stages[depth](turn - depth)
-            if tasks and depth in (4, 2, 0):
-                product(*tasks.pop(0))
-        for first, last in spans:
-            if turn - 3 == last - 1:
-                tasks += [(first, last, k) for k in range(3)]
-    for task in tasks:
-        product(*task)
     end[:, :half] = ends_sum[0]
     end[:, half:] = ends_sum[1]
     for k, a in enumerate(totals):
         sums[k : k + 1, :] = jnp.sum(a, axis=0, keepdims=True)
-    copies.finish()
 
 
 def owner_of(q, core, crossed=False):
     tmc = lax.axis_size("tmc")
     seq = lax.axis_index("seq").astype(jnp.int32)
     differs = (0, 2 - core, 1 + core, 3)[q // tmc] if crossed else q // tmc
-    return (jnp.bitwise_xor(seq, differs) * tmc + q % tmc) * 2 + core
+    along = jnp.bitwise_xor(lax.axis_index("tmc").astype(jnp.int32), q % tmc)
+    return (jnp.bitwise_xor(seq, differs) * tmc + along) * 2 + core
 
 
 def split_rows(grads, keep, give, index, crossed=False):
@@ -403,61 +378,52 @@
 
 
 def middle_gathered_kernel(u, cotl, carry, vec, own, other, wh, *refs):
-    outs, scratch = refs[:8], refs[8:]
-    *scratch, c, g, grads, sems = scratch
+    *refs, c, g = refs
     width = c.shape[0]
     assemble((c, g.at[:, :width], g.at[:, width:]), own, other, 0)
     g[...] = (g[...].astype(F32) * 0.5).astype(BF)
-
-    def put(k, value):
-        grads[k] = value.astype(BF)
-        split_rows(grads.at[k], outs[6], outs[7], 16 * k, True)
-
-    middle_body(u, cotl, carry, vec, c, g, wh, *outs[:6], *scratch, sems, put)
-
-
-def middle_plain_kernel(*refs):
-    ins, outs, scratch = refs[:7], refs[7:14], refs[14:]
-    width = outs[6].shape[0]
-
-    def put(k, value):
-        outs[6][:, k * width : (k + 1) * width] = value.astype(BF)
-
-    middle_body(*ins, *outs[:6], *scratch, put)
-
-
-def output_kernel(ends, y, tok, out, y_in, tok_in, sems):
+    middle_body(u, cotl, carry, vec, c, g, wh, *refs)
+
+
+def weight_products(act, dpre, st, dm):
+    width = st.shape[1]
+    for k, (a, b, start) in enumerate(((act, dpre, 0), (act, dpre, width), (st, dm, 0))):
+        yield k, dot(a[...], b[:, start : start + width], 0, 0).astype(BF)
+
+
+def weights_gathered_kernel(act, dpre, st, dm, keep, give, grads):
+    for k, value in weight_products(act, dpre, st, dm):
+        grads[k] = value
+        split_rows(grads.at[k], keep, give, 16 * k, True)
+
+
+def weights_plain_kernel(act, dpre, st, dm, out):
+    width = st.shape[1]
+    for k, value in weight_products(act, dpre, st, dm):
+        out[:, k * width : (k + 1) * width] = value
+
+
+def output_kernel(lengths, y, tok, out, buf, sems):
     count, length, width = tok.shape
     part = 16
     pieces = 4
     step = length // pieces
     copies = Copies(sems)
-    waits = [
-        (
-            copies.start(y, y_in, pl.ds(k * step * count, step * count)),
-            copies.start(tok, tok_in, (slice(None), pl.ds(k * step, step))),
-        )
-        for k in range(pieces)
-    ]
     for k in range(pieces):
-        for copy in waits[k]:
-            copy.wait()
         for i in range(k * step, (k + 1) * step, part):
-            live = live_rows(ends, i, part, length, width)
-            add = swap_order(y_in[i * count : (i + part) * count, :].astype(F32), count)
-            x = tok_in[:, i : i + part, :].astype(F32) + live * add
-            tok_in[:, i : i + part, :] = x.astype(BF)
-        copies.send(tok_in, out, (slice(None), pl.ds(k * step, step)))
+            live = live_rows(lengths, i, part, length, width)
+            add = swap_order(y[i * count : (i + part) * count, :].astype(F32), count)
+            buf[:, i : i + part, :] = (tok[:, i : i + part, :].astype(F32) + live * add).astype(BF)
+        copies.send(buf, out, (slice(None), pl.ds(k * step, step)))
     copies.finish()
 
 
-def adjoint_body(dst_in, u_in, st_in, wh, back, carry, vec, adj_out, adj, sems):
+def adjoint_body(dst_in, u_in, st_in, wh, back, carry, vec, adj):
     count, width = back.shape
     half = width // 2
     total = u_in.shape[0]
     step = 256
     blocks = total // step
-    copies = Copies(sems)
     lr, li = lam_rows(vec, count)
     ar, ai = back[:, :half], back[:, half:]
     zero = jnp.zeros((count, half), F32)
@@ -485,7 +451,6 @@
             adj[pair, half:] = jnp.concatenate([held[1][1], held[0][1]], axis=0).astype(BF)
         at = slice(block * step, (block + 1) * step)
         m = m + dot(wh[at, :], adj[at, :], 0, 0)
-        copies.send(adj, adj_out, pl.ds(block * step, step))
     cr, ci = carry[:, :half], carry[:, half:]
     lsr = lsr + (ar * cr + ai * ci)
     lsi = lsi + (ai * cr - ar * ci)
@@ -494,7 +459,7 @@
         return jnp.sum(a, axis=0, keepdims=True)
 
     cols = jnp.concatenate([row(csr), row(csi)], axis=1)
-    return copies, m, cols, row(lsr), row(lsi), row(gam)
+    return m, cols, row(lsr), row(lsi), row(gam)
 
 
 def by_owner(vectors, owners):
@@ -517,13 +482,12 @@
 
 
 def adjoint_gathered_kernel(
-    dst, u, st, wh, back, carry, vec, sums, adj_out, keep, give,
-    adj, grads, small, sems,
+    dst, u, st, wh, back, carry, vec, sums, adj, keep, give, grads, small,
 ):
     width = vec.shape[1]
     owners = 2 * keep.shape[0]
-    copies, m, cols, lsr, lsi, gam = adjoint_body(
-        dst, u, st, wh, back, carry, vec, adj_out, adj, sems
+    m, cols, lsr, lsi, gam = adjoint_body(
+        dst, u, st, wh, back, carry, vec, adj
     )
     bias = jnp.concatenate([sums[2:3, :], sums[3:4, :]], axis=1)
     small[:, :SIDE] = by_owner((lsr, lsi, gam), owners)
@@ -540,63 +504,47 @@
         for ref, side in ((keep, core), (give, 1 - core)):
             row = jnp.concatenate([small[pl.ds(owner_of(q, side), 1), :], rest], axis=1)
             ref[q, 16:24, :] = jnp.where(row_id == 2, row, common).astype(BF)
-    copies.finish()
 
 
 def adjoint_plain_kernel(
-    dst, u, st, wh, back, carry, vec, adj_out, m_out, rows_out, adj, sems
+    dst, u, st, wh, back, carry, vec, adj, m_out, rows_out
 ):
     half = vec.shape[1] // 2
-    copies, m, cols, lsr, lsi, gam = adjoint_body(
-        dst, u, st, wh, back, carry, vec, adj_out, adj, sems
+    m, cols, lsr, lsi, gam = adjoint_body(
+        dst, u, st, wh, back, carry, vec, adj
     )
     m_out[...] = m.astype(BF)
     rows_out[0:1, :] = cols
     rows_out[1:2, :half] = lsr
     rows_out[1:2, half:] = lsi
     rows_out[2:3, :half] = gam
-    copies.finish()
-
-
-def inputs_kernel(adj, dm, cot, inv, wh, b, vec, out, adj_in, dm_in, cot_in, inv_in, buf, sems):
+
+
+def inputs_kernel(adj, dm, cot, inv, wh, b, vec, out, res, buf, sems):
     count, length, width = cot.shape
     rows = 256
     part = 16
     steps = rows // count
-    blocks = length * count // rows
     copies = Copies(sems)
-    waits = []
-
-    def fetch(i):
-        if i < blocks:
-            at = pl.ds(i * rows, rows)
-            pairs = ((adj, adj_in), (dm, dm_in), (inv, inv_in))
-            waits.append([copies.start(src, dest, at) for src, dest in pairs])
-            waits[i].append(copies.start(cot, cot_in, (slice(None), pl.ds(i * steps, steps))))
-
-    for i in range(AHEAD):
-        fetch(i)
-    for i in range(blocks):
-        for copy in waits[i]:
-            copy.wait()
-        fetch(i + AHEAD)
-        buf[i % 2] = dot(adj_in[i * rows : (i + 1) * rows, :], b[...], 1, 1)
+    for i in range(length * count // rows):
+        buf[i % 2] = dot(adj[i * rows : (i + 1) * rows, :], b[...], 1, 1)
         for k in range(0, rows, part * count):
             r = slice(i * rows + k, i * rows + k + part * count)
             w = wh[r, :].astype(F32)
-            e = buf[i % 2, k : k + part * count, :] + dm_in[r, :].astype(F32) * vec[3:4, :]
+            e = buf[i % 2, k : k + part * count, :] + dm[r, :].astype(F32) * vec[3:4, :]
             mean = jnp.mean(e, axis=-1, keepdims=True)
             proj = jnp.mean(e * w, axis=-1, keepdims=True)
-            wide = jnp.concatenate([inv_in[r, :]] * (width // SIDE), axis=-1)
+            wide = jnp.concatenate([inv[r, :]] * (width // SIDE), axis=-1)
             d = swap_order((e - mean - w * proj) * wide, count)
             t = slice((i * rows + k) // count, (i * rows + k) // count + part)
-            cot_in[:, t, :] = (cot_in[:, t, :].astype(F32) + d).astype(BF)
-        copies.send(cot_in, out, (slice(None), pl.ds(i * steps, steps)))
+            res[:, t, :] = (cot[:, t, :].astype(F32) + d).astype(BF)
+        copies.send(res, out, (slice(None), pl.ds(i * steps, steps)))
     copies.finish()
 
 
-def finish_kernel(parts, vec, proj, gain, shift, skip, decay, phase, *refs):
-    far, near, sems = refs[:10], refs[10:20], refs[20]
+def finish_kernel(vec, proj, gain, shift, skip, decay, phase, *refs):
+    *parts, sems = refs
+    parts, far, near = parts[:-20], parts[-20:-10], parts[-10:]
     (
         gate_out, proj_out, in_out, gain_out, shift_out, skip_out, decay_out, phase_out, gamma_out, bias_out,
     ) = near
@@ -609,7 +557,7 @@
             copies.append(pltpu.make_async_copy(near[k], far[k], sems.at[k]))
             copies[-1].start()
 
-    late = jnp.sum(parts[:, 3 * n :, :].astype(F32), axis=0)
+    late = sum(part[3 * n :, :].astype(F32) for part in parts)
     scale = vec[1:2, :]
     diag = lax.broadcasted_iota(jnp.int32, (n, n), 0) == lax.broadcasted_iota(jnp.int32, (n, n), 1)
 
@@ -644,7 +592,7 @@
     decay_out[...] = -rate * (re * lam_re + im * lam_im)
     phase_out[...] = turn * (im * lam_re - re * lam_im)
     ready(3, 4, 5, 6, 7, 8, 9)
-    early = jnp.sum(parts[:, : 3 * n, :].astype(F32), axis=0)
+    early = sum(part[: 3 * n, :].astype(F32) for part in parts)
     gate_out[:, :width] = 0.5 * early[:n]
     gate_out[:, width:] = 0.5 * early[n : 2 * n]
     proj_out[...] = early[2 * n :]
@@ -783,79 +731,89 @@
         rows = 256
         blocks = total // rows
         side = ((count, length, width), BF)
-        outs = [wide_bf, wide_f, wide_bf, wide_bf, ((count, width), F32), ((4, width), F32)]
-        scratch = [wide_bf] * 3 + [
-            ((total, 2 * width), BF), ((2, rows, width), F32), ((2, rows, 2 * width), F32),
-            ((4, rows, width), F32), ((2, rows, width), F32), ((3, width, width), F32),
+        outs = [
+            wide_bf, wide_f, wide_bf, ((total, 2 * width), BF), wide_bf, wide_bf,
+            ((count, width), F32), ((4, width), F32),
+        ]
+        scratch = [
+            ((2, rows, width), F32), ((2, rows, 2 * width), F32), ((4, rows, width), F32),
+            ((2, rows, width), F32),
         ]
         if fast:
             ins = (u, cotl, carry, vec, held["own"], held["other"], wh)
-            st, dst, dm, y, back_end, sums, keep, give = call(
-                middle_gathered_kernel, "middle", outs + [((chips, 48, width), BF)] * 2, ins,
-                scratch + [((width, width), BF), ((width, 2 * width), BF), ((3, width, width), BF)], limit=32, far_out=(2, 3), copies=2 * blocks,
-            )
+            scratch += [((width, width), BF), ((width, 2 * width), BF)]
         else:
-            st, dst, dm, y, back_end, sums, out_grads = call(
-                middle_plain_kernel, "middle", outs + [((width, 3 * width), BF)],
-                (u, cotl, carry, vec, c, g, wh), scratch,
-                limit=32, far_out=(2, 3), copies=2 * blocks,
-            )
-
+            ins = (u, cotl, carry, vec, c, g, wh)
+        st, dst, act, dpre, dm, y, back_end, sums = call(
+            middle_gathered_kernel if fast else middle_body, "middle", outs, ins, scratch,
+            limit=24,
+        )
+        if not fast:
+            (out_grads,) = call(
+                weights_plain_kernel, "weights", [((width, 3 * width), BF)], (act, dpre, st, dm)
+            )
 
         def seq_parts(both):
             both = both.reshape(sizes["seq"], sizes["tmc"], -1, width)
             return [both[0]] + [swap(both[k], "seq", sizes["seq"], k) for k in range(1, sizes["seq"])]
 
         def early_sums(bit, a):
+            if fast and bit == 1:
+                now = tie(a, act)[1]
+                held["sums"] = call(
+                    weights_gathered_kernel, "weights", [((chips, 48, width), BF)] * 2,
+                    (now, dpre, st, dm), [((3, width, width), BF)],
+                )
             if fast and bit == 2:
-                got = swap(give, "core", 2, 1)
-                low, high = slice(0, chips // 2), slice(chips // 2, chips)
-                high = add_low(keep[high], got[high])
-                low = add_low(keep[low], got[low])
-                a, high, low = tie(a, high, low)
-                got = lax.ppermute(high, AXES, cross_pairs(owners, sizes["tmc"], 0))
-                held["early"] = (low, got)
+                a, *held["sums"] = tie(a, *held["sums"])
+                held["got"] = swap(held["sums"][1], "core", 2, 1)
             return a
 
         back = carry_in(back_end, pows, bits, sizes, True, early_sums)
+        if fast:
+            got = held["got"]
+            low, high = (
+                add_low(held["sums"][0][k : k + chips // 2], got[k : k + chips // 2])
+                for k in (0, chips // 2)
+            )
+            quarter = chips // 4
+            first_link = cross_pairs(owners, sizes["tmc"], 0)
+            got = [lax.ppermute(high[k : k + quarter], AXES, first_link) for k in (quarter, 0)]
+            held["early"] = (low, *got)
 
         ins = (dst, u, st, wh, back, carry, vec)
         if fast:
             adj, late_keep, late_give = call(
                 adjoint_gathered_kernel, "adjoint",
                 [wide_bf] + [((chips, 24, width), BF)] * 2, (*ins, sums),
-                [wide_bf] + [((width, width), BF), ((owners, 2 * SIDE), F32)],
-                limit=10, far_out=(0,), copies=blocks,
-            )
-            quarter = chips // 4
-            low, high = (
-                add_low(*(a[k : k + quarter] for a in held["early"])) for k in (0, quarter)
-            )
-            low, high, late_keep, late_give = tie(low, high, late_keep, late_give)
-            early = add_low(low, lax.ppermute(high, AXES, cross_pairs(owners, sizes["tmc"], 1)))
+                [((width, width), BF), ((owners, 2 * SIDE), F32)], limit=10,
+            )
+            low, got, got_own = held["early"]
+            give = add_low(low[quarter:], got)
+            give, late_keep, late_give = tie(give, late_keep, late_give)
+            got = lax.ppermute(give, AXES, cross_pairs(owners, sizes["tmc"], 1))
             late = add_low(late_keep, swap(late_give, "core", 2, 1))
             late, y = tie(late, y)
+            early = add_low(low[:quarter], got_own, got)
             both = jnp.concatenate([early, add_low(*seq_parts(late))], axis=1)
             block_out = call(
-                output_kernel, "output", [side], (lengths.T, y, tok), [wide_bf, side],
-                limit=8, far_in=(1, 2), far_out=(0,), copies=12,
+                output_kernel, "output", [side], (lengths.T, y, tok), [side],
+                limit=6, far_out=(0,), copies=4,
             )[0]
             both, adj, block_out = tie(both, adj, block_out)
-            both = lax.all_to_all(both, "tmc", 0, 0)
+            both = [both[0]] + [swap(both[k], "tmc", sizes["tmc"], k) for k in range(1, sizes["tmc"])]
         else:
             adj, m, late_rows = call(
                 adjoint_plain_kernel, "adjoint",
-                [wide_bf, ((width, width), BF), ((8, width), F32)], ins, [wide_bf],
-                limit=10, far_out=(0,), copies=blocks,
+                [wide_bf, ((width, width), BF), ((8, width), F32)], ins, limit=10,
             )
             block_out = call(
-                output_kernel, "output", [side], (lengths.T, y, tok), [wide_bf, side],
-                limit=8, far_in=(1, 2), far_out=(0,), copies=12,
+                output_kernel, "output", [side], (lengths.T, y, tok), [side],
+                limit=6, far_out=(0,), copies=4,
             )[0]
         (tok_grad,) = call(
             inputs_kernel, "inputs", [side], (adj, dm, cot, inv, wh, b, vec),
-            [wide_bf, wide_bf, side, ((total, SIDE), F32), ((2, rows, width), F32)],
-            limit=14, far_in=range(4), far_out=(0,), copies=5 * blocks,
+            [side, ((2, rows, width), F32)], limit=8, far_out=(0,), copies=blocks,
         )
 
         q = half // owners
@@ -864,7 +822,7 @@
             shapes = [(a, F32) for a in shapes]
             rows = [v.reshape(1, -1) for v in (norm_gain, norm_shift, skip_gain, decay_log, phase_log)]
             grads = call(
-                finish_kernel, "finish", shapes, (both, vec, input_proj, *rows), shapes,
+                finish_kernel, "finish", shapes, (vec, input_proj, *rows, *both), shapes,
                 far_out=range(10), copies=10,
             )
             gate_sum, proj_sum, in_grad = grads[:3]

time: 93.6 us -> 88.3 us (0.943)
  waiting for transfers between devices: 25 us -> 21 us
  Pallas kernels: 36 us -> 32.2 us
  starting transfers between devices: 27.8 us -> 30.9 us
    ppermute x21 -> x24, starting transfers between devices: 20.3 us -> 25.7 us  [swap(): return lax.ppermute(a, axis, [(k, k ^ bit) for k in range(size)])]
    pallas_call x9 -> x10, Pallas kernels: 36 us -> 32.2 us  [call(): pl.pallas_call(body, out_shape=[pltpu.HBM(s, t) if k in far_out else jax....]
    all_to_all x1 -> x0, starting transfers between devices: 3.45 us -> none  [body(): both = lax.all_to_all(both, 'tmc', 0, 0)]
    ppermute x21 -> x24, waiting for transfers between devices: 20.6 us -> 17.4 us  [swap(): return lax.ppermute(a, axis, [(k, k ^ bit) for k in range(size)])]
    all_to_all x1 -> x0, waiting for transfers between devices: 1.82 us -> none  [body(): both = lax.all_to_all(both, 'tmc', 0, 0)]
    ppermute x2 -> x3, starting transfers between devices: 2.95 us -> 4.15 us  [the longest x2 3.11 us: body(): lax.ppermute(high[k:k + quarter], AXES, first_link)]
    ppermute x2 -> x3, waiting for transfers between devices: 1.29 us -> 2.24 us  [the longest x2 2.11 us: body(): lax.ppermute(high[k:k + quarter], AXES, first_link)]
  transfers between devices with their start and end apart: 25 -> 28, of which waited for: 19 -> 17; matrix products, arithmetic and copies ran while one was open for 0% -> 1% of each run, Pallas kernels for 22% -> 22%
where the time goes in v3:
time: 88.3 us; the launch traced here: 88 us
  Pallas kernels  32.2 us (36%)
  starting transfers between devices  30.9 us (35%)
  waiting for transfers between devices  21 us (24%)
  local copies, waits for them, and re-layouts  1.76 us (2%)
  between operations  1.23 us (1%)
  other arithmetic  0.96 us (1%)
    pallas_call x10, Pallas kernels, call(): pl.pallas_call(body, out_shape=[pltpu.HBM(s, t) if k in far_out else jax....  32.2 us
    ppermute x24, starting transfers between devices, swap(): return lax.ppermute(a, axis, [(k, k ^ bit) for k in range(size)])  25.7 us
    ppermute x24, waiting for transfers between devices, swap(): return lax.ppermute(a, axis, [(k, k ^ bit) for k in range(size)])  17.4 us
    ppermute x2, starting transfers between devices, body(): lax.ppermute(high[k:k + quarter], AXES, first_link)  3.11 us
    ppermute x2, waiting for transfers between devices, body(): lax.ppermute(high[k:k + quarter], AXES, first_link)  2.11 us
  transfers between devices with their start and end apart: 28, of which 17 were waited for; matrix products, arithmetic and copies ran while one was open for 1% of the time, Pallas kernels for 22%

profile of v3, /device:TPU:0, one launch (start us, length us, event | category | flops | bytes accessed | tf_op | source)
XLA Modules:
  0.0 88.0 jit_solution(8766127018942350662)
XLA Ops:
  0.6 1.2 %pack.1 = (bf16[72,512]{1,0:T(8,128)(2,1)S(1)}, f32[1,512]{1,0:T(1,128)S(1)}) custom-call(bf16[1,16]{1,0:T(2,128)(2,1)} %bitcast.73, bf16[1,16]{1,0:T(2,128)(2,1)} %bitcast.75, bf16[1,16]{1,0:T(2,128)(2,1)} %bitcast.77, bf16[1,8]{1,0:T(2,128)(2,1)} %bitcast.79, bf16[1,8]{1,0:T(2,128)(2,1)} %bitcast.81, bf16[1,8]{1,0:T(2,128)(2,1)} %bitcast.115, ...), custom_call_target="tpu_custom_call" | custom-call | tf_op jit(solution)/shard_map/pack/pallas_call | solution.py:30
  1.8 5.1 %collective-permute-start.2 = (bf16[72,512]{1,0:T(8,128)(2,1)S(1)}, bf16[72,512]{1,0:T(8,128)(2,1)S(1)}, u32[]{:S(2)}, u32[]{:S(2)}) collective-permute-start(bf16[72,512]{1,0:T(8,128)(2,1)S(1)} %get-tuple-element.71), channel_id=1, source_target_pairs={{0,6},{2,4},{4,2},{6,0},{1,7},{3,5},{5,3},{7,1},{8,14},{10,12},{12... | collective-permute-start | bytes 221192 | tf_op jit(solution)/shard_map/ppermute | solution.py:605
  6.9 0.6 collective-permute-start
  7.6 1.6 %copy-done = bf16[4,2,256,512]{3,2,1,0:T(8,128)(2,1)S(1)} copy-done((bf16[4,2,256,512]{3,2,1,0:T(8,128)(2,1)S(1)}, bf16[4,2,256,512]{3,2,1,0:T(8,128)(2,1)}, u32[]{:S(2)}) %copy-start) | copy-done | bytes 2097176
  9.2 3.3 %whiten.1 = (bf16[2048,512]{1,0:T(8,128)(2,1)S(1)}, f32[2048,128]{1,0:T(8,128)}) custom-call(bf16[8,256,512]{2,1,0:T(8,128)(2,1)S(1)} %bitcast.62), custom_call_target="tpu_custom_call" | custom-call | tf_op jit(solution)/shard_map/whiten/pallas_call | solution.py:30
  12.5 0.7 collective-permute-done.1
  13.2 1.6 %collective-permute-start.4 = (bf16[4,24,512]{2,1,0:T(8,128)(2,1)S(1)}, bf16[4,24,512]{2,1,0:T(8,128)(2,1)S(1)}, u32[]{:S(2)}, u32[]{:S(2)}) collective-permute-start(bf16[4,24,512]{2,1,0:T(8,128)(2,1)S(1)} %get-tuple-element.146), channel_id=1, source_target_pairs={{0,16},{8,24},{16,0},{24,8},{1,17},{9,25},{17,1},{25,9},{2,18},{10... | collective-permute-start | bytes 294920 | tf_op jit(solution)/shard_map/ppermute | solution.py:605
  14.8 1.5 %collective-permute-start.3 = (bf16[4,24,512]{2,1,0:T(8,128)(2,1)S(1)}, bf16[4,24,512]{2,1,0:T(8,128)(2,1)S(1)}, u32[]{:S(2)}, u32[]{:S(2)}) collective-permute-start(bf16[4,24,512]{2,1,0:T(8,128)(2,1)S(1)} %get-tuple-element.146), channel_id=1, source_target_pairs={{0,8},{8,0},{16,24},{24,16},{1,9},{9,1},{17,25},{25,17},{2,10},{10... | collective-permute-start | bytes 294920 | tf_op jit(solution)/shard_map/ppermute | solution.py:605
  16.3 0.5 collective-permute-start.5
  16.8 1.6 %collective-permute-start.7 = (bf16[4,48,512]{2,1,0:T(8,128)(2,1)S(1)}, bf16[4,48,512]{2,1,0:T(8,128)(2,1)S(1)}, u32[]{:S(2)}, u32[]{:S(2)}) collective-permute-start(bf16[4,48,512]{2,1,0:T(8,128)(2,1)S(1)} %slice.237), channel_id=1, source_target_pairs={{0,16},{8,24},{16,0},{24,8},{1,17},{9,25},{17,1},{25,9},{2,18},{10... | collective-permute-start | bytes 589832 | tf_op jit(solution)/shard_map/ppermute | solution.py:605
  18.4 1.5 %collective-permute-start.6 = (bf16[4,48,512]{2,1,0:T(8,128)(2,1)S(1)}, bf16[4,48,512]{2,1,0:T(8,128)(2,1)S(1)}, u32[]{:S(2)}, u32[]{:S(2)}) collective-permute-start(bf16[4,48,512]{2,1,0:T(8,128)(2,1)S(1)} %slice.237), channel_id=1, source_target_pairs={{0,8},{8,0},{16,24},{24,16},{1,9},{9,1},{17,25},{25,17},{2,10},{10... | collective-permute-start | bytes 589832 | tf_op jit(solution)/shard_map/ppermute | solution.py:605
  19.9 0.5 collective-permute-done.3
  20.4 2.5 %collective-permute-done.5 = bf16[4,24,512]{2,1,0:T(8,128)(2,1)S(1)} collective-permute-done((bf16[4,24,512]{2,1,0:T(8,128)(2,1)S(1)}, bf16[4,24,512]{2,1,0:T(8,128)(2,1)S(1)}, u32[]{:S(2)}, u32[]{:S(2)}) %collective-permute-start.5) | collective-permute-done | bytes 98336 | tf_op jit(solution)/shard_map/ppermute | solution.py:605
  23.0 1.4 %collective-permute-done.7 = bf16[4,48,512]{2,1,0:T(8,128)(2,1)S(1)} collective-permute-done((bf16[4,48,512]{2,1,0:T(8,128)(2,1)S(1)}, bf16[4,48,512]{2,1,0:T(8,128)(2,1)S(1)}, u32[]{:S(2)}, u32[]{:S(2)}) %collective-permute-start.7) | collective-permute-done | bytes 196640 | tf_op jit(solution)/shard_map/ppermute | solution.py:605
  24.4 0.9 collective-permute-done.6
  25.4 1.0 %collective-permute-start.10 = (bf16[4,48,512]{2,1,0:T(8,128)(2,1)S(1)}, bf16[4,48,512]{2,1,0:T(8,128)(2,1)S(1)}, u32[]{:S(2)}, u32[]{:S(2)}) collective-permute-start(bf16[4,48,512]{2,1,0:T(8,128)(2,1)S(1)} %broadcast_select_fusion), channel_id=1, source_target_pairs={{0,16},{1,9},{2,18},{3,11},{4,20},{5,13},{6,22},{7,15},{8,24},{9,1... | collective-permute-start | bytes 589832 | tf_op jit(solution)/shard_map/ppermute | solution.py:693
  26.4 0.7 collective-permute-done.8.r_1_
  27.0 1.5 %drive.1 = (bf16[512,512]{1,0:T(8,128)(2,1)S(1)}, f32[8,512]{1,0:T(8,128)S(1)}, f32[16,512]{1,0:T(8,128)S(1)}, f32[2048,512]{1,0:T(8,128)S(1)}, f32[8,512]{1,0:T(8,128)S(1)}) custom-call(bf16[16,24,512]{2,1,0:T(8,128)(2,1)S(1)} %bitcast.69, bf16[16,24,512]{2,1,0:T(8,128)(2,1)S(1)} %collective-permute-done.8.r_1_, bf16[2048,512]{1,0:T(8,128)(2,1)S(1)} %get-tuple-element.75.r_2_.wh), custom_call_target="tpu_custom_call" | custom-call | tf_op jit(solution)/shard_map/drive/pallas_call | solution.py:30
  28.8 1.0 %collective-permute-done.9 = f32[8,512]{1,0:T(8,128)S(1)} collective-permute-done((f32[8,512]{1,0:T(8,128)S(1)}, f32[8,512]{1,0:T(8,128)S(1)}, u32[]{:S(2)}, u32[]{:S(2)}) %collective-permute-start.9) | collective-permute-done | bytes 16416 | tf_op jit(solution)/shard_map/ppermute | solution.py:605
  29.8 1.3 %collective-permute-done.10 = bf16[4,48,512]{2,1,0:T(8,128)(2,1)S(1)} collective-permute-done((bf16[4,48,512]{2,1,0:T(8,128)(2,1)S(1)}, bf16[4,48,512]{2,1,0:T(8,128)(2,1)S(1)}, u32[]{:S(2)}, u32[]{:S(2)}) %collective-permute-start.10) | collective-permute-done | bytes 196640 | tf_op jit(solution)/shard_map/ppermute | solution.py:693
  31.1 0.4 collective-permute-start.11
  31.5 1.3 %mask.1.cotl = f32[2048,512]{1,0:T(8,128)S(1)} custom-call(s32[2,4]{1,0:T(2,128)S(1)} %bitcast.71, bf16[8,256,512]{2,1,0:T(8,128)(2,1)S(1)} %bitcast.64), custom_call_target="tpu_custom_call" | custom-call | tf_op jit(solution)/shard_map/mask/pallas_call | solution.py:30
  32.8 2.0 %collective-permute-done.11 = f32[8,512]{1,0:T(8,128)S(1)} collective-permute-done((f32[8,512]{1,0:T(8,128)S(1)}, f32[8,512]{1,0:T(8,128)S(1)}, u32[]{:S(2)}, u32[]{:S(2)}) %collective-permute-start.11) | collective-permute-done | bytes 16416 | tf_op jit(solution)/shard_map/ppermute | solution.py:605
  35.1 1.3 %collective-permute-start.12 = (f32[8,512]{1,0:T(8,128)S(1)}, f32[8,512]{1,0:T(8,128)S(1)}, u32[]{:S(2)}, u32[]{:S(2)}) collective-permute-start(f32[8,512]{1,0:T(8,128)S(1)} %maximum_add_fusion.1), channel_id=1, source_target_pairs={{0,4},{2,6},{4,0},{6,2},{1,5},{3,7},{5,1},{7,3},{8,12},{10,14},{12... | collective-permute-start | bytes 49160 | tf_op jit(solution)/shard_map/ppermute | solution.py:605
  36.4 3.4 %collective-permute-done.12 = f32[8,512]{1,0:T(8,128)S(1)} collective-permute-done((f32[8,512]{1,0:T(8,128)S(1)}, f32[8,512]{1,0:T(8,128)S(1)}, u32[]{:S(2)}, u32[]{:S(2)}) %collective-permute-start.12) | collective-permute-done | bytes 16416 | tf_op jit(solution)/shard_map/ppermute | solution.py:605
  39.8 10.7 %middle.1 = (bf16[2048,512]{1,0:T(8,128)(2,1)S(1)}, f32[2048,512]{1,0:T(8,128)S(1)}, bf16[2048,512]{1,0:T(8,128)(2,1)S(1)}, bf16[2048,1024]{1,0:T(8,128)(2,1)S(1...) custom-call(f32[2048,512]{1,0:T(8,128)S(1)} %get-tuple-element.77.u,, ...), custom_call_target="tpu_custom_call" | custom-call | tf_op jit(solution)/shard_map/middle/pallas_call | solution.py:30
  50.6 1.2 %collective-permute-done.14 = f32[8,512]{1,0:T(8,128)S(1)} collective-permute-done((f32[8,512]{1,0:T(8,128)S(1)}, f32[8,512]{1,0:T(8,128)S(1)}, u32[]{:S(2)}, u32[]{:S(2)}) %collective-permute-start.14) | collective-permute-done | bytes 16416 | tf_op jit(solution)/shard_map/ppermute | solution.py:605
  51.8 0.4 collective-permute-start.15
  52.2 3.5 %weights.1 = (bf16[16,48,512]{2,1,0:T(8,128)(2,1)S(1)}, bf16[16,48,512]{2,1,0:T(8,128)(2,1)S(1)}) custom-call(bf16[2048,512]{1,0:T(8,128)(2,1)S(1)} %get-tuple-element.95.act, bf16[2048,1024]{1,0:T(8,128)(2,1)S(1)} %get-tuple-element.96.dpre, bf16[2048,512]{1,0:T(8,128)(2,1)S(1)} %get-tuple-element.97.st, bf16[2048,512]{1,0:T(8,128)(2,1)S(1)} %get-tuple-element.98.dm), custom_call_target="tpu_custom_call" | custom-call | tf_op jit(solution)/shard_map/weights/pallas_call | solution.py:30
  55.8 2.7 %collective-permute-start.19 = (f32[8,512]{1,0:T(8,128)S(1)}, f32[8,512]{1,0:T(8,128)S(1)}, u32[]{:S(2)}, u32[]{:S(2)}) collective-permute-start(f32[8,512]{1,0:T(8,128)S(1)} %maximum_add_fusion.4), channel_id=1, source_target_pairs={{0,4},{2,6},{4,0},{6,2},{1,5},{3,7},{5,1},{7,3},{8,12},{10,14},{12... | collective-permute-start | bytes 49160 | tf_op jit(solution)/shard_map/ppermute | solution.py:605
  58.6 0.2 add_convert_fusion.2
  58.8 1.6 %collective-permute-start.18 = (bf16[4,48,512]{2,1,0:T(8,128)(2,1)S(1)}, bf16[4,48,512]{2,1,0:T(8,128)(2,1)S(1)}, u32[]{:S(2)}, u32[]{:S(2)}) collective-permute-start(bf16[4,48,512]{2,1,0:T(8,128)(2,1)S(1)} %get-tuple-element.137), channel_id=1, source_target_pairs={{0,8},{1,17},{2,10},{3,19},{4,12},{5,21},{6,14},{7,23},{8,0},{9,25... | collective-permute-start | bytes 589832 | tf_op jit(solution)/shard_map/ppermute | solution.py:781
  60.6 2.9 %adjoint.1 = (bf16[2048,512]{1,0:T(8,128)(2,1)S(1)}, bf16[16,24,512]{2,1,0:T(8,128)(2,1)S(1)}, bf16[16,24,512]{2,1,0:T(8,128)(2,1)S(1)}) custom-call(f32[2048,512]{1,0:T(8,128)S(1)} %get-tuple-element.103.dst, f32[2048,512]{1,0:T(8,128)S(1)} %get-tuple-element.77.u, bf16[2048,512]{1,0:T(8,128)(2,1)S(1)} %get-tuple-element.97.st, ...), custom_call_target="tpu_custom_call" | custom-call | tf_op jit(solution)/shard_map/adjoint/pallas_call | solution.py:30
  63.4 1.1 %collective-permute-done.18 = bf16[4,48,512]{2,1,0:T(8,128)(2,1)S(1)} collective-permute-done((bf16[4,48,512]{2,1,0:T(8,128)(2,1)S(1)}, bf16[4,48,512]{2,1,0:T(8,128)(2,1)S(1)}, u32[]{:S(2)}, u32[]{:S(2)}) %collective-permute-start.18) | collective-permute-done | bytes 196640 | tf_op jit(solution)/shard_map/ppermute | solution.py:781
  64.7 1.6 %collective-permute-start.17 = (bf16[4,48,512]{2,1,0:T(8,128)(2,1)S(1)}, bf16[4,48,512]{2,1,0:T(8,128)(2,1)S(1)}, u32[]{:S(2)}, u32[]{:S(2)}) collective-permute-start(bf16[4,48,512]{2,1,0:T(8,128)(2,1)S(1)} %get-tuple-element.136), channel_id=1, source_target_pairs={{0,8},{1,17},{2,10},{3,19},{4,12},{5,21},{6,14},{7,23},{8,0},{9,25... | collective-permute-start | bytes 589832 | tf_op jit(solution)/shard_map/ppermute | solution.py:781
  66.3 1.0 %collective-permute-start.20 = (bf16[4,48,512]{2,1,0:T(8,128)(2,1)S(1)}, bf16[4,48,512]{2,1,0:T(8,128)(2,1)S(1)}, u32[]{:S(2)}, u32[]{:S(2)}) collective-permute-start(bf16[4,48,512]{2,1,0:T(8,128)(2,1)S(1)} %add_convert_fusion.4), channel_id=1, source_target_pairs={{0,16},{1,9},{2,18},{3,11},{4,20},{5,13},{6,22},{7,15},{8,24},{9,1... | collective-permute-start | bytes 589832 | tf_op jit(solution)/shard_map/ppermute | solution.py:794
  67.4 1.0 %collective-permute-start.22 = (bf16[4,24,512]{2,1,0:T(8,128)(2,1)S(1)}, bf16[4,24,512]{2,1,0:T(8,128)(2,1)S(1)}, u32[]{:S(2)}, u32[]{:S(2)}) collective-permute-start(bf16[4,24,512]{2,1,0:T(8,128)(2,1)S(1)} %get-tuple-element.138), channel_id=1, source_target_pairs={{0,8},{8,0},{16,24},{24,16},{1,9},{9,1},{17,25},{25,17},{2,10},{10... | collective-permute-start | bytes 294920 | tf_op jit(solution)/shard_map/ppermute | solution.py:605
  68.5 1.5 %collective-permute-start.24 = (bf16[4,24,512]{2,1,0:T(8,128)(2,1)S(1)}, bf16[4,24,512]{2,1,0:T(8,128)(2,1)S(1)}, u32[]{:S(2)}, u32[]{:S(2)}) collective-permute-start(bf16[4,24,512]{2,1,0:T(8,128)(2,1)S(1)} %get-tuple-element.139), channel_id=1, source_target_pairs={{0,24},{8,16},{16,8},{24,0},{1,25},{9,17},{17,9},{25,1},{2,26},{10... | collective-permute-start | bytes 294920 | tf_op jit(solution)/shard_map/ppermute | solution.py:605
  70.0 1.0 %collective-permute-start.23 = (bf16[4,24,512]{2,1,0:T(8,128)(2,1)S(1)}, bf16[4,24,512]{2,1,0:T(8,128)(2,1)S(1)}, u32[]{:S(2)}, u32[]{:S(2)}) collective-permute-start(bf16[4,24,512]{2,1,0:T(8,128)(2,1)S(1)} %get-tuple-element.140), channel_id=1, source_target_pairs={{0,16},{8,24},{16,0},{24,8},{1,17},{9,25},{17,1},{25,9},{2,18},{10... | collective-permute-start | bytes 294920 | tf_op jit(solution)/shard_map/ppermute | solution.py:605
  71.0 1.0 %collective-permute-done.17 = bf16[4,48,512]{2,1,0:T(8,128)(2,1)S(1)} collective-permute-done((bf16[4,48,512]{2,1,0:T(8,128)(2,1)S(1)}, bf16[4,48,512]{2,1,0:T(8,128)(2,1)S(1)}, u32[]{:S(2)}, u32[]{:S(2)}) %collective-permute-start.17) | collective-permute-done | bytes 196640 | tf_op jit(solution)/shard_map/ppermute | solution.py:781
  72.2 2.8 %output.1 = bf16[8,256,512]{2,1,0:T(8,128)(2,1)} custom-call(s32[2,4]{1,0:T(2,128)S(1)} %bitcast.72, bf16[2048,512]{1,0:T(8,128)(2,1)S(1)} %get-tuple-element.114.y, bf16[8,256,512]{2,1,0:T(8,128)(2,1)S(1)} %bitcast.63), custom_call_target="tpu_custom_call" | custom-call | tf_op jit(solution)/shard_map/output/pallas_call | solution.py:30
  75.1 2.4 %collective-permute-done.24 = bf16[4,24,512]{2,1,0:T(8,128)(2,1)S(1)} collective-permute-done((bf16[4,24,512]{2,1,0:T(8,128)(2,1)S(1)}, bf16[4,24,512]{2,1,0:T(8,128)(2,1)S(1)}, u32[]{:S(2)}, u32[]{:S(2)}) %collective-permute-start.24) | collective-permute-done | bytes 98336 | tf_op jit(solution)/shard_map/ppermute | solution.py:605
  77.5 1.9 %collective-permute-start.27 = (bf16[72,512]{1,0:T(8,128)(2,1)S(1)}, bf16[72,512]{1,0:T(8,128)(2,1)S(1)}, u32[]{:S(2)}, u32[]{:S(2)}) collective-permute-start(bf16[72,512]{1,0:T(8,128)(2,1)S(1)} %get-tuple-element.141), channel_id=1, source_target_pairs={{0,6},{2,4},{4,2},{6,0},{1,7},{3,5},{5,3},{7,1},{8,14},{10,12},{12... | collective-permute-start | bytes 221192 | tf_op jit(solution)/shard_map/ppermute | solution.py:605
  79.4 0.4 collective-permute-start.26
  79.9 2.1 %collective-permute-start.25 = (bf16[72,512]{1,0:T(8,128)(2,1)S(1)}, bf16[72,512]{1,0:T(8,128)(2,1)S(1)}, u32[]{:S(2)}, u32[]{:S(2)}) collective-permute-start(bf16[72,512]{1,0:T(8,128)(2,1)S(1)} %get-tuple-element.143), channel_id=1, source_target_pairs={{0,2},{2,0},{4,6},{6,4},{1,3},{3,1},{5,7},{7,5},{8,10},{10,8},{12,... | collective-permute-start | bytes 221192 | tf_op jit(solution)/shard_map/ppermute | solution.py:605
  82.0 4.1 %inputs.1 = bf16[8,256,512]{2,1,0:T(8,128)(2,1)} custom-call(bf16[2048,512]{1,0:T(8,128)(2,1)S(1)} %get-tuple-element.116.adj, bf16[2048,512]{1,0:T(8,128)(2,1)S(1)} %get-tuple-element.98.dm, bf16[8,256,512]{2,1,0:T(8,128)(2,1)S(1)} %bitcast.65, f32[2048,128]{1,0:T(8,128)S(1)} %copy-done.3, bf16[2048,512]{1,0:T(8,128)(2,1)S(1)} %get-tuple-element.75.r_2_.wh, ...), custom_call_target="tpu_custom_call" | custom-call | tf_op jit(solution)/shard_map/inputs/pallas_call | solution.py:30
  86.2 0.6 collective-permute-done.26.refs_2_
  86.9 1.0 %finish.1 = (f32[16,1024]{1,0:T(8,128)}, f32[16,512]{1,0:T(8,128)}, f32[16,512]{1,0:T(8,128)}, f32[1,16]{1,0:T(1,128)}, f32[1,16]{1,0:T(1,128)}, /*index=5*/f32[...) custom-call(f32[8,512]{1,0:T(8,128)S(1)} %get-tuple-element.86.vec, ...), custom_call_target="tpu_custom_call" | custom-call | tf_op jit(solution)/shard_map/finish/pallas_call | solution.py:30
  (79 shorter events, 1.7 us)
Async XLA Ops:
  1.8 10.6 %collective-permute-start.2 = (bf16[72,512]{1,0:T(8,128)(2,1)S(1)}, bf16[72,512]{1,0:T(8,128)(2,1)S(1)}, u32[]{:S(2)}, u32[]{:S(2)}) collective-permute-start(bf16[72,512]{1,0:T(8,128)(2,1)S(1)} %get-tuple-element.71), channel_id=1, source_target_pairs={{0,6},{2,4},{4,2},{6,0},{1,7},{3,5},{5,3},{7,1},{8,14},{10,12},{12... | collective-permute-start | bytes 221192 | tf_op jit(solution)/shard_map/ppermute | solution.py:605
  6.9 6.2 %collective-permute-start.1 = (bf16[72,512]{1,0:T(8,128)(2,1)S(1)}, bf16[72,512]{1,0:T(8,128)(2,1)S(1)}, u32[]{:S(2)}, u32[]{:S(2)}) collective-permute-start(bf16[72,512]{1,0:T(8,128)(2,1)S(1)} %get-tuple-element.71), channel_id=1, source_target_pairs={{0,4},{2,6},{4,0},{6,2},{1,5},{3,7},{5,1},{7,3},{8,12},{10,14},{12... | collective-permute-start | bytes 221192 | tf_op jit(solution)/shard_map/ppermute | solution.py:605
  6.9 6.2 %collective-permute-start = (bf16[72,512]{1,0:T(8,128)(2,1)S(1)}, bf16[72,512]{1,0:T(8,128)(2,1)S(1)}, u32[]{:S(2)}, u32[]{:S(2)}) collective-permute-start(bf16[72,512]{1,0:T(8,128)(2,1)S(1)} %get-tuple-element.71), channel_id=1, source_target_pairs={{0,2},{2,0},{4,6},{6,4},{1,3},{3,1},{5,7},{7,5},{8,10},{10,8},{12,... | collective-permute-start | bytes 221192 | tf_op jit(solution)/shard_map/ppermute | solution.py:605
  7.6 1.6 %copy-start = (bf16[4,2,256,512]{3,2,1,0:T(8,128)(2,1)S(1)}, bf16[4,2,256,512]{3,2,1,0:T(8,128)(2,1)}, u32[]{:S(2)}) copy-start(bf16[4,2,256,512]{3,2,1,0:T(8,128)(2,1)} %param.13) | copy-start | bytes 6291460
  13.2 6.7 %collective-permute-start.4 = (bf16[4,24,512]{2,1,0:T(8,128)(2,1)S(1)}, bf16[4,24,512]{2,1,0:T(8,128)(2,1)S(1)}, u32[]{:S(2)}, u32[]{:S(2)}) collective-permute-start(bf16[4,24,512]{2,1,0:T(8,128)(2,1)S(1)} %get-tuple-element.146), channel_id=1, source_target_pairs={{0,16},{8,24},{16,0},{24,8},{1,17},{9,25},{17,1},{25,9},{2,18},{10... | collective-permute-start | bytes 294920 | tf_op jit(solution)/shard_map/ppermute | solution.py:605
  14.8 5.6 %collective-permute-start.3 = (bf16[4,24,512]{2,1,0:T(8,128)(2,1)S(1)}, bf16[4,24,512]{2,1,0:T(8,128)(2,1)S(1)}, u32[]{:S(2)}, u32[]{:S(2)}) collective-permute-start(bf16[4,24,512]{2,1,0:T(8,128)(2,1)S(1)} %get-tuple-element.146), channel_id=1, source_target_pairs={{0,8},{8,0},{16,24},{24,16},{1,9},{9,1},{17,25},{25,17},{2,10},{10... | collective-permute-start | bytes 294920 | tf_op jit(solution)/shard_map/ppermute | solution.py:605
  16.3 6.6 %collective-permute-start.5 = (bf16[4,24,512]{2,1,0:T(8,128)(2,1)S(1)}, bf16[4,24,512]{2,1,0:T(8,128)(2,1)S(1)}, u32[]{:S(2)}, u32[]{:S(2)}) collective-permute-start(bf16[4,24,512]{2,1,0:T(8,128)(2,1)S(1)} %get-tuple-element.146), channel_id=1, source_target_pairs={{0,24},{8,16},{16,8},{24,0},{1,25},{9,17},{17,9},{25,1},{2,26},{10... | collective-permute-start | bytes 294920 | tf_op jit(solution)/shard_map/ppermute | solution.py:605
  16.8 7.6 %collective-permute-start.7 = (bf16[4,48,512]{2,1,0:T(8,128)(2,1)S(1)}, bf16[4,48,512]{2,1,0:T(8,128)(2,1)S(1)}, u32[]{:S(2)}, u32[]{:S(2)}) collective-permute-start(bf16[4,48,512]{2,1,0:T(8,128)(2,1)S(1)} %slice.237), channel_id=1, source_target_pairs={{0,16},{8,24},{16,0},{24,8},{1,17},{9,25},{17,1},{25,9},{2,18},{10... | collective-permute-start | bytes 589832 | tf_op jit(solution)/shard_map/ppermute | solution.py:605
  18.4 6.9 %collective-permute-start.6 = (bf16[4,48,512]{2,1,0:T(8,128)(2,1)S(1)}, bf16[4,48,512]{2,1,0:T(8,128)(2,1)S(1)}, u32[]{:S(2)}, u32[]{:S(2)}) collective-permute-start(bf16[4,48,512]{2,1,0:T(8,128)(2,1)S(1)} %slice.237), channel_id=1, source_target_pairs={{0,8},{8,0},{16,24},{24,16},{1,9},{9,1},{17,25},{25,17},{2,10},{10... | collective-permute-start | bytes 589832 | tf_op jit(solution)/shard_map/ppermute | solution.py:605
  22.9 8.6 %copy-start.2 = (bf16[4,2,256,512]{3,2,1,0:T(8,128)(2,1)S(1)}, bf16[4,2,256,512]{3,2,1,0:T(8,128)(2,1)}, u32[]{:S(2)}) copy-start(bf16[4,2,256,512]{3,2,1,0:T(8,128)(2,1)} %param.15) | copy-start | bytes 6291460
  22.9 8.6 %copy-start.5 = (s32[4,2]{0,1:T(2,128)S(1)}, s32[4,2]{0,1:T(2,128)}, u32[]{:S(2)}) copy-start(s32[4,2]{0,1:T(2,128)} %param.14) | copy-start | bytes 100
  25.3 1.7 %collective-permute-start.8 = (bf16[16,24,512]{2,1,0:T(8,128)(2,1)S(1)}, bf16[16,24,512]{2,1,0:T(8,128)(2,1)S(1)}, u32[]{:S(2)}, u32[]{:S(2)}) collective-permute-start(bf16[16,24,512]{2,1,0:T(8,128)(2,1)S(1)} %bitcast.68), channel_id=1, source_target_pairs={{0,1},{1,0},{2,3},{3,2},{4,5},{5,4},{6,7},{7,6},{8,9},{9,8},{10,11... | collective-permute-start | bytes 1179656 | tf_op jit(solution)/shard_map/ppermute | solution.py:605
  25.4 5.7 %collective-permute-start.10 = (bf16[4,48,512]{2,1,0:T(8,128)(2,1)S(1)}, bf16[4,48,512]{2,1,0:T(8,128)(2,1)S(1)}, u32[]{:S(2)}, u32[]{:S(2)}) collective-permute-start(bf16[4,48,512]{2,1,0:T(8,128)(2,1)S(1)} %broadcast_select_fusion), channel_id=1, source_target_pairs={{0,16},{1,9},{2,18},{3,11},{4,20},{5,13},{6,22},{7,15},{8,24},{9,1... | collective-permute-start | bytes 589832 | tf_op jit(solution)/shard_map/ppermute | solution.py:693
  28.5 1.2 %collective-permute-start.9 = (f32[8,512]{1,0:T(8,128)S(1)}, f32[8,512]{1,0:T(8,128)S(1)}, u32[]{:S(2)}, u32[]{:S(2)}) collective-permute-start(f32[8,512]{1,0:T(8,128)S(1)} %get-tuple-element.78), channel_id=1, source_target_pairs={{0,1},{1,0},{2,3},{3,2},{4,5},{5,4},{6,7},{7,6},{8,9},{9,8},{10,11... | collective-permute-start | bytes 49160 | tf_op jit(solution)/shard_map/ppermute | solution.py:605
  31.1 3.7 %collective-permute-start.11 = (f32[8,512]{1,0:T(8,128)S(1)}, f32[8,512]{1,0:T(8,128)S(1)}, u32[]{:S(2)}, u32[]{:S(2)}) collective-permute-start(f32[8,512]{1,0:T(8,128)S(1)} %maximum_add_fusion), channel_id=1, source_target_pairs={{0,2},{2,0},{4,6},{6,4},{1,3},{3,1},{5,7},{7,5},{8,10},{10,8},{12,... | collective-permute-start | bytes 49160 | tf_op jit(solution)/shard_map/ppermute | solution.py:605
  35.0 4.8 %collective-permute-start.13 = (bf16[16,48,512]{2,1,0:T(8,128)(2,1)S(1)}, bf16[16,48,512]{2,1,0:T(8,128)(2,1)S(1)}, u32[]{:S(2)}, u32[]{:S(2)}) collective-permute-start(bf16[16,48,512]{2,1,0:T(8,128)(2,1)S(1)} %bitcast.66), channel_id=1, source_target_pairs={{0,1},{1,0},{2,3},{3,2},{4,5},{5,4},{6,7},{7,6},{8,9},{9,8},{10,11... | collective-permute-start | bytes 2359304 | tf_op jit(solution)/shard_map/ppermute | solution.py:605
  35.1 4.7 %collective-permute-start.12 = (f32[8,512]{1,0:T(8,128)S(1)}, f32[8,512]{1,0:T(8,128)S(1)}, u32[]{:S(2)}, u32[]{:S(2)}) collective-permute-start(f32[8,512]{1,0:T(8,128)S(1)} %maximum_add_fusion.1), channel_id=1, source_target_pairs={{0,4},{2,6},{4,0},{6,2},{1,5},{3,7},{5,1},{7,3},{8,12},{10,14},{12... | collective-permute-start | bytes 49160 | tf_op jit(solution)/shard_map/ppermute | solution.py:605
  50.5 1.2 %collective-permute-start.14 = (f32[8,512]{1,0:T(8,128)S(1)}, f32[8,512]{1,0:T(8,128)S(1)}, u32[]{:S(2)}, u32[]{:S(2)}) collective-permute-start(f32[8,512]{1,0:T(8,128)S(1)} %get-tuple-element.93), channel_id=1, source_target_pairs={{0,1},{1,0},{2,3},{3,2},{4,5},{5,4},{6,7},{7,6},{8,9},{9,8},{10,11... | collective-permute-start | bytes 49160 | tf_op jit(solution)/shard_map/ppermute | solution.py:605
  51.8 3.9 %collective-permute-start.15 = (f32[8,512]{1,0:T(8,128)S(1)}, f32[8,512]{1,0:T(8,128)S(1)}, u32[]{:S(2)}, u32[]{:S(2)}) collective-permute-start(f32[8,512]{1,0:T(8,128)S(1)} %maximum_add_fusion.3), channel_id=1, source_target_pairs={{0,2},{2,0},{4,6},{6,4},{1,3},{3,1},{5,7},{7,5},{8,10},{10,8},{12,... | collective-permute-start | bytes 49160 | tf_op jit(solution)/shard_map/ppermute | solution.py:605
  55.7 2.8 %collective-permute-start.16 = (bf16[16,48,512]{2,1,0:T(8,128)(2,1)S(1)}, bf16[16,48,512]{2,1,0:T(8,128)(2,1)S(1)}, u32[]{:S(2)}, u32[]{:S(2)}) collective-permute-start(bf16[16,48,512]{2,1,0:T(8,128)(2,1)S(1)} %get-tuple-element.102), channel_id=1, source_target_pairs={{0,1},{1,0},{2,3},{3,2},{4,5},{5,4},{6,7},{7,6},{8,9},{9,8},{10,11... | collective-permute-start | bytes 2359304 | tf_op jit(solution)/shard_map/ppermute | solution.py:605
  55.8 4.7 %collective-permute-start.19 = (f32[8,512]{1,0:T(8,128)S(1)}, f32[8,512]{1,0:T(8,128)S(1)}, u32[]{:S(2)}, u32[]{:S(2)}) collective-permute-start(f32[8,512]{1,0:T(8,128)S(1)} %maximum_add_fusion.4), channel_id=1, source_target_pairs={{0,4},{2,6},{4,0},{6,2},{1,5},{3,7},{5,1},{7,3},{8,12},{10,14},{12... | collective-permute-start | bytes 49160 | tf_op jit(solution)/shard_map/ppermute | solution.py:605
  58.8 5.7 %collective-permute-start.18 = (bf16[4,48,512]{2,1,0:T(8,128)(2,1)S(1)}, bf16[4,48,512]{2,1,0:T(8,128)(2,1)S(1)}, u32[]{:S(2)}, u32[]{:S(2)}) collective-permute-start(bf16[4,48,512]{2,1,0:T(8,128)(2,1)S(1)} %get-tuple-element.137), channel_id=1, source_target_pairs={{0,8},{1,17},{2,10},{3,19},{4,12},{5,21},{6,14},{7,23},{8,0},{9,25... | collective-permute-start | bytes 589832 | tf_op jit(solution)/shard_map/ppermute | solution.py:781
  63.4 8.8 %copy-start.1 = (bf16[4,2,256,512]{3,2,1,0:T(8,128)(2,1)S(1)}, bf16[4,2,256,512]{3,2,1,0:T(8,128)(2,1)}, u32[]{:S(2)}) copy-start(bf16[4,2,256,512]{3,2,1,0:T(8,128)(2,1)} %param.13) | copy-start | bytes 6291460
  64.6 2.7 %collective-permute-start.21 = (bf16[16,24,512]{2,1,0:T(8,128)(2,1)S(1)}, bf16[16,24,512]{2,1,0:T(8,128)(2,1)S(1)}, u32[]{:S(2)}, u32[]{:S(2)}) collective-permute-start(bf16[16,24,512]{2,1,0:T(8,128)(2,1)S(1)} %get-tuple-element.110), channel_id=1, source_target_pairs={{0,1},{1,0},{2,3},{3,2},{4,5},{5,4},{6,7},{7,6},{8,9},{9,8},{10,11... | collective-permute-start | bytes 1179656 | tf_op jit(solution)/shard_map/ppermute | solution.py:605
  64.7 7.3 %collective-permute-start.17 = (bf16[4,48,512]{2,1,0:T(8,128)(2,1)S(1)}, bf16[4,48,512]{2,1,0:T(8,128)(2,1)S(1)}, u32[]{:S(2)}, u32[]{:S(2)}) collective-permute-start(bf16[4,48,512]{2,1,0:T(8,128)(2,1)S(1)} %get-tuple-element.136), channel_id=1, source_target_pairs={{0,8},{1,17},{2,10},{3,19},{4,12},{5,21},{6,14},{7,23},{8,0},{9,25... | collective-permute-start | bytes 589832 | tf_op jit(solution)/shard_map/ppermute | solution.py:781
  66.3 5.8 %collective-permute-start.20 = (bf16[4,48,512]{2,1,0:T(8,128)(2,1)S(1)}, bf16[4,48,512]{2,1,0:T(8,128)(2,1)S(1)}, u32[]{:S(2)}, u32[]{:S(2)}) collective-permute-start(bf16[4,48,512]{2,1,0:T(8,128)(2,1)S(1)} %add_convert_fusion.4), channel_id=1, source_target_pairs={{0,16},{1,9},{2,18},{3,11},{4,20},{5,13},{6,22},{7,15},{8,24},{9,1... | collective-permute-start | bytes 589832 | tf_op jit(solution)/shard_map/ppermute | solution.py:794
  67.4 7.6 %collective-permute-start.22 = (bf16[4,24,512]{2,1,0:T(8,128)(2,1)S(1)}, bf16[4,24,512]{2,1,0:T(8,128)(2,1)S(1)}, u32[]{:S(2)}, u32[]{:S(2)}) collective-permute-start(bf16[4,24,512]{2,1,0:T(8,128)(2,1)S(1)} %get-tuple-element.138), channel_id=1, source_target_pairs={{0,8},{8,0},{16,24},{24,16},{1,9},{9,1},{17,25},{25,17},{2,10},{10... | collective-permute-start | bytes 294920 | tf_op jit(solution)/shard_map/ppermute | solution.py:605
  68.5 9.0 %collective-permute-start.24 = (bf16[4,24,512]{2,1,0:T(8,128)(2,1)S(1)}, bf16[4,24,512]{2,1,0:T(8,128)(2,1)S(1)}, u32[]{:S(2)}, u32[]{:S(2)}) collective-permute-start(bf16[4,24,512]{2,1,0:T(8,128)(2,1)S(1)} %get-tuple-element.139), channel_id=1, source_target_pairs={{0,24},{8,16},{16,8},{24,0},{1,25},{9,17},{17,9},{25,1},{2,26},{10... | collective-permute-start | bytes 294920 | tf_op jit(solution)/shard_map/ppermute | solution.py:605
  70.0 7.5 %collective-permute-start.23 = (bf16[4,24,512]{2,1,0:T(8,128)(2,1)S(1)}, bf16[4,24,512]{2,1,0:T(8,128)(2,1)S(1)}, u32[]{:S(2)}, u32[]{:S(2)}) collective-permute-start(bf16[4,24,512]{2,1,0:T(8,128)(2,1)S(1)} %get-tuple-element.140), channel_id=1, source_target_pairs={{0,16},{8,24},{16,0},{24,8},{1,17},{9,25},{17,1},{25,9},{2,18},{10... | collective-permute-start | bytes 294920 | tf_op jit(solution)/shard_map/ppermute | solution.py:605
  75.0 7.0 %copy-start.3 = (f32[2048,128]{1,0:T(8,128)S(1)}, f32[2048,128]{1,0:T(8,128)}, u32[]{:S(2)}) copy-start(f32[2048,128]{1,0:T(8,128)} %get-tuple-element.117.inv) | copy-start | bytes 3145732
  77.5 8.7 %collective-permute-start.27 = (bf16[72,512]{1,0:T(8,128)(2,1)S(1)}, bf16[72,512]{1,0:T(8,128)(2,1)S(1)}, u32[]{:S(2)}, u32[]{:S(2)}) collective-permute-start(bf16[72,512]{1,0:T(8,128)(2,1)S(1)} %get-tuple-element.141), channel_id=1, source_target_pairs={{0,6},{2,4},{4,2},{6,0},{1,7},{3,5},{5,3},{7,1},{8,14},{10,12},{12... | collective-permute-start | bytes 221192 | tf_op jit(solution)/shard_map/ppermute | solution.py:605
  79.4 7.4 %collective-permute-start.26 = (bf16[72,512]{1,0:T(8,128)(2,1)S(1)}, bf16[72,512]{1,0:T(8,128)(2,1)S(1)}, u32[]{:S(2)}, u32[]{:S(2)}) collective-permute-start(bf16[72,512]{1,0:T(8,128)(2,1)S(1)} %get-tuple-element.142), channel_id=1, source_target_pairs={{0,4},{2,6},{4,0},{6,2},{1,5},{3,7},{5,1},{7,3},{8,12},{10,14},{12... | collective-permute-start | bytes 221192 | tf_op jit(solution)/shard_map/ppermute | solution.py:605
  79.9 7.0 %collective-permute-start.25 = (bf16[72,512]{1,0:T(8,128)(2,1)S(1)}, bf16[72,512]{1,0:T(8,128)(2,1)S(1)}, u32[]{:S(2)}, u32[]{:S(2)}) collective-permute-start(bf16[72,512]{1,0:T(8,128)(2,1)S(1)} %get-tuple-element.143), channel_id=1, source_target_pairs={{0,2},{2,0},{4,6},{6,4},{1,3},{3,1},{5,7},{7,5},{8,10},{10,8},{12,... | collective-permute-start | bytes 221192 | tf_op jit(solution)/shard_map/ppermute | solution.py:605
  82.0 4.9 %copy-start.4 = (bf16[16,512]{1,0:T(8,128)(2,1)S(1)}, bf16[16,512]{1,0:T(8,128)(2,1)}, u32[]{:S(2)}) copy-start(bf16[16,512]{1,0:T(8,128)(2,1)} %proj.1) | copy-start | bytes 49156
  82.0 4.9 %copy-start.6 = (bf16[16]{0:T(256)(128)(2,1)S(1)}, bf16[16]{0:T(256)(128)(2,1)}, u32[]{:S(2)}) copy-start(bf16[16]{0:T(256)(128)(2,1)} %param.16) | copy-start | bytes 100
  82.0 4.9 %copy-start.7 = (bf16[16]{0:T(256)(128)(2,1)S(1)}, bf16[16]{0:T(256)(128)(2,1)}, u32[]{:S(2)}) copy-start(bf16[16]{0:T(256)(128)(2,1)} %param.17) | copy-start | bytes 100
  82.0 4.9 %copy-start.8 = (bf16[16]{0:T(256)(128)(2,1)S(1)}, bf16[16]{0:T(256)(128)(2,1)}, u32[]{:S(2)}) copy-start(bf16[16]{0:T(256)(128)(2,1)} %param.23) | copy-start | bytes 100
  82.0 4.9 %copy-start.9 = (bf16[8]{0:T(256)(128)(2,1)S(1)}, bf16[8]{0:T(256)(128)(2,1)}, u32[]{:S(2)}) copy-start(bf16[8]{0:T(256)(128)(2,1)} %param.19) | copy-start | bytes 52
  82.0 4.9 %copy-start.10 = (bf16[8]{0:T(256)(128)(2,1)S(1)}, bf16[8]{0:T(256)(128)(2,1)}, u32[]{:S(2)}) copy-start(bf16[8]{0:T(256)(128)(2,1)} %param.20) | copy-start | bytes 52
